TPU v7x, 32 devices: a whole 2x2x4 slice. The times are simulated.
32 devices in a mesh: dp: 4 (over y, core), blk: 2 (over x), sp: 4 (over z).
Axes of the slice: x: 2, y: 2, z: 4, core: 2. Of those that a mesh axis runs over, the one named last changes fastest.
Arguments:
- clip_tokens: bfloat16 [4, 2048, 1536], P('dp', ('blk', 'sp')), may hold values from -6 to 6
- text_tokens: bfloat16 [4, 512, 1536], P('dp', ('blk', 'sp')), may hold values from -6 to 6
- text_lengths: int32 [4], P('dp'), may hold values from 64 to 512, as said below
- positions: int32 [4, 3, 2048], P('dp', None, ('blk', 'sp')), may hold values from 0 to 31
- time_embed: float32 [4, 6, 1536], P('dp'), may hold values from -4 to 4
- modulation: bfloat16 [6, 1536], P(None, ('blk', 'sp')), may hold values from -4 to 4
- gains: bfloat16 [5, 1536], P(None, ('blk', 'sp')), may hold values from 0.5 to 1.5
- biases: bfloat16 [10, 1536], P(None, ('blk', 'sp')), may hold values from -1.1953125 to 1.1953125
- self_qkv: bfloat16 [1536, 4608], P(('blk', 'sp')), may hold values from -0.15625 to 0.15625
- self_out: bfloat16 [1536, 1536], P(('blk', 'sp')), may hold values from -4 to 4
- cross_qkv: bfloat16 [1536, 4608], P(('blk', 'sp')), may hold values from -0.15625 to 0.15625
- cross_out: bfloat16 [1536, 1536], P(('blk', 'sp')), may hold values from -2 to 2
- ffn_in: bfloat16 [8960, 1536], P(('blk', 'sp')), may hold values from -0.15625 to 0.15625
- ffn_out: bfloat16 [8960, 1536], P(('blk', 'sp')), may hold values from -0.0625 to 0.0625
- ffn_bias: bfloat16 [8960], P(('blk', 'sp')), may hold values from -1.1953125 to 1.1953125
- cotangent: bfloat16 [4, 2048, 1536], P('dp', ('blk', 'sp')), may hold values from -6 to 6
Outputs:
- block_out: bfloat16 [4, 2048, 1536], P('dp', ('blk', 'sp'))
- grad_tokens: float32 [4, 2048, 1536], P('dp', ('blk', 'sp'))
- grad_text: float32 [4, 512, 1536], P('dp', ('blk', 'sp'))
- grad_modulation: float32 [6, 1536], P(None, ('blk', 'sp'))
- grad_gains: float32 [5, 1536], P(None, ('blk', 'sp'))
- grad_biases: float32 [10, 1536], P(None, ('blk', 'sp'))
- grad_self_qkv: float32 [1536, 4608], P(('blk', 'sp'))
- grad_self_out: float32 [1536, 1536], P(('blk', 'sp'))
- grad_cross_qkv: float32 [1536, 4608], P(('blk', 'sp'))
- grad_cross_out: float32 [1536, 1536], P(('blk', 'sp'))
- grad_ffn_in: float32 [8960, 1536], P(('blk', 'sp'))
- grad_ffn_out: float32 [8960, 1536], P(('blk', 'sp'))
- grad_ffn_bias: float32 [8960], P(('blk', 'sp'))
Inputs may be any that keep to these rules, and one draw needn't show every extreme that they name: `text_lengths`: valid text tokens of each clip; in every draw some clip has all 512 and another has 64.
All inputs are finite; a program needn't handle non-finite values.
Results may differ from a plain program's by a relative error of at most 0.02.
Values may be sent and summed in bfloat16 or wider, within the bound.
A program may use at most 384 MiB of HBM per device.

v0:
```python
import jax
import jax.numpy as jnp
import numpy as np
from jax import lax
from jax.sharding import PartitionSpec as P

H = 12
HD = 128


EPS = 1e-06
NEG = -1e30


def as_sent(x):

    def short(part):
        return part.astype(jnp.bfloat16) if part.dtype == jnp.float32 else part

    return jax.tree.map(short, x)


def layer_norm(values):
    centre = values - jnp.mean(values, axis=-1, keepdims=True)
    return centre * lax.rsqrt(jnp.mean(centre * centre, axis=-1, keepdims=True) + EPS)


def rms_norm(values, gain_row):
    return values * lax.rsqrt(jnp.mean(values * values, axis=-1, keepdims=True) + EPS) * gain_row


def layer_back(values, grad_out):
    return jax.vjp(layer_norm, values)[1](grad_out)[0]


def rope_tables(head_dim):
    pair_count = head_dim // 2
    side_count = head_dim // 6
    first_count = pair_count - 2 * side_count
    tables = np.zeros((3, pair_count))
    for column in range(pair_count):
        if column < first_count:
            tables[0, column] = 10000.0 ** (-column / first_count)
        elif column < first_count + side_count:
            tables[1, column] = 10000.0 ** (-(column - first_count) / side_count)
        else:
            tables[2, column] = 10000.0 ** (-(column - first_count - side_count) / side_count)
    return tables


def rope_angles(positions, head_dim):
    tables = jnp.asarray(rope_tables(head_dim), dtype=jnp.float32)
    places = positions.astype(jnp.float32)
    angles = (
        places[0][:, None] * tables[0]
        + places[1][:, None] * tables[1]
        + places[2][:, None] * tables[2]
    )
    cosine = jnp.cos(angles)
    sine_part = jnp.sin(angles)
    return (jnp.concatenate([cosine, cosine], -1), jnp.concatenate([sine_part, sine_part], -1))


def rotate(values, cosine, sine_part):
    half_dim = values.shape[-1] // 2
    turned = jnp.concatenate([-values[..., half_dim:], values[..., :half_dim]], -1)
    return values * cosine[:, None, :] + turned * sine_part[:, None, :]


def softmax_rows(scores):
    top_score = jnp.max(scores, -1, keepdims=True)
    raised = jnp.exp(scores - top_score)
    return raised / jnp.sum(raised, -1, keepdims=True)


def col_sum(values):
    return jnp.sum(values.astype(jnp.float32), 0)


def gelu_tanh(inner):
    return jax.nn.gelu(inner, approximate=True)


def clip_total(parts):
    return tuple(
        jax.tree.map(lambda part: part.astype(jnp.float32), lax.psum(as_sent(parts), "dp"))
    )


def spread_rows(rows):
    return lax.all_gather(rows, ("blk", "sp"), axis=0, tiled=True)


def group_share(terms):
    return lax.psum_scatter(
        terms.astype(jnp.bfloat16), ("blk", "sp"), scatter_dimension=0, tiled=True
    ).astype(jnp.float32)


def local(
    clip_tokens,
    text_tokens,
    text_lengths,
    positions,
    time_embed,
    modulation,
    gains,
    biases,
    self_qkv,
    self_out,
    cross_qkv,
    cross_out,
    ffn_in,
    ffn_out,
    ffn_bias,
    cotangent,
):
    gathered = (
        lax.all_gather(self_qkv, ("blk", "sp"), axis=0, tiled=True),
        lax.all_gather(self_out, ("blk", "sp"), axis=0, tiled=True),
        lax.all_gather(cross_qkv, ("blk", "sp"), axis=0, tiled=True),
        lax.all_gather(cross_out, ("blk", "sp"), axis=0, tiled=True),
        lax.all_gather(ffn_bias, ("blk", "sp"), axis=0, tiled=True),
        lax.all_gather(modulation, ("blk", "sp"), axis=1, tiled=True),
        lax.all_gather(gains, ("blk", "sp"), axis=1, tiled=True),
        lax.all_gather(biases, ("blk", "sp"), axis=1, tiled=True),
    )
    qkv_self, out_self, qkv_cross, out_cross, bias_hidden, mod_rows, gain_rows, bias_rows = gathered
    mods = time_embed[0] + mod_rows.astype(jnp.float32)
    gain_all = gain_rows.astype(jnp.float32)
    bias_all = bias_rows.astype(jnp.float32)
    bias_ffn = bias_hidden.astype(jnp.float32)
    ff_total = bias_ffn.shape[0]
    ff_here = ffn_in.shape[0]
    ff_start = lax.axis_index(("blk", "sp")) * ff_here
    tokens = clip_tokens[0].astype(jnp.float32)
    tok_rows, width = tokens.shape
    heads_here = H // lax.axis_size("sp")
    scale = HD ** (-0.5)
    normed_one = layer_norm(tokens)
    shifted = (normed_one * (1.0 + mods[1]) + mods[0]).astype(jnp.bfloat16)
    proj = jnp.dot(shifted, qkv_self, preferred_element_type=jnp.float32) + jnp.concatenate(
        [bias_all[0], bias_all[1], bias_all[2]]
    )
    q_lin = proj[:, :width]
    k_lin = proj[:, width : 2 * width]
    cosine, sine_part = rope_angles(positions[0], HD)

    def turn(lin_part, gain_row):
        return rotate(rms_norm(lin_part, gain_row).reshape(tok_rows, H, HD), cosine, sine_part)

    q_send = turn(q_lin, gain_all[0]).astype(jnp.bfloat16)
    k_send = turn(k_lin, gain_all[1]).astype(jnp.bfloat16)
    v_send = proj[:, 2 * width :].astype(jnp.bfloat16).reshape(tok_rows, H, HD)
    q_group, k_group, v_group = (
        lax.all_to_all(q_send, "sp", split_axis=1, concat_axis=0, tiled=True),
        lax.all_to_all(k_send, "sp", split_axis=1, concat_axis=0, tiled=True),
        lax.all_to_all(v_send, "sp", split_axis=1, concat_axis=0, tiled=True),
    )
    k_every, v_every = (
        lax.all_gather(k_group, "blk", axis=0, tiled=True),
        lax.all_gather(v_group, "blk", axis=0, tiled=True),
    )
    group_rows = q_group.shape[0]
    block_rows = 512
    block_count = group_rows // block_rows
    q_blocks = q_group.reshape(block_count, block_rows, heads_here, HD)

    def attend(q_block):
        scores = (
            jnp.einsum("rhe,khe->hrk", q_block, k_every, preferred_element_type=jnp.float32) * scale
        )
        top_score = jnp.max(scores, -1, keepdims=True)
        raised = jnp.exp(scores - top_score)
        total = jnp.sum(raised, -1, keepdims=True)
        probs = (raised / total).astype(jnp.bfloat16)
        result = jnp.einsum("hrk,khe->rhe", probs, v_every, preferred_element_type=jnp.float32)
        return (result, (top_score + jnp.log(total))[..., 0])

    attended, log_total = lax.map(attend, q_blocks)
    att_send = attended.reshape(group_rows, heads_here, HD).astype(jnp.bfloat16)
    att_tok = lax.all_to_all(att_send, "sp", split_axis=0, concat_axis=1, tiled=True).reshape(
        tok_rows, width
    )
    a_lin = jnp.dot(att_tok, out_self, preferred_element_type=jnp.float32) + bias_all[3]
    x_one = tokens + mods[2] * a_lin
    normed_three = layer_norm(x_one)
    cross_in = (normed_three * gain_all[2] + bias_all[8]).astype(jnp.bfloat16)
    qc_lin = (
        jnp.dot(cross_in, qkv_cross[:, :width], preferred_element_type=jnp.float32) + bias_all[4]
    )
    q_cross = rms_norm(qc_lin, gain_all[3]).astype(jnp.bfloat16).reshape(tok_rows, H, HD)
    text_rows = text_tokens[0]
    kv_lin = jnp.dot(
        text_rows, qkv_cross[:, width:], preferred_element_type=jnp.float32
    ) + jnp.concatenate([bias_all[5], bias_all[6]])
    k_text = rms_norm(kv_lin[:, :width], gain_all[4]).astype(jnp.bfloat16)
    v_text = kv_lin[:, width:].astype(jnp.bfloat16)
    k_cross, v_cross = (
        lax.all_gather(k_text, ("blk", "sp"), axis=0, tiled=True),
        lax.all_gather(v_text, ("blk", "sp"), axis=0, tiled=True),
    )
    text_total = k_cross.shape[0]
    k_cross = k_cross.reshape(text_total, H, HD)
    v_cross = v_cross.reshape(text_total, H, HD)
    valid = jnp.arange(text_total, dtype=jnp.int32) < text_lengths[0]
    scores_c = (
        jnp.einsum("rhe,khe->hrk", q_cross, k_cross, preferred_element_type=jnp.float32) * scale
    )
    probs_c = softmax_rows(jnp.where(valid[None, None, :], scores_c, NEG))
    probs_cb = probs_c.astype(jnp.bfloat16)
    crossed = (
        jnp.einsum("hrk,khe->rhe", probs_cb, v_cross, preferred_element_type=jnp.float32)
        .reshape(tok_rows, width)
        .astype(jnp.bfloat16)
    )
    c_lin = jnp.dot(crossed, out_cross, preferred_element_type=jnp.float32) + bias_all[7]
    x_two = x_one + c_lin
    normed_two = layer_norm(x_two)
    ffn_rows = (normed_two * (1.0 + mods[4]) + mods[3]).astype(jnp.bfloat16)
    rows_every = spread_rows(ffn_rows)
    own_bias = lax.dynamic_slice_in_dim(bias_ffn, ff_start, ff_here, 0)
    u_lin = (
        jnp.einsum("td,fd->tf", rows_every, ffn_in, preferred_element_type=jnp.float32) + own_bias
    )
    g_act, gelu_back = jax.vjp(gelu_tanh, u_lin)
    g_low = g_act.astype(jnp.bfloat16)
    z_lin = group_share(jnp.dot(g_low, ffn_out, preferred_element_type=jnp.float32)) + bias_all[9]
    result = x_two + mods[5] * z_lin
    block_out = result.astype(jnp.bfloat16)[None]
    grad_y = cotangent[0].astype(jnp.float32)
    d_z = (grad_y * mods[5]).astype(jnp.bfloat16)
    d_gate2 = jnp.sum(grad_y * z_lin, 0)
    dz_every = spread_rows(d_z)
    d_g = jnp.einsum("td,fd->tf", dz_every, ffn_out, preferred_element_type=jnp.float32)
    d_u = gelu_back(d_g)[0].astype(jnp.bfloat16)
    g_bias_full = lax.dynamic_update_slice_in_dim(
        jnp.zeros((ff_total,), jnp.float32), col_sum(d_u), ff_start, 0
    )
    g_hidden_in = jnp.einsum("tf,td->fd", d_u, rows_every, preferred_element_type=jnp.float32)
    g_hidden_out = jnp.einsum("tf,td->fd", g_low, dz_every, preferred_element_type=jnp.float32)
    d_rows = group_share(jnp.einsum("tf,fd->td", d_u, ffn_in, preferred_element_type=jnp.float32))
    d_shift2 = jnp.sum(d_rows, 0)
    d_scale2 = jnp.sum(d_rows * normed_two, 0)
    d_x_two = grad_y + layer_back(x_two, d_rows * (1.0 + mods[4]))
    ffn_parts = (g_hidden_in, g_hidden_out)
    d_c = d_x_two.astype(jnp.bfloat16)
    g_out_cross = jnp.einsum("td,te->de", crossed, d_c, preferred_element_type=jnp.float32)
    d_oc = (
        jnp.einsum("te,de->td", d_c, out_cross, preferred_element_type=jnp.float32)
        .astype(jnp.bfloat16)
        .reshape(tok_rows, H, HD)
    )
    d_vc = jnp.einsum("hrk,rhe->khe", probs_cb, d_oc, preferred_element_type=jnp.float32)
    d_pc = jnp.einsum("rhe,khe->hrk", d_oc, v_cross, preferred_element_type=jnp.float32)
    d_sc = (probs_c * (d_pc - jnp.sum(probs_c * d_pc, -1, keepdims=True))).astype(jnp.bfloat16)
    d_qc = jnp.einsum("hrk,khe->rhe", d_sc, k_cross, preferred_element_type=jnp.float32) * scale
    d_kc = jnp.einsum("hrk,rhe->khe", d_sc, q_cross, preferred_element_type=jnp.float32) * scale
    d_kc_own, d_vc_own = (
        lax.psum_scatter(
            d_kc.reshape(text_total, width).astype(jnp.bfloat16),
            ("blk", "sp"),
            scatter_dimension=0,
            tiled=True,
        ).astype(jnp.float32),
        lax.psum_scatter(
            d_vc.reshape(text_total, width).astype(jnp.bfloat16),
            ("blk", "sp"),
            scatter_dimension=0,
            tiled=True,
        ).astype(jnp.float32),
    )
    d_kc_lin, d_gain4 = jax.vjp(rms_norm, kv_lin[:, :width], gain_all[4])[1](d_kc_own)
    d_kv_lin = jnp.concatenate([d_kc_lin.astype(jnp.bfloat16), d_vc_own.astype(jnp.bfloat16)], -1)
    d_qc_lin, d_gain3 = jax.vjp(rms_norm, qc_lin, gain_all[3])[1](d_qc.reshape(tok_rows, width))
    d_qc_low = d_qc_lin.astype(jnp.bfloat16)
    g_qkv_cross = jnp.concatenate(
        [
            jnp.einsum("td,te->de", cross_in, d_qc_low, preferred_element_type=jnp.float32),
            jnp.einsum("td,te->de", text_rows, d_kv_lin, preferred_element_type=jnp.float32),
        ],
        1,
    )
    grad_text = jnp.einsum(
        "te,de->td", d_kv_lin, qkv_cross[:, width:], preferred_element_type=jnp.float32
    )
    d_cross_in = jnp.einsum(
        "te,de->td", d_qc_low, qkv_cross[:, :width], preferred_element_type=jnp.float32
    )
    d_gain2 = jnp.sum(d_cross_in * normed_three, 0)
    d_bias8 = jnp.sum(d_cross_in, 0)
    d_x_one = d_x_two + layer_back(x_one, d_cross_in * gain_all[2])
    d_a = (d_x_one * mods[2]).astype(jnp.bfloat16)
    d_gate1 = jnp.sum(d_x_one * a_lin, 0)
    g_out_self = jnp.einsum("td,te->de", att_tok, d_a, preferred_element_type=jnp.float32)
    d_att = (
        jnp.einsum("te,de->td", d_a, out_self, preferred_element_type=jnp.float32)
        .astype(jnp.bfloat16)
        .reshape(tok_rows, H, HD)
    )
    d_o_group = lax.all_to_all(d_att, "sp", split_axis=1, concat_axis=0, tiled=True)

    def back_block(carry, pieces):
        acc_k, acc_v = carry
        q_block, do_block, lse_block = pieces
        scores = (
            jnp.einsum("rhe,khe->hrk", q_block, k_every, preferred_element_type=jnp.float32) * scale
        )
        probs = jnp.exp(scores - lse_block[..., None])
        acc_v = acc_v + jnp.einsum(
            "hrk,rhe->khe", probs.astype(jnp.bfloat16), do_block, preferred_element_type=jnp.float32
        )
        d_p = jnp.einsum("rhe,khe->hrk", do_block, v_every, preferred_element_type=jnp.float32)
        d_s = (probs * (d_p - jnp.sum(probs * d_p, -1, keepdims=True))).astype(jnp.bfloat16)
        d_q = jnp.einsum("hrk,khe->rhe", d_s, k_every, preferred_element_type=jnp.float32) * scale
        acc_k = (
            acc_k
            + jnp.einsum("hrk,rhe->khe", d_s, q_block, preferred_element_type=jnp.float32) * scale
        )
        return ((acc_k, acc_v), d_q)

    empty_keys = jnp.zeros(k_every.shape, jnp.float32)
    (acc_k, acc_v), d_q_blocks = lax.scan(
        back_block,
        (empty_keys, empty_keys),
        (q_blocks, d_o_group.reshape(block_count, block_rows, heads_here, HD), log_total),
    )
    d_k_own, d_v_own = (
        lax.psum_scatter(acc_k.astype(jnp.bfloat16), "blk", scatter_dimension=0, tiled=True).astype(
            jnp.float32
        ),
        lax.psum_scatter(acc_v.astype(jnp.bfloat16), "blk", scatter_dimension=0, tiled=True).astype(
            jnp.float32
        ),
    )
    d_q_send = d_q_blocks.reshape(group_rows, heads_here, HD).astype(jnp.bfloat16)
    d_q_tok, d_k_tok, d_v_tok = (
        lax.all_to_all(d_q_send, "sp", split_axis=0, concat_axis=1, tiled=True),
        lax.all_to_all(d_k_own.astype(jnp.bfloat16), "sp", split_axis=0, concat_axis=1, tiled=True),
        lax.all_to_all(d_v_own.astype(jnp.bfloat16), "sp", split_axis=0, concat_axis=1, tiled=True),
    )
    d_q_lin, d_gain0 = jax.vjp(turn, q_lin, gain_all[0])[1](d_q_tok.astype(jnp.float32))
    d_k_lin, d_gain1 = jax.vjp(turn, k_lin, gain_all[1])[1](d_k_tok.astype(jnp.float32))
    d_proj = jnp.concatenate(
        [
            d_q_lin.astype(jnp.bfloat16),
            d_k_lin.astype(jnp.bfloat16),
            d_v_tok.reshape(tok_rows, width),
        ],
        -1,
    )
    g_qkv_self = jnp.einsum("td,te->de", shifted, d_proj, preferred_element_type=jnp.float32)
    d_shift = jnp.einsum("te,de->td", d_proj, qkv_self, preferred_element_type=jnp.float32)
    d_shift1 = jnp.sum(d_shift, 0)
    d_scale1 = jnp.sum(d_shift * normed_one, 0)
    grad_tokens = d_x_one + layer_back(tokens, d_shift * (1.0 + mods[1]))
    proj_sums = col_sum(d_proj)
    kv_sums = col_sum(d_kv_lin)
    g_mods = jnp.stack([d_shift1, d_scale1, d_gate1, d_shift2, d_scale2, d_gate2])
    g_gains = jnp.stack([d_gain0, d_gain1, d_gain2, d_gain3, d_gain4])
    g_biases = jnp.stack(
        [
            proj_sums[:width],
            proj_sums[width : 2 * width],
            proj_sums[2 * width :],
            col_sum(d_a),
            col_sum(d_qc_low),
            kv_sums[:width],
            kv_sums[width:],
            col_sum(d_c),
            d_bias8,
            col_sum(d_z),
        ]
    )
    attn_parts = tuple(
        (
            lax.psum_scatter(
                g_qkv_cross.astype(jnp.bfloat16), ("blk", "sp"), scatter_dimension=0, tiled=True
            ).astype(jnp.float32),
            lax.psum_scatter(
                g_out_cross.astype(jnp.bfloat16), ("blk", "sp"), scatter_dimension=0, tiled=True
            ).astype(jnp.float32),
            lax.psum_scatter(
                g_qkv_self.astype(jnp.bfloat16), ("blk", "sp"), scatter_dimension=0, tiled=True
            ).astype(jnp.float32),
            lax.psum_scatter(
                g_out_self.astype(jnp.bfloat16), ("blk", "sp"), scatter_dimension=0, tiled=True
            ).astype(jnp.float32),
            lax.psum_scatter(
                g_bias_full.astype(jnp.bfloat16), ("blk", "sp"), scatter_dimension=0, tiled=True
            ).astype(jnp.float32),
            lax.psum_scatter(
                g_mods.astype(jnp.bfloat16), ("blk", "sp"), scatter_dimension=1, tiled=True
            ).astype(jnp.float32),
            lax.psum_scatter(
                g_gains.astype(jnp.bfloat16), ("blk", "sp"), scatter_dimension=1, tiled=True
            ).astype(jnp.float32),
            lax.psum_scatter(
                g_biases.astype(jnp.bfloat16), ("blk", "sp"), scatter_dimension=1, tiled=True
            ).astype(jnp.float32),
        )
    )
    every_part = clip_total(ffn_parts + attn_parts)
    (
        part_in,
        part_out,
        part_cqkv,
        part_cout,
        part_sqkv,
        part_sout,
        part_bias,
        part_mods,
        part_gains,
        part_biases,
    ) = every_part
    return (
        block_out,
        grad_tokens[None],
        grad_text[None],
        part_mods,
        part_gains,
        part_biases,
        part_sqkv,
        part_sout,
        part_cqkv,
        part_cout,
        part_in,
        part_out,
        part_bias,
    )


def solution(mesh):
    return jax.shard_map(
        local,
        mesh=mesh,
        in_specs=(
            P("dp", ("blk", "sp"), None),
            P("dp", ("blk", "sp"), None),
            P("dp"),
            P("dp", None, ("blk", "sp")),
            P("dp", None, None),
            P(None, ("blk", "sp")),
            P(None, ("blk", "sp")),
            P(None, ("blk", "sp")),
            P(("blk", "sp"), None),
            P(("blk", "sp"), None),
            P(("blk", "sp"), None),
            P(("blk", "sp"), None),
            P(("blk", "sp"), None),
            P(("blk", "sp"), None),
            P(("blk", "sp")),
            P("dp", ("blk", "sp"), None),
        ),
        out_specs=(
            P("dp", ("blk", "sp"), None),
            P("dp", ("blk", "sp"), None),
            P("dp", ("blk", "sp"), None),
            P(None, ("blk", "sp")),
            P(None, ("blk", "sp")),
            P(None, ("blk", "sp")),
            P(("blk", "sp"), None),
            P(("blk", "sp"), None),
            P(("blk", "sp"), None),
            P(("blk", "sp"), None),
            P(("blk", "sp"), None),
            P(("blk", "sp"), None),
            P(("blk", "sp")),
        ),
        check_vma=False,
    )
```

profile of v0, /device:TPU:27, one launch (start us, length us, event | category | flops | bytes accessed | tf_op | source)
XLA Modules:
  0.0 2647.0 jit_solution(12979912120546239138)
XLA Ops:
  92.7 113.0 %all-gather.14.cloned.1.call-done = bf16[1536,4608]{1,0:T(8,128)(2,1)} async-done(((bf16[192,4608]{1,0:T(8,128)(2,1)}), bf16[1536,4608]{1,0:T(8,128)(2,1)}) %all-gather.14.cloned.1.call-update) | async-done | bytes 14155792 | tf_op jit(solution)/shard_map/all_gather | solution.py:119
  272.6 37.6 %all_to_all.114 = bf16[256,12,128]{0,2,1:T(8,128)(2,1)} all-to-all(bf16[256,12,128]{0,2,1:T(8,128)(2,1)S(1)} %get-tuple-element.431), channel_id=1, replica_groups=mesh['dp'=4,'blk'=2,'sp'=4] {'sp'}, dimensions={1} | all-to-all | bytes 1572864 | tf_op jit(solution)/shard_map/all_to_all | solution.py:157
  312.5 122.5 %all-gather.22.cloned.1.call-done = bf16[1536,4608]{1,0:T(8,128)(2,1)} async-done(((bf16[192,4608]{1,0:T(8,128)(2,1)}), bf16[1536,4608]{1,0:T(8,128)(2,1)}) %all-gather.22.cloned.1.call-update) | async-done | bytes 14155792 | tf_op jit(solution)/shard_map/all_gather | solution.py:121
  524.0 30.9 %all-gather.26.cloned.1.call-done = bf16[512,1536]{1,0:T(8,128)(2,1)} async-done(((bf16[64,1536]{1,0:T(8,128)(2,1)}), bf16[512,1536]{1,0:T(8,128)(2,1)}) %all-gather.26.cloned.1.call-update) | async-done | bytes 1572880 | tf_op jit(solution)/shard_map/all_gather | solution.py:200
  557.5 43.5 %all-gather.24.cloned.1.call-done = bf16[512,1536]{1,0:T(8,128)(2,1)} async-done(((bf16[64,1536]{1,0:T(8,128)(2,1)}), bf16[512,1536]{1,0:T(8,128)(2,1)}) %all-gather.24.cloned.1.call-update) | async-done | bytes 1572880 | tf_op jit(solution)/shard_map/all_gather | solution.py:201
  608.1 73.2 %all-gather.20.cloned.1.call-done = bf16[1536,1536]{1,0:T(8,128)(2,1)} async-done(((bf16[192,1536]{1,0:T(8,128)(2,1)}), bf16[1536,1536]{1,0:T(8,128)(2,1)}) %all-gather.20.cloned.1.call-update) | async-done | bytes 4718608 | tf_op jit(solution)/shard_map/all_gather | solution.py:120
  708.2 53.3 %all-gather.28.cloned.1.call-done = bf16[1536,1536]{1,0:T(8,128)(2,1)} async-done(((bf16[192,1536]{1,0:T(8,128)(2,1)}), bf16[1536,1536]{1,0:T(8,128)(2,1)}) %all-gather.28.cloned.1.call-update) | async-done | bytes 4718608 | tf_op jit(solution)/shard_map/all_gather | solution.py:122
  770.1 27.7 %all-reduce.4 = bf16[8960]{0:T(1024)(128)(2,1)S(1)} all-reduce(bf16[8960]{0:T(1024)(128)(2,1)S(1)} %dynamic-update-slice), channel_id=1, replica_groups=mesh['dp'=4,'blk'=2,'sp'=4] {'blk','sp'}, use_global_device_ids=true, to_apply=%add.4 | all-reduce | flops 8960 | bytes 35840
  797.9 64.7 %all-gather.32.cloned.1.call-done = bf16[2048,1536]{1,0:T(8,128)(2,1)} async-done(((bf16[256,1536]{1,0:T(8,128)(2,1)}), bf16[2048,1536]{1,0:T(8,128)(2,1)}) %all-gather.32.cloned.1.call-update) | async-done | bytes 6291472 | tf_op jit(solution)/shard_map/all_gather | solution.py:91
  875.5 86.8 %all-gather.30.cloned.1.call-done = bf16[2048,1536]{1,0:T(8,128)(2,1)} async-done(((bf16[256,1536]{1,0:T(8,128)(2,1)}), bf16[2048,1536]{1,0:T(8,128)(2,1)}) %all-gather.30.cloned.1.call-update) | async-done | bytes 6291472 | tf_op jit(solution)/shard_map/all_gather | solution.py:91
  1010.3 98.6 %reduce-scatter.22.cloned.1.call-done = bf16[256,1536]{1,0:T(8,128)(2,1)} async-done(((bf16[2048,1536]{1,0:T(8,128)(2,1)}), bf16[256,1536]{1,0:T(8,128)(2,1)}) %reduce-scatter.22.cloned.1.call-update) | async-done | bytes 786448 | tf_op jit(solution)/shard_map/reduce_scatter | solution.py:95
  1111.2 118.2 %reduce-scatter.20.cloned.1.call-done = bf16[256,1536]{1,0:T(8,128)(2,1)} async-done(((bf16[2048,1536]{1,0:T(8,128)(2,1)}), bf16[256,1536]{1,0:T(8,128)(2,1)}) %reduce-scatter.20.cloned.1.call-update) | async-done | bytes 786448 | tf_op jit(solution)/shard_map/reduce_scatter | solution.py:95
  1301.8 49.4 %while.28 = (s32[]{:T(128)}, f32[2048,3,128]{0,2,1:T(8,128)}, f32[2048,3,128]{0,2,1:T(8,128)}, bf16[2,512,3,128]{3,1,0,2:T(8,128)(2,1)}, bf16[2,512,3,128]{3,1,2...) while((s32[]{:T(128)}, f32[2048,3,128]{0,2,1:T(8,128)}, ...), condition=%wide.region_26.27_spmd.clone, body=%wide.region_24.26_spmd.clone.sunk | while | flops 4068407808 | bytes 176994704 | solution.py:323
  1436.6 63.3 %all-reduce.16.cloned.1.call-done = (bf16[2048,3,128]{2,1,0:T(4,128)(2,1)}, bf16[2048,3,128]{2,1,0:T(4,128)(2,1)}) async-done(((bf16[2048,3,128]{2,1,0:T(4,128)(2,1)}, bf16[2048,3,128]{2,1,0:T(4,128)(2,1)}), (bf16[2048,3,128]{2,1,0:T(4,128)(2,1)}, bf16[2048,3,128]{2,1,0:T(4,128)(2,1)})) %all-reduce.16.cloned.1.call-update) | async-done | bytes 3145744
  1509.5 37.4 %all-to-all-done.7 = bf16[1024,3,128]{2,1,0:T(4,128)(2,1)S(1)} async-done(((bf16[1024,3,128]{2,1,0:T(4,128)(2,1)}), bf16[1024,3,128]{2,1,0:T(4,128)(2,1)S(1)}, u32[]{:S(2)}, u32[]{:S(2)}) %all-to-all-start.7) | async-done | bytes 786464 | tf_op jit(solution)/shard_map/all_to_all | solution.py:340
  1563.8 40.0 %all-to-all-done.6 = bf16[1024,3,128]{2,1,0:T(4,128)(2,1)} async-done(((bf16[1024,3,128]{2,1,0:T(4,128)(2,1)}), bf16[1024,3,128]{2,1,0:T(4,128)(2,1)}, u32[]{:S(2)}, u32[]{:S(2)}) %all-to-all-start.6) | async-done | bytes 786464 | tf_op jit(solution)/shard_map/all_to_all | solution.py:339
  1678.2 98.3 %reduce-scatter.40.cloned.1.call-done = bf16[192,4608]{1,0:T(8,128)(2,1)} async-done(((bf16[1536,4608]{1,0:T(8,128)(2,1)}), bf16[192,4608]{1,0:T(8,128)(2,1)}) %reduce-scatter.40.cloned.1.call-update) | async-done | bytes 1769488
  1780.6 95.6 %reduce-scatter.32.cloned.1.call-done = bf16[192,1536]{1,0:T(8,128)(2,1)} async-done(((bf16[1536,1536]{1,0:T(8,128)(2,1)}), bf16[192,1536]{1,0:T(8,128)(2,1)}) %reduce-scatter.32.cloned.1.call-update) | async-done | bytes 589840 | tf_op jit(solution)/shard_map/reduce_scatter | solution.py:380
  1876.2 99.6 %reduce-scatter.30.cloned.1.call-done = bf16[192,1536]{1,0:T(8,128)(2,1)} async-done(((bf16[1536,1536]{1,0:T(8,128)(2,1)}), bf16[192,1536]{1,0:T(8,128)(2,1)}) %reduce-scatter.30.cloned.1.call-update) | async-done | bytes 589840 | tf_op jit(solution)/shard_map/reduce_scatter | solution.py:386
  1975.7 232.4 %reduce-scatter.28.cloned.1.call-done = bf16[192,4608]{1,0:T(8,128)(2,1)} async-done(((bf16[1536,4608]{1,0:T(8,128)(2,1)}), bf16[192,4608]{1,0:T(8,128)(2,1)}) %reduce-scatter.28.cloned.1.call-update) | async-done | bytes 1769488 | tf_op jit(solution)/shard_map/reduce_scatter | solution.py:383
  2242.7 27.4 %reduce-scatter.36.cloned.1.call-done = bf16[192,5]{1,0:T(8,128)(2,1)} async-done(((bf16[1536,5]{1,0:T(8,128)(2,1)}), bf16[192,5]{1,0:T(8,128)(2,1)}) %reduce-scatter.36.cloned.1.call-update) | async-done | bytes 1936
  2271.1 63.7 %reduce-scatter.34.cloned.1.call-done = bf16[192,6]{1,0:T(8,128)(2,1)} async-done(((bf16[1536,6]{1,0:T(8,128)(2,1)}), bf16[192,6]{1,0:T(8,128)(2,1)}) %reduce-scatter.34.cloned.1.call-update) | async-done | bytes 2320
  2335.7 63.8 %reduce-scatter.38.cloned.1.call-done = bf16[192,10]{1,0:T(8,128)(2,1)} async-done(((bf16[1536,10]{1,0:T(8,128)(2,1)}), bf16[192,10]{1,0:T(8,128)(2,1)}) %reduce-scatter.38.cloned.1.call-update) | async-done | bytes 3856
  2414.9 207.6 %all-reduce.14.cloned.1.call-done = (bf16[192,4608]{0,1:T(8,128)(2,1)}, bf16[192,4608]{1,0:T(8,128)(2,1)}, bf16[192,1536]{1,0:T(8,128)(2,1)}, bf16[192,1536]{1,0...) async-done(((bf16[192,4608]{0,1:T(8,128)(2,1)}, bf16[192,4608]{1,0:T(8,128)(2,1)}, bf16[192,1536]{1,0:T(8,128)(2,1)}, bf16[192,1536]{1,0:T(8,128)(2,1)}, ...) | async-done | bytes 11599888 | tf_op jit(solution)/shard_map/psum | solution.py:86
  (597 shorter events, 750.5 us)
Async XLA Ops:
  7.2 198.4 %all-gather.14.cloned.1.call-start = ((), (), s32[]{:S(2)}) async-start(), calls=%async_computation.19 | async-start | bytes 15925248 | tf_op jit(solution)/shard_map/all_gather | solution.py:119
  8.0 427.0 %all-gather.22.cloned.1.call-start = ((), (), s32[]{:S(2)}) async-start(), calls=%async_computation.23 | async-start | bytes 15925248 | tf_op jit(solution)/shard_map/all_gather | solution.py:121
  224.5 248.3 %all-gather.18.cloned.1.call-start = ((), (), s32[]{:S(2)}) async-start(), calls=%async_computation.21 | async-start | bytes 2359296 | tf_op jit(solution)/shard_map/all_gather | solution.py:162
  267.0 226.6 %all-gather.16.cloned.1.call-start = ((), (), s32[]{:S(2)}) async-start(), calls=%async_computation.20 | async-start | bytes 2359296 | tf_op jit(solution)/shard_map/all_gather | solution.py:161
  312.5 242.5 %all-gather.26.cloned.1.call-start = ((), (), s32[]{:S(2)}) async-start(), calls=%async_computation.25 | async-start | bytes 1769472 | tf_op jit(solution)/shard_map/all_gather | solution.py:200
  442.3 158.7 %all-gather.24.cloned.1.call-start = ((), (), s32[]{:S(2)}) async-start(), calls=%async_computation.24 | async-start | bytes 1769472 | tf_op jit(solution)/shard_map/all_gather | solution.py:201
  444.0 237.3 %all-gather.20.cloned.1.call-start = ((), (), s32[]{:S(2)}) async-start(), calls=%async_computation.22 | async-start | bytes 5308416 | tf_op jit(solution)/shard_map/all_gather | solution.py:120
  444.8 316.7 %all-gather.28.cloned.1.call-start = ((), (), s32[]{:S(2)}) async-start(), calls=%async_computation.26 | async-start | bytes 5308416 | tf_op jit(solution)/shard_map/all_gather | solution.py:122
  451.4 411.2 %all-gather.32.cloned.1.call-start = ((), (), s32[]{:S(2)}) async-start(), calls=%async_computation.29 | async-start | bytes 7077888 | tf_op jit(solution)/shard_map/all_gather | solution.py:91
  518.8 84.8 %all-to-all-start.3 = ((bf16[1024,3,128]{2,1,0:T(4,128)(2,1)}), bf16[1024,3,128]{2,1,0:T(4,128)(2,1)}, u32[]{:S(2)}, u32[]{:S(2)}) async-start(bf16[1024,3,128]{2,1,0:T(4,128)(2,1)} %copy.324), calls=%async_computation.3 | async-start | bytes 2097152 | tf_op jit(solution)/shard_map/all_to_all | solution.py:182
  523.4 439.0 %all-gather.30.cloned.1.call-start = ((), (), s32[]{:S(2)}) async-start(), calls=%async_computation.27 | async-start | bytes 7077888 | tf_op jit(solution)/shard_map/all_gather | solution.py:91
  768.5 340.4 %reduce-scatter.22.cloned.1.call-start = ((), (), s32[]{:S(2)}) async-start(), calls=%async_computation.30 | async-start | bytes 7077888 | tf_op jit(solution)/shard_map/reduce_scatter | solution.py:95
  991.5 237.9 %reduce-scatter.20.cloned.1.call-start = ((), (), s32[]{:S(2)}) async-start(), calls=%async_computation.28 | async-start | bytes 7077888 | tf_op jit(solution)/shard_map/reduce_scatter | solution.py:95
  1010.0 359.8 %reduce-scatter.24.cloned.1.call-start = ((), (), s32[]{:S(2)}) async-start(), calls=%async_computation.31 | async-start | bytes 1769472 | tf_op jit(solution)/shard_map/reduce_scatter | solution.py:260
  1279.6 107.6 %reduce-scatter.26.cloned.1.call-start = ((), (), s32[]{:S(2)}) async-start(), calls=%async_computation.32 | async-start | bytes 1769472 | tf_op jit(solution)/shard_map/reduce_scatter | solution.py:266
  1284.8 215.1 %all-reduce.16.cloned.1.call-start = ((), (), s32[]{:S(2)}) async-start(), calls=%async_computation.41 | async-start | bytes 8388608
  1364.5 412.1 %reduce-scatter.40.cloned.1.call-start = ((), (), s32[]{:S(2)}) async-start(), calls=%async_computation.39 | async-start | bytes 15925248
  1418.1 458.0 %reduce-scatter.32.cloned.1.call-start = ((), (), s32[]{:S(2)}) async-start(), calls=%async_computation.35 | async-start | bytes 5308416 | tf_op jit(solution)/shard_map/reduce_scatter | solution.py:380
  1423.1 552.7 %reduce-scatter.30.cloned.1.call-start = ((), (), s32[]{:S(2)}) async-start(), calls=%async_computation.34 | async-start | bytes 5308416 | tf_op jit(solution)/shard_map/reduce_scatter | solution.py:386
  1560.0 648.1 %reduce-scatter.28.cloned.1.call-start = ((), (), s32[]{:S(2)}) async-start(), calls=%async_computation.33 | async-start | bytes 15925248 | tf_op jit(solution)/shard_map/reduce_scatter | solution.py:383
  1632.8 637.4 %reduce-scatter.36.cloned.1.call-start = ((), (), s32[]{:S(2)}) async-start(), calls=%async_computation.37 | async-start | bytes 442368
  1659.2 675.6 %reduce-scatter.34.cloned.1.call-start = ((), (), s32[]{:S(2)}) async-start(), calls=%async_computation.36 | async-start | bytes 442368
  1664.8 734.6 %reduce-scatter.38.cloned.1.call-start = ((), (), s32[]{:S(2)}) async-start(), calls=%async_computation.38 | async-start | bytes 442368
  1666.0 956.5 %all-reduce.14.cloned.1.call-start = ((), (), s32[]{:S(2)}) async-start(), calls=%async_computation.40 | async-start | bytes 24379392 | tf_op jit(solution)/shard_map/psum | solution.py:86
  (160 other events, 5563.5 us)
Sparse Core Ops, SparseCore 0:
  10.2 195.4 all-gather.13
  207.8 227.2 all-gather.21
  437.2 27.1 all-gather.17
  466.4 27.1 all-gather.15
  496.1 58.7 all-gather.25
  557.5 43.4 all-gather.23
  603.1 78.1 all-gather.19
  683.4 78.0 all-gather.27
  764.2 98.3 all-gather.31
  865.1 97.2 all-gather.29
  991.7 117.1 reduce-scatter.21
  1112.3 117.1 reduce-scatter.19
  1254.9 64.2 reduce-scatter.23
  1323.4 63.7 reduce-scatter.25
  1390.1 109.7 all-reduce.15
  1503.8 272.7 reduce-scatter.39
  1781.1 95.0 reduce-scatter.31
  1880.7 95.0 reduce-scatter.29
  1979.8 228.2 reduce-scatter.27
  2211.5 58.6 reduce-scatter.35
  2274.4 60.3 reduce-scatter.33
  2339.0 60.3 reduce-scatter.37
  2404.0 218.4 all-reduce.13
where the time goes:
time: 2660 us; the launch traced here: 2650 us
  waiting for transfers between devices  1930 us (73%)
  matrix products  232 us (9%)
  blocking collectives  177 us (7%)
  local copies, waits for them, and re-layouts  149 us (6%)
  other arithmetic  99 us (4%)
  starting transfers between devices  45.5 us (2%)
    unnamed x28, waiting for transfers between devices  320 us
    reduce_scatter x1, waiting for transfers between devices, local(): lax.psum_scatter(g_qkv_self.astype(jnp.bfloat16), ('blk', 'sp'), scatter_...  232 us
    reduce_scatter x2, waiting for transfers between devices, group_share(): lax.psum_scatter(terms.astype(jnp.bfloat16), ('blk', 'sp'), scatter_dimen...  217 us
    psum x1, waiting for transfers between devices, clip_total(): lax.psum(as_sent(parts), 'dp')  208 us
    all_gather x2, waiting for transfers between devices, spread_rows(): return lax.all_gather(rows, ('blk', 'sp'), axis=0, tiled=True)  152 us
    all_gather x1, waiting for transfers between devices, local(): lax.all_gather(cross_qkv, ('blk', 'sp'), axis=0, tiled=True)  123 us
    all_gather x1, waiting for transfers between devices, local(): lax.all_gather(self_qkv, ('blk', 'sp'), axis=0, tiled=True)  113 us
    reduce_scatter x1, waiting for transfers between devices, local(): lax.psum_scatter(g_out_self.astype(jnp.bfloat16), ('blk', 'sp'), scatter_...  99.6 us
  transfers between devices with their start and end apart: 30, of which 26 were waited for; matrix products, arithmetic and copies ran while one was open for 14% of the time, Pallas kernels for 0%

commit v1 on v0

v1 whole, which is shorter than its diff:
```python
import functools

import jax
import jax.numpy as jnp
import numpy as np
from jax import lax
from jax.experimental import pallas as pl
from jax.experimental.pallas import tpu as pltpu
from jax.sharding import PartitionSpec as P

H = 12
HD = 128


EPS = 1e-06
NEG = -1e30


def layer_norm(values):
    centre = values - jnp.mean(values, axis=-1, keepdims=True)
    return centre * lax.rsqrt(jnp.mean(centre * centre, axis=-1, keepdims=True) + EPS)


def rms_norm(values, gain_row):
    return values * lax.rsqrt(jnp.mean(values * values, axis=-1, keepdims=True) + EPS) * gain_row


def layer_back(values, grad_out):
    return jax.vjp(layer_norm, values)[1](grad_out)[0]


def rope_tables(head_dim):
    pair_count = head_dim // 2
    side_count = head_dim // 6
    first_count = pair_count - 2 * side_count
    tables = np.zeros((3, pair_count))
    for column in range(pair_count):
        if column < first_count:
            tables[0, column] = 10000.0 ** (-column / first_count)
        elif column < first_count + side_count:
            tables[1, column] = 10000.0 ** (-(column - first_count) / side_count)
        else:
            tables[2, column] = 10000.0 ** (-(column - first_count - side_count) / side_count)
    return tables


def rotate(values, cosine, sine_part):
    half_dim = values.shape[-1] // 2
    turned = jnp.concatenate([-values[..., half_dim:], values[..., :half_dim]], -1)
    return values * cosine[:, None, :] + turned * sine_part[:, None, :]


def softmax_rows(scores):
    top_score = jnp.max(scores, -1, keepdims=True)
    raised = jnp.exp(scores - top_score)
    return raised / jnp.sum(raised, -1, keepdims=True)


def col_sum(values):
    return jnp.sum(values.astype(jnp.float32), 0)


def gelu_tanh(inner):
    return jax.nn.gelu(inner, approximate=True)


BF = jnp.bfloat16
F32 = jnp.float32


MESH = pl.DeviceIdType.MESH
PARAM_ROWS = 32
SMALL_ROWS = 16 + PARAM_ROWS
SMALL_LANES = 256


def remote_copy(src, dst, send, recv, target):
    return pltpu.make_async_remote_copy(
        src_ref=src,
        dst_ref=dst,
        send_sem=send,
        recv_sem=recv,
        device_id=target,
        device_id_type=MESH,
    )


def meet(targets):
    barrier = pltpu.get_barrier_semaphore()
    for target in targets:
        pl.semaphore_signal(barrier, inc=1, device_id=target, device_id_type=MESH)
    pl.semaphore_wait(barrier, len(targets))


def rows_at(start, size):
    return pl.ds(pl.multiple_of(start, 16), size)


def lanes_at(start, size):
    return pl.ds(pl.multiple_of(start, 128), size)


def mm(a, b):
    return lax.dot_general(a, b, (((1,), (0,)), ((), ())), preferred_element_type=F32)


def mm_t(a, b):
    return lax.dot_general(a, b, (((1,), (1,)), ((), ())), preferred_element_type=F32)


def mm_first(a, b):
    return lax.dot_general(a, b, (((0,), (0,)), ((), ())), preferred_element_type=F32)


def exact_first(a, b):
    return lax.dot_general(
        a,
        b,
        (((0,), (0,)), ((), ())),
        precision=lax.Precision.HIGHEST,
        preferred_element_type=F32,
    )


def exact_sums(values):
    ones = jnp.ones((8, values.shape[1]), F32)
    return lax.dot_general(
        ones,
        values,
        (((1,), (1,)), ((), ())),
        precision=lax.Precision.HIGHEST,
        preferred_element_type=F32,
    )


def row_pick(which):
    return (lax.broadcasted_iota(jnp.int32, (8, 128), 0) == which).astype(F32)


def turn_sign():
    lane = lax.broadcasted_iota(jnp.int32, (1, HD), 1)
    return jnp.where(lane < HD // 2, -1.0, 1.0).astype(F32)


def turned(value, cosine, sine):
    return value * cosine + pltpu.roll(value, HD // 2, 1) * (sine * turn_sign())


def front_kernel(
    n_sp,
    x_ref,
    small_ref,
    qkv_ref,
    rest_ref,
    in_ref,
    out_ref,
    text_ref,
    cot_ref,
    time_ref,
    table_ref,
    par_ref,
    h1_out,
    w_out_ref,
    lin_out,
    rho_out,
    trig_out,
    q_out,
    kv_out,
    lse_out,
    att_out,
    tok_out,
    rest_out,
    in_out,
    out_out,
    text_out,
    cot_out,
    xall_ref,
    sall_ref,
    w_ref,
    lin_ref,
    sums_ref,
    rho_ref,
    trig_ref,
    q_ref,
    kv_ref,
    acc_ref,
    stat_ref,
    att_ref,
    h1_ref,
    *sems,
):
    lo, zs, zr, ss, sr, ws, wr, xs, xr, cs, cr, ps, pr, vs, vr, qs, qr, ts, tr, out = sems[:20]
    (ls, lr, lxs, lxr, lys, lyr, lcs, lcr, fs, fr, es, er, exs, exr, os, osr) = sems[20:]
    spot_d = lax.axis_index("dp")
    spot_b = lax.axis_index("blk")
    spot_s = lax.axis_index("sp")
    core = lax.rem(spot_d, 2)
    pair = lax.rem(spot_d // 2, 2)
    core_id = {"dp": spot_d + 1 - 2 * core}
    pair_id = {"dp": spot_d + 2 - 4 * pair}
    blk_id = {"blk": 1 - spot_b}
    line = [{"sp": lax.rem(spot_s + step, n_sp)} for step in range(1, n_sp)]
    rows = x_ref.shape[0]
    shard = qkv_ref.shape[0]
    half = shard // 2
    cols = w_ref.shape[1] // 3
    wide = qkv_ref.shape[1] // 3
    heads_here = cols // HD
    total_rows = n_sp * rows
    sums_ref[spot_s] = jnp.zeros((8, total_rows), F32)
    meet(line + [core_id, blk_id, pair_id])

    def w_rows(blk, spot, part):
        return rows_at((blk * n_sp + spot) * shard + part * half, half)

    here = spot_b * n_sp + spot_s
    keep = [
        pltpu.make_async_copy(
            qkv_ref.at[:, lanes_at(j * wide + spot_s * cols, cols)],
            w_ref.at[rows_at(here * shard, shard), pl.ds(j * cols, cols)],
            lo.at[j],
        )
        for j in range(3)
    ]
    keep.append(pltpu.make_async_copy(x_ref, xall_ref.at[rows_at(spot_s * rows, rows)], lo.at[3]))
    keep.append(pltpu.make_async_copy(small_ref, sall_ref.at[here], lo.at[4]))
    for copy in keep:
        copy.start()
    small_away = [
        remote_copy(small_ref, sall_ref.at[here], ss.at[k], sr.at[k], line[k])
        for k in range(n_sp - 1)
    ]
    for copy in small_away:
        copy.start()
    w_away = []
    for k in range(n_sp - 1):
        spot = lax.rem(spot_s + k + 1, n_sp)
        for j in range(3):
            copy = remote_copy(
                qkv_ref.at[rows_at(core * half, half), lanes_at(j * wide + spot * cols, cols)],
                w_ref.at[w_rows(spot_b, spot_s, core), pl.ds(j * cols, cols)],
                ws.at[3 * k + j],
                wr.at[3 * k + j],
                line[k],
            )
            copy.start()
            w_away.append(copy)

    def sends(way, k):
        if way == 0:
            return jnp.logical_and(spot_s < n_sp - 1, spot_s >= k)
        return jnp.logical_and(spot_s > 0, spot_s + k < n_sp)

    def gets(way, k):
        return spot_s > k if way == 0 else spot_s + k + 1 < n_sp

    def line_gather(first, place, pieces, send, recv, then=None):
        def copy(way, k, part):
            block = spot_s - k if way == 0 else spot_s + k
            at = place(block, part)
            src = first(part) if k == 0 else at
            target = {"sp": spot_s + 1 if way == 0 else spot_s - 1}
            index = (way * (n_sp - 1) + k) * pieces + part
            return remote_copy(src, at, send.at[index], recv.at[index], target)

        def step(k):
            for part in range(pieces):
                for way in range(2):
                    if k > 0:

                        @pl.when(gets(way, k - 1))
                        def _():
                            copy(way, k - 1, part).wait_recv()

                    if k < n_sp - 1:

                        @pl.when(sends(way, k))
                        def _():
                            copy(way, k, part).start()

                    if k > 0 and then is not None:

                        @pl.when(gets(way, k - 1))
                        def _():
                            then(spot_s - k if way == 0 else spot_s + k)

        def sent():
            for k in range(n_sp - 1):
                for part in range(pieces):
                    for way in range(2):

                        @pl.when(sends(way, k))
                        def _():
                            copy(way, k, part).wait_send()

        return step, sent

    pieces = 2
    piece = rows // pieces
    token_step, token_sent = line_gather(
        lambda part: x_ref.at[pl.ds(part * piece, piece)],
        lambda block, part: xall_ref.at[rows_at(block * rows + part * piece, piece)],
        pieces,
        zs,
        zr,
    )

    fourth = shard // 4
    quarter = core * 2 + pair

    def rest_rows(blk, spot, which):
        return rest_out.at[rows_at((blk * n_sp + spot) * shard + which * fourth, fourth)]

    def rest_copy(sems, blk, spot, which, slot, target):
        at = rest_rows(blk, spot, which)
        index = (slot * 2 + blk) * n_sp + spot
        return remote_copy(at, at, sems[0].at[index], sems[1].at[index], target)

    def rest_core(blk, spot, slot):
        which = core * 2 + (pair if slot == 0 else 1 - pair)
        return rest_copy((lcs, lcr), blk, spot, which, slot, core_id)

    def rest_pair(blk, spot):
        return rest_copy((lys, lyr), blk, spot, quarter, 0, pair_id)

    def rest_blk(spot):
        at = rest_rows(spot_b, spot, quarter)
        return remote_copy(at, at, lxs.at[spot], lxr.at[spot], blk_id)

    def rest_arrived(spot):
        rest_blk(spot).start()
        rest_pair(spot_b, spot).start()
        rest_core(spot_b, spot, 0).start()

    rest_step, rest_sent = line_gather(
        lambda part: rest_ref.at[rows_at(quarter * fourth, fourth)],
        lambda block, part: rest_rows(spot_b, block, quarter),
        1,
        ls,
        lr,
        rest_arrived,
    )
    rest_own = remote_copy(
        rest_ref.at[rows_at(quarter * fourth, fourth)],
        rest_rows(spot_b, spot_s, quarter),
        lxs.at[spot_s],
        lxr.at[spot_s],
        blk_id,
    )
    rest_keep = pltpu.make_async_copy(
        rest_ref, rest_out.at[rows_at((spot_b * n_sp + spot_s) * shard, shard)], out.at[9]
    )

    def at_distance(k, call):
        if k == 0:
            call(spot_s)
        else:
            for way in range(2):

                @pl.when(gets(way, k - 1))
                def _():
                    call(spot_s - k if way == 0 else spot_s + k)

    def rest_from_blk(k):
        def one(spot):
            rest_blk(spot).wait_recv()
            rest_pair(1 - spot_b, spot).start()
            rest_core(1 - spot_b, spot, 0).start()

        at_distance(k, one)

    def rest_from_pair(k):
        def one(spot):
            if k > 0:
                rest_pair(spot_b, spot).wait_recv()
                rest_core(spot_b, spot, 1).start()
            rest_pair(1 - spot_b, spot).wait_recv()
            rest_core(1 - spot_b, spot, 1).start()

        at_distance(k, one)

    def rest_last(k):
        def one(spot):
            for slot in range(2):
                if k > 0:
                    rest_core(spot_b, spot, slot).wait_recv()
                rest_core(1 - spot_b, spot, slot).wait_recv()

        at_distance(k, one)

    def rest_done(k):
        def one(spot):
            rest_blk(spot).wait_send()
            for slot in range(2):
                if k > 0:
                    rest_core(spot_b, spot, slot).wait_send()
                rest_core(1 - spot_b, spot, slot).wait_send()
            if k > 0:
                rest_pair(spot_b, spot).wait_send()
            rest_pair(1 - spot_b, spot).wait_send()

        at_distance(k, one)

    hidden = in_ref.shape[0]
    hidden_half = hidden // 2
    hidden_at = rows_at(core * hidden_half, hidden_half)

    def hidden_blk(which):
        src = in_ref if which == 0 else out_ref
        dst = in_out if which == 0 else out_out
        return remote_copy(
            src.at[hidden_at], dst.at[hidden_at], fs.at[which], fr.at[which], blk_id
        )

    def hidden_core(which):
        at = (in_out if which == 0 else out_out).at[hidden_at]
        return remote_copy(at, at, fs.at[2 + which], fr.at[2 + which], core_id)

    text_rows = text_ref.shape[0]

    def text_at(blk, spot):
        return text_out.at[rows_at((blk * n_sp + spot) * text_rows, text_rows)]

    def text_blk(spot, own):
        at = text_at(spot_b, spot)
        src = text_ref if own else at
        return remote_copy(src, at, exs.at[spot], exr.at[spot], blk_id)

    text_step, text_sent = line_gather(
        lambda part: text_ref,
        lambda block, part: text_at(spot_b, block),
        1,
        es,
        er,
        lambda spot: text_blk(spot, False).start(),
    )
    text_keep = pltpu.make_async_copy(text_ref, text_at(spot_b, spot_s), out.at[10])
    cot_step, cot_sent = line_gather(
        lambda part: cot_ref,
        lambda block, part: cot_out.at[rows_at(block * rows, rows)],
        1,
        os,
        osr,
    )
    cot_keep = pltpu.make_async_copy(
        cot_ref, cot_out.at[rows_at(spot_s * rows, rows)], out.at[11]
    )

    token_step(0)
    hidden_blk(0).start()
    for copy in (rest_keep, text_keep, cot_keep):
        copy.start()
    rest_own.start()
    text_blk(spot_s, True).start()
    for copy in small_away:
        copy.wait_recv()
    keep[4].wait()
    small_pass = []
    for spot in range(n_sp):
        at = sall_ref.at[spot_b * n_sp + spot]
        copy = remote_copy(at, at, ps.at[spot], pr.at[spot], blk_id)
        copy.start()
        small_pass.append(copy)
    for j in range(3):
        keep[j].wait()
    blk_away = []
    core_away = []

    def pass_core(blk, spot, which):
        at = w_ref.at[w_rows(blk, spot, core)]
        copy = remote_copy(at, at, cs.at[which], cr.at[which], core_id)
        copy.start()
        core_away.append(copy)

    def pass_blk(step):
        at = w_ref.at[w_rows(spot_b, lax.rem(spot_s + n_sp - step, n_sp), core)]
        copy = remote_copy(at, at, xs.at[step], xr.at[step], blk_id)
        copy.start()
        blk_away.append(copy)

    pass_blk(0)
    for k in range(n_sp - 1):
        for j in range(3):
            w_away[3 * k + j].wait_recv()
        pass_blk(k + 1)
        pass_core(spot_b, lax.rem(spot_s + n_sp - k - 1, n_sp), k)

    for copy in small_pass:
        copy.wait_recv()
    lanes = wide // (2 * n_sp)
    at_row = lax.broadcasted_iota(jnp.int32, (2 * SMALL_LANES, 2 * lanes), 0)
    at_col = lax.broadcasted_iota(jnp.int32, (2 * SMALL_LANES, 2 * lanes), 1)
    place = jnp.where(at_row < SMALL_LANES, at_row, at_row - SMALL_LANES)
    goal = jnp.where(at_row < SMALL_LANES, place, place + lanes)
    chosen = jnp.logical_and(place < lanes, goal == at_col).astype(F32).astype(BF)
    for two in range(n_sp):
        both = jnp.concatenate(
            [sall_ref[2 * two, 16:, :], sall_ref[2 * two + 1, 16:, :]], axis=1
        )
        par_ref[:, 2 * lanes * two : 2 * lanes * (two + 1)] = mm(both, chosen)

    token_step(1)
    for step in range(n_sp):
        blk_away[step].wait_recv()
        pass_core(1 - spot_b, lax.rem(spot_s + n_sp - step, n_sp), n_sp - 1 + step)
    for copy in core_away:
        copy.wait_recv()
    w_keep = pltpu.make_async_copy(w_ref, w_out_ref, lo.at[5])
    w_keep.start()
    keep[3].wait()

    shift = time_ref[0:1, :] + par_ref[0:1, :]
    scale = 1.0 + (time_ref[1:2, :] + par_ref[1:2, :])
    own = lanes_at(spot_s * cols, cols)

    def project(block):
        at = rows_at(block * rows, rows)
        values = xall_ref[at, :].astype(F32)
        centre = values - jnp.mean(values, axis=-1, keepdims=True)
        spread = jnp.mean(centre * centre, axis=-1, keepdims=True)
        h1_ref[at, :] = (centre * lax.rsqrt(spread + EPS) * scale + shift).astype(BF)
        for j in range(3):
            lin = mm(h1_ref[at, :], w_ref[:, j * cols : (j + 1) * cols])
            lin = lin + par_ref[11 + j : 12 + j, own]
            if j < 2:
                lin_ref[j, at, :] = lin
                sums = exact_sums(lin * lin)
                sums_ref[spot_s, j : j + 1, lanes_at(block * rows, rows)] = sums[0:1]
            else:
                kv_ref[1, at, :] = lin.astype(BF)
        value_copy(block).start()
        angle = exact_first(
            sall_ref[spot_b * n_sp + block, 0:16, :].astype(F32), table_ref[...]
        )
        trig_ref[0, at, :] = jnp.cos(angle)
        trig_ref[1, at, :] = jnp.sin(angle)

    def kv_copy(which, block):
        return remote_copy(
            kv_ref.at[which, rows_at(block * rows, rows)],
            kv_ref.at[which, rows_at(total_rows + block * rows, rows)],
            vs.at[which * n_sp + block],
            vr.at[which * n_sp + block],
            blk_id,
        )

    def value_copy(block):
        return kv_copy(1, block)

    def arrived(k):
        first = (spot_s >= k).astype(jnp.int32)
        last = (spot_s + k < n_sp).astype(jnp.int32)

        def one(i, carry):
            ahead = jnp.logical_and(first == 1, i == 0)
            project(jnp.where(ahead, spot_s - k, spot_s + k))
            return carry

        lax.fori_loop(0, first + last, one, 0)

    project(spot_s)
    arrived(1)
    for k in range(2, n_sp):
        token_step(k)
        arrived(k)
    rest_step(0)

    sums_away = []
    for k in range(n_sp - 1):
        copy = remote_copy(
            sums_ref.at[spot_s], sums_ref.at[spot_s], qs.at[k], qr.at[k], line[k]
        )
        copy.start()
        sums_away.append(copy)
    for copy in sums_away:
        copy.wait_recv()
    squares = sums_ref[0]
    for k in range(1, n_sp):
        squares = squares + sums_ref[k]
    rho_rows = lax.rsqrt(squares / wide + EPS)
    sums_ref[n_sp] = rho_rows

    def turn_block(which, block):
        at = rows_at(block * rows, rows)
        rho = exact_first(sums_ref[n_sp, :, lanes_at(block * rows, rows)], row_pick(which))
        rho_ref[which, at, :] = rho
        cosine = trig_ref[0, at, :]
        sine = trig_ref[1, at, :]
        for h in range(heads_here):
            gain = par_ref[6 + which : 7 + which, lanes_at(spot_s * cols + h * HD, HD)]
            value = lin_ref[which, at, h * HD : (h + 1) * HD] * rho * gain
            value = turned(value, cosine, sine).astype(BF)
            if which == 0:
                q_ref[at, h * HD : (h + 1) * HD] = value
            else:
                kv_ref[0, at, h * HD : (h + 1) * HD] = value

    def turn_key(block, carry):
        turn_block(1, block)
        kv_copy(0, block).start()
        return carry

    def turn_query(block, carry):
        turn_block(0, block)
        return carry

    lax.fori_loop(0, n_sp, turn_key, 0)
    lax.fori_loop(0, n_sp, turn_query, 0)
    rest_from_blk(0)
    text_step(0)
    hidden_blk(0).wait_recv()
    hidden_core(0).start()
    saves = [
        pltpu.make_async_copy(h1_ref, h1_out, out.at[0]),
        pltpu.make_async_copy(lin_ref, lin_out, out.at[1]),
        pltpu.make_async_copy(rho_ref, rho_out, out.at[2]),
        pltpu.make_async_copy(trig_ref, trig_out, out.at[3]),
        pltpu.make_async_copy(q_ref, q_out, out.at[4]),
    ]
    for copy in saves:
        copy.start()
    score_scale = HD ** (-0.5)

    def attend(block, h, part):
        at = rows_at(block * rows, rows)
        head = pl.ds(h * HD, HD)
        keys = pl.ds(part * total_rows, total_rows)
        scores = mm_t(q_ref[at, head], kv_ref[0, keys, head]) * score_scale
        top = jnp.max(scores, -1, keepdims=True)
        if part == 1:
            before = stat_ref[0, h, at, 0:1]
            top = jnp.maximum(top, before)
        raised = jnp.exp(scores - top)
        total = jnp.sum(raised, -1, keepdims=True)
        result = mm(raised.astype(BF), kv_ref[1, keys, head])
        if part == 0:
            stat_ref[0, h, at, :] = jnp.broadcast_to(top, (rows, 128))
            stat_ref[1, h, at, :] = jnp.broadcast_to(total, (rows, 128))
            acc_ref[h, at, :] = result
        else:
            fade = jnp.exp(before - top)
            total = total + fade * stat_ref[1, h, at, 0:1]
            result = result + fade * acc_ref[h, at, :]
            att_ref[at, head] = (result / total).astype(BF)
            stat_ref[0, h, at, :] = jnp.broadcast_to(top + jnp.log(total), (rows, 128))

    def first_pass(block, carry):
        for h in range(heads_here):
            attend(block, h, 0)
        return carry

    lax.fori_loop(0, n_sp, first_pass, 0)
    rest_step(1)

    def key_wait(block, carry):
        kv_copy(0, block).wait_recv()
        kv_copy(1, block).wait_recv()
        return carry

    lax.fori_loop(0, n_sp, key_wait, 0)
    kv_save = pltpu.make_async_copy(kv_ref, kv_out, out.at[5])
    kv_save.start()
    hidden_blk(1).start()

    def att_copy(step):
        block = lax.rem(spot_s + step, n_sp)
        return remote_copy(
            att_ref.at[rows_at(block * rows, rows)],
            tok_out.at[:, lanes_at(spot_s * cols, cols)],
            ts.at[step - 1],
            tr.at[step - 1],
            {"sp": block},
        )

    for step in list(range(1, n_sp)) + [0]:
        block = lax.rem(spot_s + step, n_sp)

        def one_head(block=block):
            for h in range(heads_here):
                attend(block, h, 1)

        one_head()
        if step > 0:
            att_copy(step).start()
        if step == 1:
            rest_step(2)
            text_step(1)
        if step == 2:
            rest_from_blk(1)
            rest_from_pair(0)
    own_att = pltpu.make_async_copy(
        att_ref.at[rows_at(spot_s * rows, rows)],
        tok_out.at[:, lanes_at(spot_s * cols, cols)],
        out.at[6],
    )
    own_att.start()
    saves.append(own_att)
    last = [
        pltpu.make_async_copy(stat_ref.at[0], lse_out, out.at[7]),
        pltpu.make_async_copy(att_ref, att_out, out.at[8]),
    ]
    for copy in last:
        copy.start()
    rest_step(3)
    cot_step(0)
    text_step(2)
    rest_from_pair(1)
    rest_from_blk(2)
    text_step(3)
    rest_from_blk(3)
    cot_step(1)
    rest_from_pair(2)
    cot_step(2)
    hidden_blk(1).wait_recv()
    hidden_core(1).start()
    rest_from_pair(3)
    cot_step(3)
    for k in range(n_sp):
        rest_last(k)
        at_distance(k, lambda spot: text_blk(spot, False).wait_recv())
    for which in range(2):
        hidden_core(which).wait_recv()
    for step in range(1, n_sp):
        att_copy(step).wait_recv()
    for copy in (rest_keep, text_keep, cot_keep):
        copy.wait()
    for k in range(n_sp):
        rest_done(k)
        at_distance(k, lambda spot: text_blk(spot, False).wait_send())
    for which in range(2):
        hidden_blk(which).wait_send()
        hidden_core(which).wait_send()
    rest_sent()
    text_sent()
    cot_sent()
    token_sent()
    for copy in saves + last + [kv_save, w_keep]:
        copy.wait()
    for copy in small_away + w_away + blk_away + core_away + small_pass + sums_away:
        copy.wait_send()

    def kv_sent(block, carry):
        kv_copy(0, block).wait_send()
        kv_copy(1, block).wait_send()
        return carry

    lax.fori_loop(0, n_sp, kv_sent, 0)
    for step in range(1, n_sp):
        att_copy(step).wait_send()


def front(x_own, small_own, qkv, rest, shard_in, shard_out, text, cot, time_rows):
    n_sp = lax.axis_size("sp")
    groups = 2 * n_sp
    rows, width = x_own.shape
    total = n_sp * rows
    cols = qkv.shape[1] // 3 // n_sp
    heads_here = cols // HD
    table = np.zeros((16, HD), np.float32)
    pairs = rope_tables(HD)
    table[:3, : HD // 2] = pairs
    table[:3, HD // 2 :] = pairs
    any_place = pl.BlockSpec(memory_space=pl.ANY)
    in_vmem = pl.BlockSpec(memory_space=pltpu.VMEM)
    dma = pltpu.SemaphoreType.DMA
    line = n_sp - 1
    counts = [6, 4 * line, 4 * line, line, line, 3 * line, 3 * line, n_sp, n_sp]
    counts += [2 * n_sp - 1, 2 * n_sp - 1, n_sp, n_sp, 2 * n_sp, 2 * n_sp, line, line]
    counts += [line, line, 12]
    counts += [2 * line, 2 * line, n_sp, n_sp, groups, groups, 2 * groups, 2 * groups, 4, 4]
    counts += [2 * line, 2 * line, n_sp, n_sp, 2 * line, 2 * line]
    shape = jax.ShapeDtypeStruct
    outs = (
        shape((PARAM_ROWS, width), F32),
        shape((total, width), BF),
        shape((width, 3 * cols), BF),
        shape((2, total, cols), F32),
        shape((2, total, HD), F32),
        shape((2, total, HD), F32),
        shape((total, cols), BF),
        shape((2, 2 * total, cols), BF),
        shape((heads_here, total, HD), F32),
        shape((total, cols), BF),
        shape((rows, width), BF),
        shape((groups * rest.shape[0], rest.shape[1]), BF),
        shape(shard_in.shape, BF),
        shape(shard_out.shape, BF),
        shape((groups * text.shape[0], width), BF),
        shape((total, width), BF),
    )
    vmem = pltpu.VMEM
    return pl.pallas_call(
        functools.partial(front_kernel, n_sp),
        out_shape=outs,
        in_specs=[any_place] * 8 + [in_vmem] * 2,
        out_specs=(in_vmem,) + (any_place,) * (len(outs) - 1),
        scratch_shapes=[
            vmem((total, width), BF),
            vmem((groups, SMALL_ROWS, SMALL_LANES), BF),
            vmem((width, 3 * cols), BF),
            vmem((2, total, cols), F32),
            vmem((n_sp + 1, 8, total), F32),
            vmem((2, total, HD), F32),
            vmem((2, total, HD), F32),
            vmem((total, cols), BF),
            vmem((2, 2 * total, cols), BF),
            vmem((heads_here, total, HD), F32),
            vmem((2, heads_here, total, HD), F32),
            vmem((total, cols), BF),
            vmem((total, width), BF),
        ]
        + [dma((count,)) for count in counts],
        compiler_params=pltpu.CompilerParams(
            collective_id=1, has_side_effects=True, vmem_limit_bytes=56 * 2**20
        ),
    )(x_own, small_own, qkv, rest, shard_in, shard_out, text, cot, time_rows, jnp.asarray(table))


def dot(a, b):
    return jnp.dot(a, b, preferred_element_type=F32)


def dot_t(a, b):
    return jnp.einsum("te,de->td", a, b, preferred_element_type=F32)


def dot_g(a, b):
    return jnp.einsum("td,te->de", a, b, preferred_element_type=F32)


def after(value, *others):
    return lax.optimization_barrier((value, others))[0]


def from_back(value, step):
    size = lax.axis_size("sp")
    return lax.ppermute(value, "sp", [(i, (i + step) % size) for i in range(size)])


def to_back(value, step):
    size = lax.axis_size("sp")
    return lax.ppermute(value, "sp", [(i, (i - step) % size) for i in range(size)])


def swap_blk(value):
    return lax.ppermute(value, "blk", [(0, 1), (1, 0)])


def swap_dp(value, bit):
    size = lax.axis_size("dp")
    return lax.ppermute(value, "dp", [(i, i ^ bit) for i in range(size)])


def gather_sp(value):
    size = lax.axis_size("sp")
    return [value] + [from_back(value, step) for step in range(1, size)]


def total_sp(own, parts):
    total = own
    for step in range(1, len(parts)):
        total = total + to_back(parts[step].astype(BF), step).astype(F32)
    return total


def in_order_back(blocks, place, axis):
    size = len(blocks)
    back = blocks[::-1]
    whole = jnp.concatenate(back + back[:-1], axis)
    width = blocks[0].shape[axis]
    return lax.dynamic_slice_in_dim(whole, (size - 1 - place) * width, size * width, axis)


def in_order_ahead(blocks, place, axis):
    size = len(blocks)
    whole = jnp.concatenate(blocks + blocks[:-1], axis)
    width = blocks[0].shape[axis]
    return lax.dynamic_slice_in_dim(whole, ((size - place) % size) * width, size * width, axis)


def pair_order(own, other, place, axis):
    return jnp.where(
        place == 0, jnp.concatenate([own, other], axis), jnp.concatenate([other, own], axis)
    )


def part_of(value, index, count, axis):
    width = value.shape[axis] // count
    return lax.dynamic_slice_in_dim(value, index * width, width, axis)


def sum_sp_rows(sums):
    size = lax.axis_size("sp")
    total = sums
    for step in range(1, size):
        total = total + from_back(sums, step)
    return total


def local(
    clip_tokens,
    text_tokens,
    text_lengths,
    positions,
    time_embed,
    modulation,
    gains,
    biases,
    self_qkv,
    self_out,
    cross_qkv,
    cross_out,
    ffn_in,
    ffn_out,
    ffn_bias,
    cotangent,
):
    n_sp = lax.axis_size("sp")
    n_dp = lax.axis_size("dp")
    spot_dp = lax.axis_index("dp")
    spot_b = lax.axis_index("blk")
    spot_s = lax.axis_index("sp")
    core = spot_dp % 2
    pair = (spot_dp // 2) % 2
    x_own = clip_tokens[0]
    tok_rows, width = x_own.shape
    heads_here = H // n_sp
    cols_here = heads_here * HD
    shard_rows = self_qkv.shape[0]
    scale = HD ** (-0.5)

    small_rows = jnp.concatenate([modulation, gains, biases], 0)
    lanes_here = small_rows.shape[1]
    small_own = jnp.concatenate(
        [
            jnp.pad(
                positions[0].astype(BF), ((0, 13), (0, SMALL_LANES - positions.shape[2]))
            ),
            jnp.pad(
                small_rows, ((0, PARAM_ROWS - 21), (0, SMALL_LANES - lanes_here))
            ),
        ],
        0,
    )
    (
        params,
        h1_all,
        qkv_mine,
        lin_parts,
        rho,
        trig,
        q_flat,
        kv_flat,
        lse_wide,
        att_all,
        att_tok,
        rest_all,
        in_other,
        out_other,
        text_every,
        cot_every,
    ) = front(
        x_own,
        small_own,
        self_qkv,
        jnp.concatenate([self_out, cross_out, cross_qkv], 1),
        ffn_in,
        ffn_out,
        text_tokens[0],
        cotangent[0],
        time_embed[0],
    )
    out_self = rest_all[:, :width]
    out_cross = rest_all[:, width : 2 * width]
    qkv_cross = rest_all[:, 2 * width :]
    in_all = jnp.concatenate([ffn_in, in_other], 0)
    out_all = jnp.concatenate([ffn_out, out_other], 0)
    cot_blocks = [part_of(cot_every, (spot_s - step) % n_sp, n_sp, 0) for step in range(n_sp)]
    mods = time_embed[0] + params[:6]
    gain_all = params[6:11]
    bias_all = params[11:21]
    ff_here = ffn_in.shape[0]
    bias_own = ffn_bias.astype(F32)
    bias_ff = jnp.concatenate([bias_own, swap_blk(ffn_bias).astype(F32)])
    half_rows = shard_rows // 2

    def own_cols(row):
        return part_of(row, spot_s, n_sp, row.ndim - 1)

    gain_cols = own_cols(gain_all)
    q_lin = lin_parts[0]
    k_lin = lin_parts[1]
    rows_all = q_lin.shape[0]
    rho = rho[:, :, :1]
    cosine = trig[0]
    sine_part = trig[1]

    def heads(value):
        return value.reshape(-1, heads_here, HD)

    q_own = heads(q_flat)
    k_every = heads(kv_flat[0])
    v_every = heads(kv_flat[1])

    block_count = 2
    block_rows = rows_all // block_count
    lse_parts = [
        lse_wide[:, block * block_rows : (block + 1) * block_rows, 0]
        for block in range(block_count)
    ]

    tokens = x_own.astype(F32)
    a_lin = dot(att_tok, out_self) + bias_all[3]
    x_one = tokens + mods[2] * a_lin
    normed_three = layer_norm(x_one)
    cross_in = (normed_three * gain_all[2] + bias_all[8]).astype(BF)
    qc_lin = dot(cross_in, qkv_cross[:, :width]) + bias_all[4]
    q_cross = rms_norm(qc_lin, gain_all[3]).astype(BF).reshape(tok_rows, H, HD)
    kv_lin = dot(text_every, qkv_cross[:, width:]) + jnp.concatenate([bias_all[5], bias_all[6]])
    k_cross = rms_norm(kv_lin[:, :width], gain_all[4]).astype(BF).reshape(-1, H, HD)
    v_cross = kv_lin[:, width:].astype(BF).reshape(-1, H, HD)
    text_rows = text_tokens.shape[1]
    valid = jnp.arange(text_every.shape[0], dtype=jnp.int32) < text_lengths[0]
    scores_c = (
        jnp.einsum("rhe,khe->hrk", q_cross, k_cross, preferred_element_type=F32) * scale
    )
    probs_c = softmax_rows(jnp.where(valid[None, None, :], scores_c, NEG))
    probs_cb = probs_c.astype(BF)
    crossed = (
        jnp.einsum("hrk,khe->rhe", probs_cb, v_cross, preferred_element_type=F32)
        .reshape(tok_rows, width)
        .astype(BF)
    )
    c_lin = dot(crossed, out_cross) + bias_all[7]
    x_two = x_one + c_lin
    normed_two = layer_norm(x_two)
    ffn_rows = (normed_two * (1.0 + mods[4]) + mods[3]).astype(BF)

    h2_blocks = gather_sp(ffn_rows)
    z_parts = []
    dh2_parts = []
    g_blocks = []
    du_blocks = []
    dz_blocks = []
    for step in range(n_sp):
        u_lin = dot_t(h2_blocks[step], in_all) + bias_ff
        g_act, gelu_back = jax.vjp(gelu_tanh, u_lin)
        g_low = g_act.astype(BF)
        d_z = (cot_blocks[step].astype(F32) * mods[5]).astype(BF)
        d_g = dot_t(d_z, out_all)
        d_u = gelu_back(d_g)[0].astype(BF)
        dh2_parts.append(dot(d_u, in_all))
        z_parts.append(dot(g_low, out_all))
        g_blocks.append(g_low)
        du_blocks.append(d_u)
        dz_blocks.append(d_z)
    d_rows = total_sp(dh2_parts[0], dh2_parts)
    z_line = jnp.zeros((n_sp, tok_rows, width), BF)
    for step in range(n_sp):
        z_line = lax.dynamic_update_index_in_dim(
            z_line, z_parts[step].astype(BF), (spot_s - step) % n_sp, 0
        )
    z_lin = (
        lax.psum_scatter(z_line, "sp", scatter_dimension=0, tiled=False).astype(F32) + bias_all[9]
    )
    grad_y = cotangent[0].astype(F32)
    result = x_two + mods[5] * z_lin
    block_out = result.astype(BF)[None]
    d_gate2 = jnp.sum(grad_y * z_lin, 0)
    du_all = jnp.concatenate(du_blocks, 0)
    g_all = jnp.concatenate(g_blocks, 0)
    h2_all = jnp.concatenate(h2_blocks, 0)
    dz_all = jnp.concatenate(dz_blocks, 0)
    g_hidden_in = dot_g(du_all, h2_all).astype(BF)
    g_hidden_out = dot_g(g_all, dz_all).astype(BF)
    du_sums = col_sum(du_all)

    def round_add(own, got):
        return own.astype(F32) + got.astype(F32)

    def core_half(grad, which):
        return part_of(grad[:ff_here], which, 2, 0), part_of(grad[ff_here:], which, 2, 0)

    keep_in = core_half(g_hidden_in, core)
    keep_out = core_half(g_hidden_out, core)
    away_in = core_half(g_hidden_in, 1 - core)
    away_out = core_half(g_hidden_out, 1 - core)
    ff_core = swap_dp(jnp.stack([away_in[0], away_out[0], away_in[1], away_out[1]]), 1)
    ff_sum = round_add(
        jnp.stack([keep_in[0], keep_out[0], keep_in[1], keep_out[1]]), ff_core
    )
    ff_part = ff_sum[:2] + swap_blk(ff_sum[2:].astype(BF)).astype(F32)
    bit = 2
    while bit < n_dp:
        low = ff_part.astype(BF)
        ff_part = round_add(low, swap_dp(low, bit))
        bit *= 2
    ff_low = ff_part.astype(BF)
    ff_final = pair_order(ff_low, swap_dp(ff_low, 1), core, 1).astype(F32)

    d_shift2 = jnp.sum(d_rows, 0)
    d_scale2 = jnp.sum(d_rows * normed_two, 0)
    d_x_two = grad_y + layer_back(x_two, d_rows * (1.0 + mods[4]))

    def scatter_weight(rows, grads):
        def half(which):
            return dot_g(rows, part_of(grads, which, 2, 1))

        got = swap_dp(half(1 - core).astype(BF), 1)
        total = half(core) + got.astype(F32)
        away = part_of(total, 1 - pair, 2, 1).astype(BF)
        total = part_of(total, pair, 2, 1) + swap_dp(away, 2).astype(F32)
        return lax.psum_scatter(
            total.astype(BF), ("blk", "sp"), scatter_dimension=0, tiled=True
        ).astype(F32)

    def spread_weight(total):
        bit = 4
        while bit < n_dp:
            low = total.astype(BF)
            total = round_add(low, swap_dp(low, bit))
            bit *= 2
        low = total.astype(BF)
        low = pair_order(low, swap_dp(low, 2), pair, 1)
        return pair_order(low, swap_dp(low, 1), core, 1).astype(F32)

    d_c = d_x_two.astype(BF)
    g_out_cross = scatter_weight(crossed, d_c)
    d_oc = dot_t(d_c, out_cross).astype(BF).reshape(tok_rows, H, HD)
    d_vc = jnp.einsum("hrk,rhe->khe", probs_cb, d_oc, preferred_element_type=F32)
    d_pc = jnp.einsum("rhe,khe->hrk", d_oc, v_cross, preferred_element_type=F32)
    d_sc = (probs_c * (d_pc - jnp.sum(probs_c * d_pc, -1, keepdims=True))).astype(BF)
    d_qc = jnp.einsum("hrk,khe->rhe", d_sc, k_cross, preferred_element_type=F32) * scale
    d_kc = jnp.einsum("hrk,rhe->khe", d_sc, q_cross, preferred_element_type=F32) * scale
    d_qc_lin, d_gain3 = jax.vjp(rms_norm, qc_lin, gain_all[3])[1](d_qc.reshape(tok_rows, width))
    d_qc_low = d_qc_lin.astype(BF)
    d_cross_in = dot_t(d_qc_low, qkv_cross[:, :width])
    d_gain2 = jnp.sum(d_cross_in * normed_three, 0)
    d_bias8 = jnp.sum(d_cross_in, 0)
    d_x_one = d_x_two + layer_back(x_one, d_cross_in * gain_all[2])
    d_a = (d_x_one * mods[2]).astype(BF)
    d_gate1 = jnp.sum(d_x_one * a_lin, 0)
    d_att = dot_t(d_a, out_self).astype(BF)

    d_o_line = lax.all_to_all(
        d_att.reshape(tok_rows, n_sp, cols_here).transpose(1, 0, 2),
        "sp",
        split_axis=0,
        concat_axis=0,
        tiled=True,
    )
    d_o = heads(d_o_line.reshape(rows_all, cols_here))

    text_all = d_kc.shape[0]
    d_kc_lin, d_gain4 = jax.vjp(rms_norm, kv_lin[:, :width], gain_all[4])[1](
        d_kc.reshape(text_all, width)
    )
    d_kv_lin = jnp.concatenate(
        [d_kc_lin.astype(BF), d_vc.reshape(text_all, width).astype(BF)], -1
    )
    text_part = dot_t(d_kv_lin, qkv_cross[:, width:])
    grad_text = lax.psum_scatter(
        text_part.astype(BF), ("blk", "sp"), scatter_dimension=0, tiled=True
    ).astype(F32)
    g_q_cross = scatter_weight(cross_in, d_qc_low)
    g_kv_cross = scatter_weight(text_every, d_kv_lin)
    g_out_self = scatter_weight(att_tok, d_a)

    acc_k = jnp.zeros(k_every.shape, F32)
    acc_v = jnp.zeros(k_every.shape, F32)
    dq_parts = []
    for block in range(block_count):
        q_block = q_own[block * block_rows : (block + 1) * block_rows]
        do_block = d_o[block * block_rows : (block + 1) * block_rows]
        scores = (
            jnp.einsum("rhe,khe->hrk", q_block, k_every, preferred_element_type=F32) * scale
        )
        probs = jnp.exp(scores - lse_parts[block][..., None])
        acc_v = acc_v + jnp.einsum(
            "hrk,rhe->khe", probs.astype(BF), do_block, preferred_element_type=F32
        )
        d_p = jnp.einsum("rhe,khe->hrk", do_block, v_every, preferred_element_type=F32)
        d_s = (probs * (d_p - jnp.sum(probs * d_p, -1, keepdims=True))).astype(BF)
        dq_parts.append(
            jnp.einsum("hrk,khe->rhe", d_s, k_every, preferred_element_type=F32) * scale
        )
        acc_k = (
            acc_k
            + jnp.einsum("hrk,rhe->khe", d_s, q_block, preferred_element_type=F32) * scale
        )
    kv_away = jnp.stack([acc_k[rows_all:].astype(BF), acc_v[rows_all:].astype(BF)])
    kv_got = swap_blk(kv_away.reshape(2, rows_all, cols_here)).astype(F32)
    d_k = acc_k[:rows_all].reshape(rows_all, cols_here) + kv_got[0]
    d_v = acc_v[:rows_all].reshape(rows_all, cols_here) + kv_got[1]
    d_q = jnp.concatenate(dq_parts, 0)

    def unturn(grad):
        return rotate(heads(grad), cosine, -sine_part).reshape(rows_all, cols_here)

    e_q = unturn(d_q)
    e_k = unturn(d_k)
    vge_q = q_lin * gain_cols[0] * e_q
    vge_k = k_lin * gain_cols[1] * e_k
    means = jnp.stack([jnp.sum(vge_q, -1), jnp.sum(vge_k, -1)])
    means = sum_sp_rows(means) / width
    cubes = (rho * rho * rho) * means[..., None]
    d_q_lin = rho[0] * gain_cols[0] * e_q - q_lin * cubes[0]
    d_k_lin = rho[1] * gain_cols[1] * e_k - k_lin * cubes[1]
    d_gain0 = jnp.sum(e_q * q_lin * rho[0], 0)
    d_gain1 = jnp.sum(e_k * k_lin * rho[1], 0)
    d_proj = jnp.concatenate([d_q_lin.astype(BF), d_k_lin.astype(BF), d_v.astype(BF)], -1)
    dh1_part = dot_t(d_proj, qkv_mine)
    dh1_steps = [part_of(dh1_part, (spot_s - step) % n_sp, n_sp, 0) for step in range(n_sp)]
    d_shift = total_sp(dh1_steps[0], dh1_steps)
    normed_one = layer_norm(tokens)
    grad_tokens = d_x_one + layer_back(tokens, d_shift * (1.0 + mods[1]))
    d_shift1 = jnp.sum(d_shift, 0)
    d_scale1 = jnp.sum(d_shift * normed_one, 0)

    g_qkv = dot_g(h1_all, d_proj).astype(BF).reshape(2 * n_sp, 2, half_rows, 3 * cols_here)
    qkv_core = swap_dp(jnp.take(g_qkv, 1 - core, axis=1), 1)
    qkv_sum = round_add(jnp.take(g_qkv, core, axis=1), qkv_core)
    qkv_sum = part_of(qkv_sum, spot_b, 2, 0) + swap_blk(
        part_of(qkv_sum, 1 - spot_b, 2, 0).astype(BF)
    ).astype(F32)
    qkv_line = lax.all_to_all(
        qkv_sum.astype(BF), "sp", split_axis=0, concat_axis=0, tiled=True
    )
    bit = 2
    while bit < n_dp:
        qkv_line = round_add(qkv_line, swap_dp(qkv_line, bit)).astype(BF)
        bit *= 2
    qkv_rows = pair_order(qkv_line, swap_dp(qkv_line, 1), core, 1)
    part_sqkv = (
        qkv_rows.reshape(n_sp, shard_rows, 3, cols_here)
        .transpose(1, 2, 0, 3)
        .reshape(shard_rows, 3 * width)
        .astype(F32)
    )

    def wide(row):
        return lax.dynamic_update_slice_in_dim(
            jnp.zeros((width,), F32), row, spot_s * cols_here, 0
        )

    proj_sums = col_sum(d_proj)
    kv_sums = col_sum(d_kv_lin)
    ff_total = ff_here * 2 * n_sp
    ff_row = jnp.zeros((-(-ff_total // width) * width,), F32)
    own_at = (spot_b * n_sp + spot_s) * ff_here
    far_at = ((1 - spot_b) * n_sp + spot_s) * ff_here
    ff_row = lax.dynamic_update_slice_in_dim(ff_row, du_sums[:ff_here], own_at, 0)
    ff_row = lax.dynamic_update_slice_in_dim(ff_row, du_sums[ff_here:], far_at, 0)
    small = jnp.concatenate(
        [
            jnp.stack(
                [
                    d_shift1,
                    d_scale1,
                    d_gate1,
                    d_shift2,
                    d_scale2,
                    d_gate2,
                    wide(d_gain0),
                    wide(d_gain1),
                    d_gain2,
                    d_gain3,
                    d_gain4,
                    wide(proj_sums[:cols_here]),
                    wide(proj_sums[cols_here : 2 * cols_here]),
                    wide(proj_sums[2 * cols_here :]),
                    col_sum(d_a),
                    col_sum(d_qc_low),
                    kv_sums[:width],
                    kv_sums[width:],
                    col_sum(d_c),
                    d_bias8,
                    col_sum(dz_blocks[0]),
                ]
            ),
            ff_row.reshape(-1, width),
        ],
        0,
    )
    bit = 1
    while bit < n_dp:
        small = small + swap_dp(small, bit)
        bit *= 2
    small = small + swap_blk(small)
    bit = 1
    while bit < n_sp:
        small = small + lax.ppermute(small, "sp", [(i, i ^ bit) for i in range(n_sp)])
        bit *= 2
    spot = spot_b * n_sp + spot_s
    small_own = lax.dynamic_slice_in_dim(small[:21], spot * lanes_here, lanes_here, 1)
    part_bias = lax.dynamic_slice_in_dim(small[21:].reshape(-1), own_at, ff_here, 0)
    return (
        block_out,
        grad_tokens[None],
        grad_text[None],
        small_own[:6],
        small_own[6:11],
        small_own[11:21],
        part_sqkv,
        spread_weight(g_out_self),
        jnp.concatenate([spread_weight(g_q_cross), spread_weight(g_kv_cross)], 1),
        spread_weight(g_out_cross),
        ff_final[0],
        ff_final[1],
        part_bias,
    )


def solution(mesh):
    return jax.shard_map(
        local,
        mesh=mesh,
        in_specs=(
            P("dp", ("blk", "sp"), None),
            P("dp", ("blk", "sp"), None),
            P("dp"),
            P("dp", None, ("blk", "sp")),
            P("dp", None, None),
            P(None, ("blk", "sp")),
            P(None, ("blk", "sp")),
            P(None, ("blk", "sp")),
            P(("blk", "sp"), None),
            P(("blk", "sp"), None),
            P(("blk", "sp"), None),
            P(("blk", "sp"), None),
            P(("blk", "sp"), None),
            P(("blk", "sp"), None),
            P(("blk", "sp")),
            P("dp", ("blk", "sp"), None),
        ),
        out_specs=(
            P("dp", ("blk", "sp"), None),
            P("dp", ("blk", "sp"), None),
            P("dp", ("blk", "sp"), None),
            P(None, ("blk", "sp")),
            P(None, ("blk", "sp")),
            P(None, ("blk", "sp")),
            P(("blk", "sp"), None),
            P(("blk", "sp"), None),
            P(("blk", "sp"), None),
            P(("blk", "sp"), None),
            P(("blk", "sp"), None),
            P(("blk", "sp"), None),
            P(("blk", "sp")),
        ),
        check_vma=False,
    )
```

time: 2660 us -> 1170 us (0.44)
  waiting for transfers between devices: 1930 us -> 240 us
  Pallas kernels: 0 us -> 278 us
  blocking collectives: 177 us -> 0 us
  other arithmetic: 99 us -> 146 us
    reduce_scatter x7 -> x6, waiting for transfers between devices: 659 us -> 39.3 us  [the longest x1 29.8 us: local(): lax.psum_scatter(z_line, 'sp', scatter_dimension=0, tiled=False).astype(F32)]
    all_gather x10 -> x0, waiting for transfers between devices: 609 us -> none  [the longest x2 152 us: spread_rows(): return lax.all_gather(rows, ('blk', 'sp'), axis=0, tiled=True)]
    unnamed x28 -> x6, waiting for transfers between devices: 320 us -> 0.1 us
    pallas_call x0 -> x1, Pallas kernels: none -> 278 us  [front(): pl.pallas_call(functools.partial(front_kernel, n_sp), out_shape=outs, in_...]
    psum x1 -> x0, waiting for transfers between devices: 208 us -> none  [clip_total(): lax.psum(as_sent(parts), 'dp')]
    ppermute x0 -> x43, waiting for transfers between devices: none -> 201 us  [the longest x24 75.1 us: swap_dp(): return lax.ppermute(value, 'dp', [(i, i ^ bit) for i in range(size)])]
    all_to_all x7 -> x2, waiting for transfers between devices: 130 us -> 0.01 us  [the longest x1 0.01 us: local(): lax.all_to_all(d_att.reshape(tok_rows, n_sp, cols_here).transpose(1, 0, 2...]
    all_gather x3 -> x0, blocking collectives: 73.6 us -> none  [the longest x1 24.6 us: local(): lax.all_gather(gains, ('blk', 'sp'), axis=1, tiled=True)]
  transfers between devices with their start and end apart: 30 -> 51, of which waited for: 26 -> 16; matrix products, arithmetic and copies ran while one was open for 14% -> 40% of each run, Pallas kernels for 0% -> 0%
where the time goes in v1:
time: 1170 us; the launch traced here: 1150 us
  Pallas kernels  278 us (24%)
  matrix products  245 us (21%)
  waiting for transfers between devices  240 us (21%)
  local copies, waits for them, and re-layouts  167 us (14%)
  other arithmetic  146 us (12%)
  starting transfers between devices  58 us (5%)
  between operations  17.2 us (1%)
    pallas_call x1, Pallas kernels, front(): pl.pallas_call(functools.partial(front_kernel, n_sp), out_shape=outs, in_...  278 us
    ppermute x24, waiting for transfers between devices, swap_dp(): return lax.ppermute(value, 'dp', [(i, i ^ bit) for i in range(size)])  75.1 us
    dot_general x13, matrix products, dot_t(): return jnp.einsum('te,de->td', a, b, preferred_element_type=F32)  68 us
    ppermute x6, waiting for transfers between devices, to_back(): lax.ppermute(value, 'sp', [(i, (i - step) % size) for i in range(size)])  63 us
    dot_general x12, matrix products, dot(): return jnp.dot(a, b, preferred_element_type=F32)  50.5 us
    unnamed x397, local copies, waits for them, and re-layouts  49.1 us
    dot_general x11, matrix products, dot_g(): return jnp.einsum('td,te->de', a, b, preferred_element_type=F32)  48.5 us
    ppermute x5, waiting for transfers between devices, swap_blk(): return lax.ppermute(value, 'blk', [(0, 1), (1, 0)])  39.9 us
  transfers between devices with their start and end apart: 51, of which 16 were waited for; matrix products, arithmetic and copies ran while one was open for 40% of the time, Pallas kernels for 0%

profile of v1, /device:TPU:27, one launch (start us, length us, event | category | flops | bytes accessed | tf_op | source)
XLA Modules:
  0.0 1152.7 jit_solution(15259922851147124414)
XLA Ops:
  14.2 278.4 %shard_map.264 = (f32[32,1536]{1,0:T(8,128)}, bf16[1024,1536]{1,0:T(8,128)(2,1)}, bf16[1536,1152]{1,0:T(8,128)(2,1)}, f32[2,1024,384]{2,1,0:T(8,128)}, f32[2,102...) custom-call(bf16[256,1536]{1,0:T(8,128)(2,1)} %bitcast.295, ...), custom_call_target="tpu_custom_call" | custom-call | tf_op jit(solution)/shard_map/pallas_call | solution.py:792
  295.4 8.1 fusion.17
  367.8 7.8 fusion.239
  389.9 7.3 fusion.243
  421.2 8.4 fusion.99
  458.2 9.5 convolution_convert_fusion
  495.2 9.3 convolution_convert_fusion.1
  517.5 11.0 collective-permute-done.4
  534.9 29.8 %reduce-scatter.7.cloned.1.call-done = bf16[1,256,1536]{2,1,0:T(8,128)(2,1)} async-done(((bf16[4,256,1536]{2,1,0:T(8,128)(2,1)}), bf16[1,256,1536]{2,1,0:T(8,128)(2,1)}) %reduce-scatter.7.cloned.1.call-update) | async-done | bytes 786448 | tf_op jit(solution)/shard_map/reduce_scatter | solution.py:1064
  648.1 7.1 collective-permute-done.36
  670.5 8.5 fusion.58
  695.9 9.0 fusion.9
  704.9 11.0 multiply_reduce_fusion
  717.6 11.1 multiply_convert_fusion
  779.6 35.5 %collective-permute-done.7 = bf16[2,1024,384]{2,1,0:T(8,128)(2,1)} collective-permute-done((bf16[2,1024,384]{2,1,0:T(8,128)(2,1)}, bf16[2,1024,384]{2,1,0:T(8,128)(2,1)}, u32[]{:S(2)}, u32[]{:S(2)}) %collective-permute-start.7) | collective-permute-done | bytes 1572896 | tf_op jit(solution)/shard_map/ppermute | solution.py:846
  875.1 6.9 fusion.7
  898.5 18.3 %collective-permute-done.13 = bf16[256,1536]{1,0:T(8,128)(2,1)S(1)} collective-permute-done((bf16[256,1536]{1,0:T(8,128)(2,1)}, bf16[256,1536]{1,0:T(8,128)(2,1)S(1)}, u32[]{:S(2)}, u32[]{:S(2)}) %collective-permute-start.13) | collective-permute-done | bytes 786464 | tf_op jit(solution)/shard_map/ppermute | solution.py:842
  916.8 33.7 %collective-permute-done.12 = bf16[256,1536]{1,0:T(8,128)(2,1)S(1)} collective-permute-done((bf16[256,1536]{1,0:T(8,128)(2,1)}, bf16[256,1536]{1,0:T(8,128)(2,1)S(1)}, u32[]{:S(2)}, u32[]{:S(2)}) %collective-permute-start.12) | collective-permute-done | bytes 786464 | tf_op jit(solution)/shard_map/ppermute | solution.py:842
  961.1 57.0 %collective-permute-done.32 = bf16[1536,768]{1,0:T(8,128)(2,1)} collective-permute-done((bf16[1536,768]{1,0:T(8,128)(2,1)}, bf16[1536,768]{1,0:T(8,128)(2,1)}, u32[]{:S(2)}, u32[]{:S(2)}) %collective-permute-start.32) | collective-permute-done | bytes 2359328 | tf_op jit(solution)/shard_map/ppermute | solution.py:851
  1059.6 11.0 collective-permute-done.17
  1074.0 11.5 collective-permute-done.18
  1107.9 9.5 reduce-scatter.15.cloned.1.call-done
  1118.5 10.3 fusion.8
  1130.9 11.5 slice_bitcast_fusion
  (743 shorter events, 514.1 us)
Async XLA Ops:
  7.2 557.5 %reduce-scatter.7.cloned.1.call-start = ((), (), s32[]{:S(2)}) async-start(), calls=%async_computation.8 | async-start | bytes 3932160 | tf_op jit(solution)/shard_map/reduce_scatter | solution.py:1064
  347.4 86.9 %collective-permute-start.3 = (bf16[256,1536]{1,0:T(8,128)(2,1)}, bf16[256,1536]{1,0:T(8,128)(2,1)}, u32[]{:S(2)}, u32[]{:S(2)}) collective-permute-start(bf16[256,1536]{1,0:T(8,128)(2,1)} %add_convert_fusion.7), channel_id=1, source_target_pairs={{0,3},{1,0},{2,1},{3,2},{4,7},{5,4},{6,5},{7,6},{8,11},{9,8},{10,9... | collective-permute-start | bytes 2359304 | tf_op jit(solution)/shard_map/ppermute | solution.py:837
  347.4 95.1 %collective-permute-start.2 = (bf16[256,1536]{1,0:T(8,128)(2,1)}, bf16[256,1536]{1,0:T(8,128)(2,1)}, u32[]{:S(2)}, u32[]{:S(2)}) collective-permute-start(bf16[256,1536]{1,0:T(8,128)(2,1)} %add_convert_fusion.7), channel_id=1, source_target_pairs={{0,2},{1,3},{2,0},{3,1},{4,6},{5,7},{6,4},{7,5},{8,10},{9,11},{10,... | collective-permute-start | bytes 2359304 | tf_op jit(solution)/shard_map/ppermute | solution.py:837
  349.6 102.7 %collective-permute-start.1 = (bf16[256,1536]{1,0:T(8,128)(2,1)}, bf16[256,1536]{1,0:T(8,128)(2,1)}, u32[]{:S(2)}, u32[]{:S(2)}) collective-permute-start(bf16[256,1536]{1,0:T(8,128)(2,1)} %add_convert_fusion.7), channel_id=1, source_target_pairs={{0,1},{1,2},{2,3},{3,0},{4,5},{5,6},{6,7},{7,4},{8,9},{9,10},{10,1... | collective-permute-start | bytes 2359304 | tf_op jit(solution)/shard_map/ppermute | solution.py:837
  350.9 69.5 %collective-permute-start = (bf16[1120]{0:T(1024)(128)(2,1)}, bf16[1120]{0:T(1024)(128)(2,1)}, u32[]{:S(2)}, u32[]{:S(2)}) collective-permute-start(bf16[1120]{0:T(1024)(128)(2,1)} %param.33), channel_id=1, source_target_pairs={{0,4},{4,0},{1,5},{5,1},{2,6},{6,2},{3,7},{7,3},{8,12},{12,8},{9,1... | collective-permute-start | bytes 6728 | tf_op jit(solution)/shard_map/ppermute | solution.py:846
  442.2 75.4 %collective-permute-start.6 = (bf16[256,1536]{1,0:T(8,128)(2,1)}, bf16[256,1536]{1,0:T(8,128)(2,1)}, u32[]{:S(2)}, u32[]{:S(2)}) collective-permute-start(bf16[256,1536]{1,0:T(8,128)(2,1)} %convolution_convert_fusion.7), channel_id=1, source_target_pairs={{0,1},{1,2},{2,3},{3,0},{4,5},{5,6},{6,7},{7,4},{8,9},{9,10},{10,1... | collective-permute-start | bytes 2359304 | tf_op jit(solution)/shard_map/ppermute | solution.py:842
  450.9 66.6 %collective-permute-start.5 = (bf16[256,1536]{1,0:T(8,128)(2,1)}, bf16[256,1536]{1,0:T(8,128)(2,1)}, u32[]{:S(2)}, u32[]{:S(2)}) collective-permute-start(bf16[256,1536]{1,0:T(8,128)(2,1)} %convolution_convert_fusion.8), channel_id=1, source_target_pairs={{0,2},{1,3},{2,0},{3,1},{4,6},{5,7},{6,4},{7,5},{8,10},{9,11},{10,... | collective-permute-start | bytes 2359304 | tf_op jit(solution)/shard_map/ppermute | solution.py:842
  514.6 164.5 %collective-permute-start.39 = (bf16[4,560,1536]{2,1,0:T(8,128)(2,1)}, bf16[4,560,1536]{2,1,0:T(8,128)(2,1)}, u32[]{:S(2)}, u32[]{:S(2)}) collective-permute-start(bf16[4,560,1536]{2,1,0:T(8,128)(2,1)} %pad_maximum_fusion), channel_id=1, source_target_pairs={{0,8},{8,0},{16,24},{24,16},{1,9},{9,1},{17,25},{25,17},{2,10},{10... | collective-permute-start | bytes 20643848 | tf_op jit(solution)/shard_map/ppermute | solution.py:851
  648.1 422.7 %reduce-scatter.17.cloned.1.call-start = ((), (), s32[]{:S(2)}) async-start(), calls=%async_computation.13 | async-start | bytes 1327104 | tf_op jit(solution)/shard_map/reduce_scatter | solution.py:1113
  658.5 413.7 %reduce-scatter.9.cloned.1.call-start = ((), (), s32[]{:S(2)}) async-start(), calls=%async_computation.9 | async-start | bytes 1769472 | tf_op jit(solution)/shard_map/reduce_scatter | solution.py:1162
  661.9 106.7 %collective-permute-start.27 = (bf16[1536,768]{1,0:T(8,128)(2,1)}, bf16[1536,768]{1,0:T(8,128)(2,1)}, u32[]{:S(2)}, u32[]{:S(2)}) collective-permute-start(bf16[1536,768]{1,0:T(8,128)(2,1)} %convolution_convert_fusion.5), channel_id=1, source_target_pairs={{0,8},{8,0},{16,24},{24,16},{1,9},{9,1},{17,25},{25,17},{2,10},{10... | collective-permute-start | bytes 7077896 | tf_op jit(solution)/shard_map/ppermute | solution.py:851
  665.1 108.7 %collective-permute-start.23 = (bf16[1536,768]{1,0:T(8,128)(2,1)}, bf16[1536,768]{1,0:T(8,128)(2,1)}, u32[]{:S(2)}, u32[]{:S(2)}) collective-permute-start(bf16[1536,768]{1,0:T(8,128)(2,1)} %convolution_convert_fusion.6), channel_id=1, source_target_pairs={{0,8},{8,0},{16,24},{24,16},{1,9},{9,1},{17,25},{25,17},{2,10},{10... | collective-permute-start | bytes 7077896 | tf_op jit(solution)/shard_map/ppermute | solution.py:851
  670.0 211.9 %collective-permute-start.31 = (bf16[1536,1536]{1,0:T(8,128)(2,1)}, bf16[1536,1536]{1,0:T(8,128)(2,1)}, u32[]{:S(2)}, u32[]{:S(2)}) collective-permute-start(bf16[1536,1536]{1,0:T(8,128)(2,1)} %convolution_convert_fusion.3), channel_id=1, source_target_pairs={{0,8},{8,0},{16,24},{24,16},{1,9},{9,1},{17,25},{25,17},{2,10},{10... | collective-permute-start | bytes 14155784 | tf_op jit(solution)/shard_map/ppermute | solution.py:851
  679.1 406.5 %reduce-scatter.13.cloned.1.call-start = ((), (), s32[]{:S(2)}) async-start(), calls=%async_computation.11 | async-start | bytes 1327104 | tf_op jit(solution)/shard_map/reduce_scatter | solution.py:1113
  692.2 179.5 %collective-permute-start.40 = (bf16[2,560,1536]{2,1,0:T(8,128)(2,1)}, bf16[2,560,1536]{2,1,0:T(8,128)(2,1)}, u32[]{:S(2)}, u32[]{:S(2)}) collective-permute-start(bf16[2,560,1536]{2,1,0:T(8,128)(2,1)} %slice.489), channel_id=1, source_target_pairs={{0,4},{4,0},{1,5},{5,1},{2,6},{6,2},{3,7},{7,3},{8,12},{12,8},{9,1... | collective-permute-start | bytes 10321928 | tf_op jit(solution)/shard_map/ppermute | solution.py:846
  755.2 60.0 %collective-permute-start.7 = (bf16[2,1024,384]{2,1,0:T(8,128)(2,1)}, bf16[2,1024,384]{2,1,0:T(8,128)(2,1)}, u32[]{:S(2)}, u32[]{:S(2)}) collective-permute-start(bf16[2,1024,384]{2,1,0:T(8,128)(2,1)} %pad_maximum_fusion.7), channel_id=1, source_target_pairs={{0,4},{4,0},{1,5},{5,1},{2,6},{6,2},{3,7},{7,3},{8,12},{12,8},{9,1... | collective-permute-start | bytes 4718600 | tf_op jit(solution)/shard_map/ppermute | solution.py:846
  857.5 96.9 %collective-permute-start.19 = (bf16[8,96,1152]{2,1,0:T(8,128)(2,1)}, bf16[8,96,1152]{2,1,0:T(8,128)(2,1)}, u32[]{:S(2)}, u32[]{:S(2)}) collective-permute-start(bf16[8,96,1152]{2,1,0:T(8,128)(2,1)} %fusion.121), channel_id=1, source_target_pairs={{0,8},{8,0},{16,24},{24,16},{1,9},{9,1},{17,25},{25,17},{2,10},{10... | collective-permute-start | bytes 5308424 | tf_op jit(solution)/shard_map/ppermute | solution.py:851
  871.7 217.8 %reduce-scatter.11.cloned.1.call-start = ((), (), s32[]{:S(2)}) async-start(), calls=%async_computation.10 | async-start | bytes 1327104 | tf_op jit(solution)/shard_map/reduce_scatter | solution.py:1113
  881.9 68.6 %collective-permute-start.12 = (bf16[256,1536]{1,0:T(8,128)(2,1)}, bf16[256,1536]{1,0:T(8,128)(2,1)S(1)}, u32[]{:S(2)}, u32[]{:S(2)}) collective-permute-start(bf16[256,1536]{1,0:T(8,128)(2,1)} %get-tuple-element.124), channel_id=1, source_target_pairs={{0,2},{1,3},{2,0},{3,1},{4,6},{5,7},{6,4},{7,5},{8,10},{9,11},{10,... | collective-permute-start | bytes 2359304 | tf_op jit(solution)/shard_map/ppermute | solution.py:842
  894.3 135.4 %collective-permute-start.41 = (bf16[2,560,1536]{2,1,0:T(8,128)(2,1)}, bf16[2,560,1536]{2,1,0:T(8,128)(2,1)}, u32[]{:S(2)}, u32[]{:S(2)}) collective-permute-start(bf16[2,560,1536]{2,1,0:T(8,128)(2,1)} %fusion.7), channel_id=1, source_target_pairs={{0,16},{8,24},{16,0},{24,8},{1,17},{9,25},{17,1},{25,9},{2,18},{10... | collective-permute-start | bytes 10321928 | tf_op jit(solution)/shard_map/ppermute | solution.py:851
  895.8 122.3 %collective-permute-start.32 = (bf16[1536,768]{1,0:T(8,128)(2,1)}, bf16[1536,768]{1,0:T(8,128)(2,1)}, u32[]{:S(2)}, u32[]{:S(2)}) collective-permute-start(bf16[1536,768]{1,0:T(8,128)(2,1)} %dynamic-slice_convert_fusion), channel_id=1, source_target_pairs={{0,16},{8,24},{16,0},{24,8},{1,17},{9,25},{17,1},{25,9},{2,18},{10... | collective-permute-start | bytes 7077896 | tf_op jit(solution)/shard_map/ppermute | solution.py:851
  898.4 218.9 %reduce-scatter.15.cloned.1.call-start = ((), (), s32[]{:S(2)}) async-start(), calls=%async_computation.12 | async-start | bytes 2654208 | tf_op jit(solution)/shard_map/reduce_scatter | solution.py:1113
  959.2 62.9 %collective-permute-start.20 = (bf16[4,96,1152]{2,1,0:T(8,128)(2,1)S(1)}, bf16[4,96,1152]{2,1,0:T(8,128)(2,1)}, u32[]{:S(2)}, u32[]{:S(2)}) collective-permute-start(bf16[4,96,1152]{2,1,0:T(8,128)(2,1)S(1)} %dynamic-slice_convert_fusion.4), channel_id=1, source_target_pairs={{0,4},{4,0},{1,5},{5,1},{2,6},{6,2},{3,7},{7,3},{8,12},{12,8},{9,1... | collective-permute-start | bytes 2654216 | tf_op jit(solution)/shard_map/ppermute | solution.py:846
  1035.6 82.9 %collective-permute-start.42 = (bf16[2,560,1536]{2,1,0:T(8,128)(2,1)}, bf16[2,560,1536]{2,1,0:T(8,128)(2,1)}, u32[]{:S(2)}, u32[]{:S(2)}) collective-permute-start(bf16[2,560,1536]{2,1,0:T(8,128)(2,1)} %add_convert_fusion), channel_id=1, source_target_pairs={{0,8},{8,0},{16,24},{24,16},{1,9},{9,1},{17,25},{25,17},{2,10},{10... | collective-permute-start | bytes 10321928 | tf_op jit(solution)/shard_map/ppermute | solution.py:851
  (225 other events, 2496.0 us)
Sparse Core Ops, SparseCore 0:
  479.9 84.6 reduce-scatter.6
  658.6 63.4 reduce-scatter.16
  725.5 69.0 reduce-scatter.8
  871.8 95.9 reduce-scatter.12
  972.0 63.1 reduce-scatter.10
  1039.5 77.7 reduce-scatter.14

commit v2 on v1

--- a/solution.py
+++ b/solution.py
@@ -1,4 +1,5 @@
 import functools
+import types
 
 import jax
 import jax.numpy as jnp
@@ -12,21 +13,9 @@
 HD = 128
 
 
+DP, BLK, SP = "dp", "blk", "sp"
 EPS = 1e-06
 NEG = -1e30
-
-
-def layer_norm(values):
-    centre = values - jnp.mean(values, axis=-1, keepdims=True)
-    return centre * lax.rsqrt(jnp.mean(centre * centre, axis=-1, keepdims=True) + EPS)
-
-
-def rms_norm(values, gain_row):
-    return values * lax.rsqrt(jnp.mean(values * values, axis=-1, keepdims=True) + EPS) * gain_row
-
-
-def layer_back(values, grad_out):
-    return jax.vjp(layer_norm, values)[1](grad_out)[0]
 
 
 def rope_tables(head_dim):
@@ -42,26 +31,6 @@
         else:
             tables[2, column] = 10000.0 ** (-(column - first_count - side_count) / side_count)
     return tables
-
-
-def rotate(values, cosine, sine_part):
-    half_dim = values.shape[-1] // 2
-    turned = jnp.concatenate([-values[..., half_dim:], values[..., :half_dim]], -1)
-    return values * cosine[:, None, :] + turned * sine_part[:, None, :]
-
-
-def softmax_rows(scores):
-    top_score = jnp.max(scores, -1, keepdims=True)
-    raised = jnp.exp(scores - top_score)
-    return raised / jnp.sum(raised, -1, keepdims=True)
-
-
-def col_sum(values):
-    return jnp.sum(values.astype(jnp.float32), 0)
-
-
-def gelu_tanh(inner):
-    return jax.nn.gelu(inner, approximate=True)
 
 
 BF = jnp.bfloat16
@@ -191,15 +160,15 @@
 ):
     lo, zs, zr, ss, sr, ws, wr, xs, xr, cs, cr, ps, pr, vs, vr, qs, qr, ts, tr, out = sems[:20]
     (ls, lr, lxs, lxr, lys, lyr, lcs, lcr, fs, fr, es, er, exs, exr, os, osr) = sems[20:]
-    spot_d = lax.axis_index("dp")
-    spot_b = lax.axis_index("blk")
-    spot_s = lax.axis_index("sp")
+    spot_d = lax.axis_index(DP)
+    spot_b = lax.axis_index(BLK)
+    spot_s = lax.axis_index(SP)
     core = lax.rem(spot_d, 2)
     pair = lax.rem(spot_d // 2, 2)
-    core_id = {"dp": spot_d + 1 - 2 * core}
-    pair_id = {"dp": spot_d + 2 - 4 * pair}
-    blk_id = {"blk": 1 - spot_b}
-    line = [{"sp": lax.rem(spot_s + step, n_sp)} for step in range(1, n_sp)]
+    core_id = {DP: spot_d + 1 - 2 * core}
+    pair_id = {DP: spot_d + 2 - 4 * pair}
+    blk_id = {BLK: 1 - spot_b}
+    line = [{SP: lax.rem(spot_s + step, n_sp)} for step in range(1, n_sp)]
     rows = x_ref.shape[0]
     shard = qkv_ref.shape[0]
     half = shard // 2
@@ -259,7 +228,7 @@
             block = spot_s - k if way == 0 else spot_s + k
             at = place(block, part)
             src = first(part) if k == 0 else at
-            target = {"sp": spot_s + 1 if way == 0 else spot_s - 1}
+            target = {SP: spot_s + 1 if way == 0 else spot_s - 1}
             index = (way * (n_sp - 1) + k) * pieces + part
             return remote_copy(src, at, send.at[index], recv.at[index], target)
 
@@ -403,18 +372,52 @@
 
     hidden = in_ref.shape[0]
     hidden_half = hidden // 2
-    hidden_at = rows_at(core * hidden_half, hidden_half)
-
-    def hidden_blk(which):
+
+    def hidden_place(which, half):
+        goal = in_out if which == 0 else out_out
+        return goal.at[pl.ds(half * hidden_half, hidden_half)]
+
+    def hidden_each(call):
+        for which in range(2):
+            for half in range(2):
+
+                @pl.when(jnp.logical_and(core == half, pair == which))
+                def _():
+                    call(which, half)
+
+    def hidden_blk(which, half):
         src = in_ref if which == 0 else out_ref
-        dst = in_out if which == 0 else out_out
         return remote_copy(
-            src.at[hidden_at], dst.at[hidden_at], fs.at[which], fr.at[which], blk_id
-        )
-
-    def hidden_core(which):
-        at = (in_out if which == 0 else out_out).at[hidden_at]
-        return remote_copy(at, at, fs.at[2 + which], fr.at[2 + which], core_id)
+            src.at[pl.ds(half * hidden_half, hidden_half)],
+            hidden_place(which, half),
+            fs.at[0],
+            fr.at[0],
+            blk_id,
+        )
+
+    def hidden_pair(which, half):
+        at = hidden_place(which, half)
+        return remote_copy(at, at, fs.at[1], fr.at[1], pair_id)
+
+    def hidden_core(slot, which, half):
+        at = hidden_place(which, half)
+        return remote_copy(at, at, fs.at[2 + slot], fr.at[2 + slot], core_id)
+
+    def hidden_next(which, half):
+        hidden_blk(which, half).wait_recv()
+        hidden_pair(which, half).start()
+        hidden_core(0, which, half).start()
+
+    def hidden_last(which, half):
+        hidden_pair(which, half).wait_recv()
+        hidden_core(1, 1 - which, half).start()
+
+    def hidden_end(which, half):
+        for slot in range(2):
+            hidden_core(slot, which, half).wait_recv()
+            hidden_core(slot, which, half).wait_send()
+        hidden_pair(which, half).wait_send()
+        hidden_blk(which, half).wait_send()
 
     text_rows = text_ref.shape[0]
 
@@ -447,11 +450,10 @@
     )
 
     token_step(0)
-    hidden_blk(0).start()
+    rest_own.start()
+    rest_step(0)
     for copy in (rest_keep, text_keep, cot_keep):
         copy.start()
-    rest_own.start()
-    text_blk(spot_s, True).start()
     for copy in small_away:
         copy.wait_recv()
     keep[4].wait()
@@ -508,6 +510,8 @@
     w_keep = pltpu.make_async_copy(w_ref, w_out_ref, lo.at[5])
     w_keep.start()
     keep[3].wait()
+    hidden_each(lambda which, half: hidden_blk(which, half).start())
+    rest_from_blk(0)
 
     shift = time_ref[0:1, :] + par_ref[0:1, :]
     scale = 1.0 + (time_ref[1:2, :] + par_ref[1:2, :])
@@ -559,11 +563,14 @@
         lax.fori_loop(0, first + last, one, 0)
 
     project(spot_s)
+    rest_step(1)
     arrived(1)
-    for k in range(2, n_sp):
-        token_step(k)
-        arrived(k)
-    rest_step(0)
+    token_step(2)
+    rest_from_blk(1)
+    arrived(2)
+    rest_step(2)
+    token_step(3)
+    arrived(3)
 
     sums_away = []
     for k in range(n_sp - 1):
@@ -606,10 +613,12 @@
 
     lax.fori_loop(0, n_sp, turn_key, 0)
     lax.fori_loop(0, n_sp, turn_query, 0)
-    rest_from_blk(0)
+    text_blk(spot_s, True).start()
     text_step(0)
-    hidden_blk(0).wait_recv()
-    hidden_core(0).start()
+    rest_from_pair(0)
+    rest_step(3)
+    rest_from_blk(2)
+    cot_step(0)
     saves = [
         pltpu.make_async_copy(h1_ref, h1_out, out.at[0]),
         pltpu.make_async_copy(lin_ref, lin_out, out.at[1]),
@@ -650,7 +659,7 @@
         return carry
 
     lax.fori_loop(0, n_sp, first_pass, 0)
-    rest_step(1)
+    hidden_each(hidden_next)
 
     def key_wait(block, carry):
         kv_copy(0, block).wait_recv()
@@ -660,7 +669,8 @@
     lax.fori_loop(0, n_sp, key_wait, 0)
     kv_save = pltpu.make_async_copy(kv_ref, kv_out, out.at[5])
     kv_save.start()
-    hidden_blk(1).start()
+    rest_from_blk(3)
+    rest_from_pair(1)
 
     def att_copy(step):
         block = lax.rem(spot_s + step, n_sp)
@@ -669,7 +679,7 @@
             tok_out.at[:, lanes_at(spot_s * cols, cols)],
             ts.at[step - 1],
             tr.at[step - 1],
-            {"sp": block},
+            {SP: block},
         )
 
     for step in list(range(1, n_sp)) + [0]:
@@ -683,11 +693,10 @@
         if step > 0:
             att_copy(step).start()
         if step == 1:
-            rest_step(2)
             text_step(1)
+            cot_step(1)
         if step == 2:
-            rest_from_blk(1)
-            rest_from_pair(0)
+            rest_from_pair(2)
     own_att = pltpu.make_async_copy(
         att_ref.at[rows_at(spot_s * rows, rows)],
         tok_out.at[:, lanes_at(spot_s * cols, cols)],
@@ -701,25 +710,15 @@
     ]
     for copy in last:
         copy.start()
-    rest_step(3)
-    cot_step(0)
     text_step(2)
-    rest_from_pair(1)
-    rest_from_blk(2)
+    cot_step(2)
+    hidden_each(hidden_last)
     text_step(3)
-    rest_from_blk(3)
-    cot_step(1)
-    rest_from_pair(2)
-    cot_step(2)
-    hidden_blk(1).wait_recv()
-    hidden_core(1).start()
     rest_from_pair(3)
     cot_step(3)
     for k in range(n_sp):
         rest_last(k)
         at_distance(k, lambda spot: text_blk(spot, False).wait_recv())
-    for which in range(2):
-        hidden_core(which).wait_recv()
     for step in range(1, n_sp):
         att_copy(step).wait_recv()
     for copy in (rest_keep, text_keep, cot_keep):
@@ -727,9 +726,7 @@
     for k in range(n_sp):
         rest_done(k)
         at_distance(k, lambda spot: text_blk(spot, False).wait_send())
-    for which in range(2):
-        hidden_blk(which).wait_send()
-        hidden_core(which).wait_send()
+    hidden_each(hidden_end)
     rest_sent()
     text_sent()
     cot_sent()
@@ -750,7 +747,7 @@
 
 
 def front(x_own, small_own, qkv, rest, shard_in, shard_out, text, cot, time_rows):
-    n_sp = lax.axis_size("sp")
+    n_sp = lax.axis_size(SP)
     groups = 2 * n_sp
     rows, width = x_own.shape
     total = n_sp * rows
@@ -816,85 +813,1254 @@
     )(x_own, small_own, qkv, rest, shard_in, shard_out, text, cot, time_rows, jnp.asarray(table))
 
 
-def dot(a, b):
-    return jnp.dot(a, b, preferred_element_type=F32)
-
-
-def dot_t(a, b):
-    return jnp.einsum("te,de->td", a, b, preferred_element_type=F32)
-
-
-def dot_g(a, b):
-    return jnp.einsum("td,te->de", a, b, preferred_element_type=F32)
-
-
-def after(value, *others):
-    return lax.optimization_barrier((value, others))[0]
-
-
-def from_back(value, step):
-    size = lax.axis_size("sp")
-    return lax.ppermute(value, "sp", [(i, (i + step) % size) for i in range(size)])
-
-
-def to_back(value, step):
-    size = lax.axis_size("sp")
-    return lax.ppermute(value, "sp", [(i, (i - step) % size) for i in range(size)])
+def normal(values):
+    centre = values - jnp.mean(values, axis=-1, keepdims=True)
+    spread = lax.rsqrt(jnp.mean(centre * centre, axis=-1, keepdims=True) + EPS)
+    return centre * spread, spread
+
+
+def normal_back(normed, spread, grad):
+    lean = jnp.mean(grad, axis=-1, keepdims=True)
+    tilt = jnp.mean(grad * normed, axis=-1, keepdims=True)
+    return spread * (grad - lean - normed * tilt)
+
+
+def column_total(values):
+    return jnp.sum(values.astype(F32), 0, keepdims=True)
+
+
+def wide_dot(dst, left, right, call=mm, tile=512, add=None):
+    across = dst.shape[-1]
+    for start in range(0, across, tile):
+        at = pl.ds(start, min(tile, across - start))
+        value = call(left, right[:, at])
+        if add is not None:
+            value = value + add[:, at]
+        dst[:, at] = value.astype(dst.dtype)
+
+
+def wide_dot_t(dst, left, right, tile=512, add=None):
+    across = dst.shape[-1]
+    for start in range(0, across, tile):
+        at = pl.ds(start, min(tile, across - start))
+        value = mm_t(left, right[at, :])
+        if add is not None:
+            value = value + add[:, at]
+        dst[:, at] = value.astype(dst.dtype)
+
+
+def rest_loads(rest_ref, goals, sems, order):
+    width = goals[0].shape[1]
+    copies = {}
+    for slot in order:
+        copies[slot] = pltpu.make_async_copy(
+            rest_ref.at[:, pl.ds(slot * width, width)], goals[slot], sems.at[slot]
+        )
+        copies[slot].start()
+    return copies
+
+
+def own_kernel(
+    len_ref,
+    rest_ref,
+    x_ref,
+    att_ref,
+    text_ref,
+    time_ref,
+    par_ref,
+    a_out,
+    one_out,
+    cin_out,
+    ql_out,
+    kl_out,
+    q_out,
+    kv_out,
+    lse_out,
+    oc_out,
+    two_out,
+    h2_out,
+    w_o,
+    w_co,
+    w_cq,
+    w_ck,
+    w_cv,
+    sems,
+):
+    loads = rest_loads(rest_ref, (w_o, w_co, w_cq, w_ck, w_cv), sems, (0, 2, 3, 4, 1))
+    mods = time_ref[...] + par_ref[0:6, :]
+    width = x_ref.shape[1]
+    loads[0].wait()
+    wide_dot(a_out, att_ref[...], w_o, add=par_ref.at[14:15])
+    x_one = x_ref[...].astype(F32) + mods[2:3] * a_out[...]
+    one_out[...] = x_one
+    normed, _ = normal(x_one)
+    cin_out[...] = (normed * par_ref[8:9, :] + par_ref[19:20, :]).astype(BF)
+    loads[2].wait()
+    wide_dot(ql_out, cin_out[...], w_cq, add=par_ref.at[15:16])
+    value = ql_out[...]
+    rho = lax.rsqrt(jnp.mean(value * value, axis=-1, keepdims=True) + EPS)
+    q_out[...] = (value * rho * par_ref[9:10, :]).astype(BF)
+    loads[3].wait()
+    wide_dot(kl_out, text_ref[...], w_ck, add=par_ref.at[16:17])
+    value = kl_out[...]
+    rho = lax.rsqrt(jnp.mean(value * value, axis=-1, keepdims=True) + EPS)
+    kv_out[0] = (value * rho * par_ref[10:11, :]).astype(BF)
+    loads[4].wait()
+    wide_dot(kv_out.at[1], text_ref[...], w_cv, add=par_ref.at[17:18])
+    texts = text_ref.shape[0]
+    rows = x_ref.shape[0]
+    valid = lax.broadcasted_iota(jnp.int32, (rows, texts), 1) < len_ref[0]
+
+    def attend(h, carry):
+        head = lanes_at(h * HD, HD)
+        scores = mm_t(q_out[:, head], kv_out[0, :, head]) * (HD ** (-0.5))
+        scores = jnp.where(valid, scores, NEG)
+        top = jnp.max(scores, -1, keepdims=True)
+        raised = jnp.exp(scores - top)
+        total = jnp.sum(raised, -1, keepdims=True)
+        result = mm((raised / total).astype(BF), kv_out[1, :, head])
+        oc_out[:, head] = result.astype(BF)
+        lse_out[h] = jnp.broadcast_to(top + jnp.log(total), (rows, HD))
+        return carry
+
+    lax.fori_loop(0, width // HD, attend, 0)
+    loads[1].wait()
+    wide_dot(two_out, oc_out[...], w_co, add=par_ref.at[18:19])
+    x_two = one_out[...] + two_out[...]
+    two_out[...] = x_two
+    normed, _ = normal(x_two)
+    h2_out[...] = (normed * (1.0 + mods[4:5]) + mods[3:4]).astype(BF)
+
+
+def own_tokens(lengths, rest, x_own, att_tok, text, time_rows, params):
+    rows, width = x_own.shape
+    texts = text.shape[0]
+    shape = jax.ShapeDtypeStruct
+    in_vmem = pl.BlockSpec(memory_space=pltpu.VMEM)
+    weight = pltpu.VMEM((width, width), BF)
+    names = ("a", "one", "cin", "ql", "kl", "q", "kv", "lse", "oc", "two", "h2")
+    outs = (
+        shape((rows, width), F32),
+        shape((rows, width), F32),
+        shape((rows, width), BF),
+        shape((rows, width), F32),
+        shape((texts, width), F32),
+        shape((rows, width), BF),
+        shape((2, texts, width), BF),
+        shape((width // HD, rows, HD), F32),
+        shape((rows, width), BF),
+        shape((rows, width), F32),
+        shape((rows, width), BF),
+    )
+    results = pl.pallas_call(
+        own_kernel,
+        out_shape=outs,
+        in_specs=[
+            pl.BlockSpec(memory_space=pltpu.SMEM),
+            pl.BlockSpec(memory_space=pl.ANY),
+        ]
+        + [in_vmem] * 5,
+        out_specs=(in_vmem,) * len(outs),
+        scratch_shapes=[weight] * 5 + [pltpu.SemaphoreType.DMA((5,))],
+        compiler_params=pltpu.CompilerParams(vmem_limit_bytes=58 * 2**20),
+    )(lengths, rest, x_own, att_tok, text, time_rows, params)
+    return types.SimpleNamespace(**dict(zip(names, results)))
+
+
+def own_back_kernel(names, *refs):
+    ref = types.SimpleNamespace(**dict(zip(names, refs)))
+    sems, out_sem = ref.sems, ref.out_sem
+    w_a, w_b, w_c = (getattr(ref, name) for name in ("w_a", "w_b", "w_c"))
+    loads = rest_loads(ref.rest, (w_a, w_a, w_b, w_c, w_b), sems, (1, 2, 3))
+    par_ref, sums = ref.par, ref.sums
+    mods = ref.time[...] + par_ref[0:6, :]
+    rows, width = ref.x_two.shape
+    texts = ref.text_in.shape[0]
+    sums[...] = jnp.zeros(sums.shape, F32)
+    grad_y = ref.cot[...].astype(F32)
+    sums[20:21, :] = column_total((grad_y * mods[5:6]).astype(BF))
+    d_rows = ref.d_rows[...]
+    normed, spread = normal(ref.x_two[...])
+    sums[3:4, :] = column_total(d_rows)
+    sums[4:5, :] = column_total(d_rows * normed)
+    dx_ref = ref.dx
+    dx_ref[...] = grad_y + normal_back(normed, spread, d_rows * (1.0 + mods[4:5]))
+    low_ref = ref.low
+    low_ref[...] = dx_ref[...].astype(BF)
+    sums[18:19, :] = column_total(low_ref[...])
+
+    saves = []
+
+    def weight_grad(name, left, right):
+        stage = ref.stage
+        tile = 384
+        for k, start in enumerate(range(0, width, tile)):
+            slot = len(saves) % 2
+            if len(saves) >= 2:
+                saves[-2].wait()
+            stage[slot] = mm_first(left[:, start : start + tile], right[...]).astype(BF)
+            copy = pltpu.make_async_copy(
+                stage.at[slot], getattr(ref, name).at[pl.ds(start, tile)], out_sem.at[slot]
+            )
+            copy.start()
+            saves.append(copy)
+
+    weight_grad("co", ref.oc, low_ref)
+    loads[1].wait()
+    doc_ref = ref.doc
+    wide_dot_t(doc_ref, low_ref[...], w_a)
+    loads.update(rest_loads(ref.rest, (w_a,), sems, (0,)))
+    dq_ref, dkv_ref = ref.dq, ref.dkv
+    q_ref, kv_ref = ref.q, ref.kv
+    scale = HD ** (-0.5)
+    valid = lax.broadcasted_iota(jnp.int32, (rows, texts), 1) < ref.len[0]
+
+    def attend(h, carry):
+        head = lanes_at(h * HD, HD)
+        query, keys, grad = q_ref[:, head], kv_ref[0, :, head], doc_ref[:, head]
+        scores = mm_t(query, keys) * scale
+        scores = jnp.where(valid, scores, NEG)
+        probs = jnp.exp(scores - ref.lse[h, :, 0:1])
+        dkv_ref[1, :, head] = mm_first(probs.astype(BF), grad)
+        d_probs = mm_t(grad, kv_ref[1, :, head])
+        lean = jnp.sum(probs * d_probs, -1, keepdims=True)
+        d_scores = (probs * (d_probs - lean)).astype(BF)
+        dq_ref[:, head] = mm(d_scores, keys) * scale
+        dkv_ref[0, :, head] = mm_first(d_scores, query) * scale
+        return carry
+
+    lax.fori_loop(0, width // HD, attend, 0)
+
+    def rms_back(value, gain, grad):
+        rho = lax.rsqrt(jnp.mean(value * value, axis=-1, keepdims=True) + EPS)
+        lean = jnp.mean(value * gain * grad, axis=-1, keepdims=True)
+        return (
+            rho * gain * grad - value * (rho * rho * rho * lean),
+            jnp.sum(grad * value * rho, 0, keepdims=True),
+        )
+
+    back_q, gain_q = rms_back(ref.ql[...], par_ref[9:10, :], dq_ref[...])
+    low_ref[...] = back_q.astype(BF)
+    sums[9:10, :] = gain_q
+    sums[15:16, :] = column_total(low_ref[...])
+    loads[2].wait()
+    wide_dot_t(dq_ref, low_ref[...], w_b)
+    loads.update(rest_loads(ref.rest, (w_b,) * 5, sems, (4,)))
+    d_cin = dq_ref[...]
+    normed, spread = normal(ref.x_one[...])
+    sums[8:9, :] = column_total(d_cin * normed)
+    sums[19:20, :] = column_total(d_cin)
+    dx_ref[...] += normal_back(normed, spread, d_cin * par_ref[8:9, :])
+    weight_grad("cq", ref.cin, low_ref)
+    sums[2:3, :] = column_total(dx_ref[...] * ref.a[...])
+    low_ref[...] = (dx_ref[...] * mods[2:3]).astype(BF)
+    sums[14:15, :] = column_total(low_ref[...])
+    loads[0].wait()
+    wide_dot_t(ref.d_att, low_ref[...], w_a)
+    weight_grad("o", ref.att, low_ref)
+    back_k, gain_k = rms_back(ref.kl[...], par_ref[10:11, :], dkv_ref[0])
+    sums[10:11, :] = gain_k
+    klow_ref, vlow_ref = ref.klow, ref.vlow
+    klow_ref[...] = back_k.astype(BF)
+    vlow_ref[...] = dkv_ref[1].astype(BF)
+    sums[16:17, :] = column_total(klow_ref[...])
+    sums[17:18, :] = column_total(vlow_ref[...])
+    weight_grad("ck", ref.text_in, klow_ref)
+    weight_grad("cv", ref.text_in, vlow_ref)
+    loads[3].wait()
+    wide_dot_t(dkv_ref.at[0], klow_ref[...], w_c)
+    loads[4].wait()
+    wide_dot_t(ref.text_part, vlow_ref[...], w_b, add=dkv_ref.at[0])
+    for copy in saves[-2:]:
+        copy.wait()
+
+
+def own_back(**values):
+    arrays = types.SimpleNamespace(**values)
+    shape = jax.ShapeDtypeStruct
+    rows, width = arrays.x_two.shape
+    texts = arrays.text_in.shape[0]
+    in_any = ["rest"]
+    ins = ["x_two", "x_one", "d_rows", "cot", "time", "par", "a", "cin", "ql", "kl", "q", "kv"]
+    ins += ["lse", "oc", "att", "text_in"]
+    any_outs = {name: shape((width, width), BF) for name in ("o", "co", "cq", "ck", "cv")}
+    outs = dict(
+        d_att=shape((rows, width), BF),
+        dx=shape((rows, width), F32),
+        text_part=shape((texts, width), BF),
+        sums=shape((32, width), F32),
+    )
+    vmem = pltpu.VMEM
+    weight = vmem((width, width), BF)
+    scratch = {name: weight for name in ("w_a", "w_b", "w_c")}
+    scratch.update(
+        dict(
+            low=vmem((rows, width), BF),
+            doc=vmem((rows, width), BF),
+            dq=vmem((rows, width), F32),
+            dkv=vmem((2, texts, width), F32),
+            klow=vmem((texts, width), BF),
+            vlow=vmem((texts, width), BF),
+            stage=vmem((2, 384, width), BF),
+            sems=pltpu.SemaphoreType.DMA((5,)),
+            out_sem=pltpu.SemaphoreType.DMA((2,)),
+        )
+    )
+    any_place = pl.BlockSpec(memory_space=pl.ANY)
+    in_vmem = pl.BlockSpec(memory_space=pltpu.VMEM)
+    names = ["len"] + in_any + ins + list(any_outs) + list(outs) + list(scratch)
+    results = pl.pallas_call(
+        functools.partial(own_back_kernel, names),
+        out_shape=tuple(any_outs.values()) + tuple(outs.values()),
+        in_specs=[pl.BlockSpec(memory_space=pltpu.SMEM), any_place] + [in_vmem] * len(ins),
+        out_specs=(any_place,) * len(any_outs) + (in_vmem,) * len(outs),
+        scratch_shapes=list(scratch.values()),
+        compiler_params=pltpu.CompilerParams(vmem_limit_bytes=60 * 2**20),
+    )(*[getattr(arrays, name) for name in ["len"] + in_any + ins])
+    return types.SimpleNamespace(**dict(zip(list(any_outs) + list(outs), results)))
+
+
+def feed_kernel(n_sp, names, *refs):
+    ref = types.SimpleNamespace(**dict(zip(names, refs)))
+    zs, zr, ds, dr, local, cs, cr, saves_sem = (
+        getattr(ref, name) for name in ("zs", "zr", "ds", "dr", "local", "cs", "cr", "saves")
+    )
+    spot_d = lax.axis_index(DP)
+    spot_s = lax.axis_index(SP)
+    core = lax.rem(spot_d, 2)
+    core_id = {DP: spot_d + 1 - 2 * core}
+    line = [{SP: lax.rem(spot_s + step, n_sp)} for step in range(1, n_sp)]
+    h2_ref, all_ref = ref.h2, ref.h2_all
+    rows, width = h2_ref.shape
+    hidden = ref.in_own.shape[0]
+    win, wout = ref.win, ref.wout
+    meet(line + [core_id])
+
+    pieces = 2
+    piece = rows // pieces
+
+    def token_copy(way, k, part):
+        block = spot_s - k if way == 0 else spot_s + k
+        at = all_ref.at[rows_at(block * rows + part * piece, piece)]
+        src = h2_ref.at[pl.ds(part * piece, piece)] if k == 0 else at
+        target = {SP: spot_s + 1 if way == 0 else spot_s - 1}
+        index = (way * (n_sp - 1) + k) * pieces + part
+        return remote_copy(src, at, zs.at[index], zr.at[index], target)
+
+    def sends(way, k):
+        if way == 0:
+            return jnp.logical_and(spot_s < n_sp - 1, spot_s >= k)
+        return jnp.logical_and(spot_s > 0, spot_s + k < n_sp)
+
+    def gets(way, k):
+        return spot_s > k if way == 0 else spot_s + k + 1 < n_sp
+
+    def token_step(k):
+        for part in range(pieces):
+            for way in range(2):
+                if k > 0:
+
+                    @pl.when(gets(way, k - 1))
+                    def _():
+                        token_copy(way, k - 1, part).wait_recv()
+
+                if k < n_sp - 1:
+
+                    @pl.when(sends(way, k))
+                    def _():
+                        token_copy(way, k, part).start()
+
+    token_step(0)
+    keep = pltpu.make_async_copy(h2_ref, all_ref.at[rows_at(spot_s * rows, rows)], local.at[0])
+    keep.start()
+    loads = [
+        pltpu.make_async_copy(getattr(ref, src), goal.at[pl.ds(part * hidden, hidden)], local.at[1 + k])
+        for k, (src, goal, part) in enumerate(
+            (("in_own", win, 0), ("in_other", win, 1), ("out_own", wout, 0), ("out_other", wout, 1))
+        )
+    ]
+    for copy in loads:
+        copy.start()
+    gate = ref.time[5:6, :] + ref.par[5:6, :]
+    ref.du_sums[...] = jnp.zeros(ref.du_sums.shape, F32)
+    cot_ref, dz_ref, g_ref, du_ref = ref.cot, ref.dz, ref.g, ref.du
+    z_ref, part_ref, recv_ref, own_ref = ref.z, ref.part, ref.recv, ref.own
+    tiles = []
+    start = 0
+    while start < 2 * hidden:
+        tiles.append((start, min(768, 2 * hidden - start)))
+        start += 768
+    bend = (2.0 / np.pi) ** 0.5
+    keep.wait()
+    for copy in loads:
+        copy.wait()
+
+    def near(k):
+        first = (spot_s >= k).astype(jnp.int32)
+        return first, first + (spot_s + k < n_sp).astype(jnp.int32)
+
+    def grad_copy(block, owner):
+        return remote_copy(
+            part_ref.at[block],
+            recv_ref.at[spot_s],
+            ds.at[block],
+            dr.at[owner],
+            {SP: block},
+        )
+
+    def one(i, carry):
+        block = spot_s
+        before = jnp.int32(1)
+        for k in range(1, n_sp):
+            first, count = near(k)
+
+            @pl.when(i == before)
+            def _(k=k):
+                token_step(k)
+
+            here = jnp.logical_and(i >= before, i < before + count)
+            ahead = jnp.logical_and(first == 1, i == before)
+            block = jnp.where(here, jnp.where(ahead, spot_s - k, spot_s + k), block)
+            before = before + count
+        at = rows_at(block * rows, rows)
+        dz_ref[at, :] = (cot_ref[at, :].astype(F32) * gate).astype(BF)
+        for start, size in tiles:
+            place = pl.ds(start, size)
+            u = mm_t(all_ref[at, :], win[place, :]) + ref.bias[:, place]
+            cube = bend * (u + 0.044715 * (u * u * u))
+            t = jnp.tanh(cube)
+            g_ref[at, place] = (0.5 * u * (1.0 + t)).astype(BF)
+            slope = 0.5 * (1.0 + t) + (0.5 * bend) * u * (1.0 - t * t) * (
+                1.0 + (3 * 0.044715) * (u * u)
+            )
+            grad = (mm_t(dz_ref[at, :], wout[place, :]) * slope).astype(BF)
+            du_ref[at, place] = grad
+            ref.du_sums[:, place] += column_total(grad)
+        for start in range(0, width, 512):
+            place = pl.ds(start, 512)
+            value = mm(du_ref[at, :], win[:, place])
+            part_ref[block, :, place] = value.astype(BF)
+
+            @pl.when(i == 0)
+            def _():
+                own_ref[:, place] = value
+
+        @pl.when(i > 0)
+        def _():
+            grad_copy(block, spot_s).start()
+
+        for start in range(0, width, 512):
+            place = pl.ds(start, 512)
+            z_ref[block, :, place] = mm(g_ref[at, :], wout[:, place]).astype(BF)
+        return carry
+
+    lax.fori_loop(0, n_sp, one, 0)
+    z_save = pltpu.make_async_copy(z_ref, ref.z_out, local.at[5])
+    z_save.start()
+
+    def weight_grad(goal, left, right):
+        start = 0
+        while start < 2 * hidden:
+            size = min(256, 2 * hidden - start)
+            goal[start : start + size, :] = mm_first(
+                left[:, start : start + size], right[...]
+            ).astype(BF)
+            start += size
+
+    half = hidden // 2
+    core_copies = []
+
+    def core_hop(which, goal):
+        for part in range(2):
+            copy = remote_copy(
+                goal.at[rows_at(part * hidden + (1 - core) * half, half)],
+                ref.core_recv.at[which, part],
+                cs.at[2 * which + part],
+                cr.at[2 * which + part],
+                core_id,
+            )
+            copy.start()
+            core_copies.append(copy)
+
+    weight_grad(win, du_ref, all_ref)
+    core_hop(0, win)
+    weight_grad(wout, g_ref, dz_ref)
+    core_hop(1, wout)
+    low_ref = ref.core_recv
+    out_copies = []
+    chunk = half // 5
+    for which, goal in enumerate((win, wout)):
+        for part in range(2):
+            core_copies[2 * which + part].wait_recv()
+            for k in range(5):
+                at = rows_at(part * hidden + core * half + k * chunk, chunk)
+                value = goal[at, :].astype(F32) + low_ref[
+                    which, part, k * chunk : (k + 1) * chunk
+                ].astype(F32)
+                low_ref[which, part, k * chunk : (k + 1) * chunk] = value.astype(BF)
+            copy = pltpu.make_async_copy(
+                low_ref.at[which, part],
+                ref.f_out.at[which, part],
+                saves_sem.at[2 * which + part],
+            )
+            copy.start()
+            out_copies.append(copy)
+    for step in range(1, n_sp):
+        other = lax.rem(spot_s + step, n_sp)
+        grad_copy(other, other).wait_recv()
+    total = own_ref[...]
+    for step in range(1, n_sp):
+        total = total + recv_ref[lax.rem(spot_s + step, n_sp)].astype(F32)
+    ref.d_rows[...] = total
+    for copy in out_copies + [z_save]:
+        copy.wait()
+    for copy in core_copies:
+        copy.wait_send()
+    for step in range(1, n_sp):
+        other = lax.rem(spot_s + step, n_sp)
+        grad_copy(other, other).wait_send()
+    for k in range(n_sp - 1):
+        for part in range(pieces):
+            for way in range(2):
+
+                @pl.when(sends(way, k))
+                def _():
+                    token_copy(way, k, part).wait_send()
+
+
+def feed(**values):
+    arrays = types.SimpleNamespace(**values)
+    n_sp = lax.axis_size(SP)
+    shape = jax.ShapeDtypeStruct
+    rows, width = arrays.h2.shape
+    hidden = arrays.in_own.shape[0]
+    total = n_sp * rows
+    ins_any = ["in_own", "in_other", "out_own", "out_other", "h2"]
+    ins = ["cot", "bias", "time", "par"]
+    any_outs = dict(
+        z_out=shape((n_sp, rows, width), BF),
+        f_out=shape((2, 2, hidden // 2, width), BF),
+    )
+    outs = {"d_rows": shape((rows, width), F32), "du_sums": shape((1, 2 * hidden), F32)}
+    vmem = pltpu.VMEM
+    dma = pltpu.SemaphoreType.DMA
+    scratch = dict(
+        h2_all=vmem((total, width), BF),
+        win=vmem((2 * hidden, width), BF),
+        wout=vmem((2 * hidden, width), BF),
+        dz=vmem((total, width), BF),
+        g=vmem((total, 2 * hidden), BF),
+        du=vmem((total, 2 * hidden), BF),
+        z=vmem((n_sp, rows, width), BF),
+        part=vmem((n_sp, rows, width), BF),
+        recv=vmem((n_sp, rows, width), BF),
+        own=vmem((rows, width), F32),
+        core_recv=vmem((2, 2, hidden // 2, width), BF),
+        zs=dma((4 * (n_sp - 1),)),
+        zr=dma((4 * (n_sp - 1),)),
+        ds=dma((n_sp,)),
+        dr=dma((n_sp,)),
+        local=dma((6,)),
+        cs=dma((4,)),
+        cr=dma((4,)),
+        saves=dma((4,)),
+    )
+    any_place = pl.BlockSpec(memory_space=pl.ANY)
+    in_vmem = pl.BlockSpec(memory_space=pltpu.VMEM)
+    names = ins_any + ins + list(any_outs) + list(outs) + list(scratch)
+    results = pl.pallas_call(
+        functools.partial(feed_kernel, n_sp, names),
+        out_shape=tuple(any_outs.values()) + tuple(outs.values()),
+        in_specs=[any_place] * len(ins_any) + [in_vmem] * len(ins),
+        out_specs=(any_place,) * len(any_outs) + (in_vmem,) * len(outs),
+        scratch_shapes=list(scratch.values()),
+        compiler_params=pltpu.CompilerParams(
+            collective_id=3, has_side_effects=True, vmem_limit_bytes=60 * 2**20
+        ),
+    )(*[getattr(arrays, name) for name in ins_any + ins])
+    return types.SimpleNamespace(**dict(zip(list(any_outs) + list(outs), results)))
+
+
+class Later:
+    def __init__(self, make):
+        self.make = make
+
+    def wait_recv(self):
+        self.make().wait_recv()
+
+    def wait_send(self):
+        self.make().wait_send()
+
+
+def back_kernel(n_sp, n_dp, names, *refs):
+    ref = types.SimpleNamespace(**dict(zip(names, refs)))
+    sem_send, sem_recv, sem_local = ref.send, ref.recv, ref.local
+    spot_d = lax.axis_index(DP)
+    spot_b = lax.axis_index(BLK)
+    spot_s = lax.axis_index(SP)
+    core = lax.rem(spot_d, 2)
+    pair = lax.rem(spot_d // 2, 2)
+
+    def dp_id(bit):
+        return {DP: spot_d + bit - 2 * bit * lax.rem(spot_d // bit, 2)}
+
+    bits = []
+    bit = 4
+    while bit < n_dp:
+        bits.append(bit)
+        bit *= 2
+    core_id, pair_id, blk_id = dp_id(1), dp_id(2), {BLK: 1 - spot_b}
+    line = [{SP: lax.rem(spot_s + step, n_sp)} for step in range(1, n_sp)]
+    used = [0]
+    sent = []
+
+    def send(src, dst, target, view=None):
+        index = used[0]
+        used[0] += 1
+        copy = remote_copy(src, dst, sem_send.at[index], sem_recv.at[index], target)
+        copy.start()
+        if view is not None:
+            copy = Later(
+                lambda: remote_copy(
+                    view(), view(), sem_send.at[index], sem_recv.at[index], target
+                )
+            )
+        sent.append(copy)
+        return copy
+
+    def add_blocks(dst, sources):
+        lead = len(dst.shape) - 2
+
+        def body(*blocks):
+            total = blocks[0][...].astype(F32)
+            for block in blocks[1:-1]:
+                total = total + block[...].astype(F32)
+            blocks[-1][...] = total.astype(blocks[-1].dtype)
+
+        if lead == 0:
+            grid = (dst.shape[0] // 16,)
+            spec = pl.BlockSpec((16, dst.shape[1]), lambda place: (place, 0))
+        else:
+            group = 1
+            each = 2 * int(np.prod(dst.shape[1:]))
+            while dst.shape[0] % (2 * group) == 0 and 2 * group * each <= 700_000:
+                group *= 2
+            grid = (dst.shape[0] // group,)
+            spec = pl.BlockSpec(
+                (group,) + tuple(dst.shape[1:]), lambda place: (place,) + (0,) * (lead + 1)
+            )
+        pltpu.emit_pipeline(
+            body,
+            grid=grid,
+            in_specs=[spec] * len(sources),
+            out_specs=[spec],
+        )(*sources, dst)
+
+    meet(line + [core_id, pair_id, blk_id] + [dp_id(bit) for bit in bits])
+    d_att, do_ref = ref.d_att, ref.do
+    rows = d_att.shape[0]
+    total_rows = n_sp * rows
+    cols = do_ref.shape[1]
+    heads_here = cols // HD
+    width = d_att.shape[1]
+
+    def tok(block):
+        return rows_at(block * rows, rows)
+
+    do_own = pltpu.make_async_copy(
+        d_att.at[:, lanes_at(spot_s * cols, cols)], do_ref.at[tok(spot_s)], sem_local.at[0]
+    )
+    do_own.start()
+    do_away = [
+        send(
+            d_att.at[:, lanes_at(lax.rem(spot_s + step, n_sp) * cols, cols)],
+            do_ref.at[tok(spot_s)],
+            line[step - 1],
+        )
+        for step in range(1, n_sp)
+    ]
+    groups = ("co", "ckv")
+    hop = {}
+    for name in groups:
+        hop[name] = send(getattr(ref, name).at[:, 1 - core], getattr(ref, name + "_rc"), core_id)
+    hop["text"] = send(ref.text.at[1 - spot_b], ref.text_rx, blk_id)
+
+    blocks8 = 2 * n_sp
+
+    def core_done(name):
+        hop[name].wait_recv()
+        add_blocks(getattr(ref, name + "_kc"), [getattr(ref, name).at[:, core], getattr(ref, name + "_rc")])
+
+    score_scale = HD ** (-0.5)
+    dq_ref, dkv_ref = ref.dq, ref.dkv
+
+    def ff_last(name):
+        at = getattr(ref, name + "_out").at[core]
+        ry = getattr(ref, name + "_ry")
+        kx = getattr(ref, name + "_kx")
+        hop[name].wait_recv()
+        for k in range(len(bits) + 1):
+            goal = at if k == len(bits) else getattr(ref, name + "_ky").at[k]
+            source = kx if k == 0 else getattr(ref, name + "_ky").at[k - 1]
+            add_blocks(goal, [source, ry.at[k]])
+            if k < len(bits):
+                send(goal, ry.at[k + 1], dp_id(bits[k])).wait_recv()
+        hop[name] = send(at, at, core_id)
+
+    def pair_done(name, go=True):
+        if name in hop:
+            hop[name].wait_recv()
+            add_blocks(getattr(ref, name + "_ky"), [getattr(ref, name + "_kc").at[:, pair], getattr(ref, name + "_ry")])
+            del hop[name]
+        if not go:
+            return
+        hop[name] = send(
+            getattr(ref, name + "_ky").at[pl.ds((1 - spot_b) * n_sp, n_sp)], getattr(ref, name + "_rx"), blk_id
+        )
+
+    def blk_done(name):
+        hop[name].wait_recv()
+        own_blk = getattr(ref, name + "_ky").at[pl.ds(spot_b * n_sp, n_sp)]
+        add_blocks(getattr(ref, name + "_kx"), [own_blk, getattr(ref, name + "_rx")])
+
+    def line_send(name):
+        hop[name] = [
+            send(
+                getattr(ref, name + "_kx").at[lax.rem(spot_s + step, n_sp)],
+                getattr(ref, name + "_rz").at[step - 1],
+                line[step - 1],
+            )
+            for step in range(1, n_sp)
+        ]
+
+    def first_blk_done(name):
+        hop[name].wait_recv()
+        own_blk = getattr(ref, name + "_kc").at[pl.ds(spot_b * n_sp, n_sp)]
+        add_blocks(getattr(ref, name + "_ky"), [own_blk, getattr(ref, name + "_rx")])
+        hop[name] = send(getattr(ref, name + "_ky").at[:, 1 - pair], getattr(ref, name + "_ry"), pair_id)
+
+    def then_pair_done(name):
+        hop[name].wait_recv()
+        add_blocks(getattr(ref, name + "_kx"), [getattr(ref, name + "_ky").at[:, pair], getattr(ref, name + "_ry")])
+        line_send(name)
+
+    def attention(q_here, kv_here, lse_here):
+        ref.q_here, ref.kv_here, ref.lse_here = q_here, kv_here, lse_here
+        loads = [
+            pltpu.make_async_copy(getattr(ref, name), getattr(ref, name + "_here"), sem_local.at[2 + k])
+            for k, name in enumerate(("q", "kv", "lse"))
+        ]
+        for copy in loads:
+            copy.start()
+        q_ref, kv_ref, lse_ref = ref.q_here, ref.kv_here, ref.lse_here
+        dkv_ref[...] = jnp.zeros(dkv_ref.shape, F32)
+
+        def attend(block, carry):
+            at = tok(block)
+            for h in range(heads_here):
+                head = pl.ds(h * HD, HD)
+                query = q_ref[at, head]
+                grad = do_ref[at, head]
+                keys = kv_ref[0, :, head]
+                scores = mm_t(query, keys) * score_scale
+                probs = jnp.exp(scores - lse_ref[h, at, 0:1])
+                dkv_ref[1, :, head] += mm_first(probs.astype(BF), grad)
+                d_probs = mm_t(grad, kv_ref[1, :, head])
+                lean = jnp.sum(probs * d_probs, -1, keepdims=True)
+                d_scores = (probs * (d_probs - lean)).astype(BF)
+                dq_ref[at, head] = mm(d_scores, keys) * score_scale
+                dkv_ref[0, :, head] += mm_first(d_scores, query) * score_scale
+            return carry
+
+        for name in ("fi", "fo"):
+            add_blocks(getattr(ref, name + "_kx"), [getattr(ref, name), getattr(ref, name + "_rx")])
+            if name == "fi":
+                goal = lambda: ref.fi_ry.at[0]
+                hop[name] = send(ref.fi_kx, goal(), pair_id, goal)
+        for copy in loads:
+            copy.wait()
+        do_own.wait()
+        for copy in do_away:
+            copy.wait_recv()
+        lax.fori_loop(0, 1, attend, 0)
+        core_done("co")
+        goal = lambda: ref.co_rx
+        hop["co"] = send(
+            ref.co_kc.at[pl.ds((1 - spot_b) * n_sp, n_sp)], goal(), blk_id, goal
+        )
+        core_done("ckv")
+        goal = lambda: ref.ckv_ry
+        hop["ckv"] = send(ref.ckv_kc.at[:, 1 - pair], goal(), pair_id, goal)
+        for name in ("cq", "o"):
+            goal = lambda name=name: getattr(ref, name + "_rc")
+            hop[name] = send(getattr(ref, name).at[:, 1 - core], goal(), core_id, goal)
+        lax.fori_loop(1, 2, attend, 0)
+        core_done("cq")
+        goal = lambda: ref.cq_rx
+        hop["cq"] = send(
+            ref.cq_kc.at[pl.ds((1 - spot_b) * n_sp, n_sp)], goal(), blk_id, goal
+        )
+        lax.fori_loop(2, n_sp, attend, 0)
+
+    pl.run_scoped(
+        attention,
+        pltpu.VMEM(ref.q.shape, BF),
+        pltpu.VMEM(ref.kv.shape, BF),
+        pltpu.VMEM(ref.lse.shape, F32),
+    )
+
+    kv_recv, proj_ref = ref.kv_recv, ref.proj
+    kv_away = []
+    for which in range(2):
+        place = pl.ds(which * cols, cols)
+        proj_ref[:, place] = dkv_ref[which, total_rows:, :].astype(BF)
+        kv_away.append(send(proj_ref.at[:, place], kv_recv.at[which], blk_id))
+    core_done("o")
+    hop["text"].wait_recv()
+    text_kx = ref.text_kx
+    add_blocks(text_kx, [ref.text.at[spot_b], ref.text_rx])
+    hop["text"] = [
+        send(
+            text_kx.at[lax.rem(spot_s + step, n_sp)],
+            ref.text_rz.at[step - 1],
+            line[step - 1],
+        )
+        for step in range(1, n_sp)
+    ]
+
+    lin_ref, rho_ref, trig_ref = ref.lin, ref.rho, ref.trig
+    par_ref, sums_ref = ref.par, ref.sums
+    sums_ref[spot_s] = jnp.zeros((8, total_rows), F32)
+
+    def gain_of(which, h):
+        return par_ref[6 + which : 7 + which, lanes_at(spot_s * cols + h * HD, HD)]
+
+    def unturn(which, block, carry):
+        at = tok(block)
+        cosine = trig_ref[0, at, :]
+        sine = trig_ref[1, at, :]
+        lean = jnp.zeros((rows, HD), F32)
+        for h in range(heads_here):
+            head = pl.ds(h * HD, HD)
+            if which == 0:
+                grad = dq_ref[at, head]
+            else:
+                grad = dkv_ref[0, at, head] + kv_recv[0, at, head].astype(F32)
+            grad = turned(grad, cosine, -sine)
+            if which == 0:
+                dq_ref[at, head] = grad
+            else:
+                dkv_ref[0, at, head] = grad
+            lean = lean + lin_ref[which, at, head] * gain_of(which, h) * grad
+        total = exact_sums(lean)
+        sums_ref[spot_s, which : which + 1, lanes_at(block * rows, rows)] = total[0:1]
+        return carry
+
+    lax.fori_loop(0, n_sp, functools.partial(unturn, 0), 0)
+    first_blk_done("co")
+    ff_last("fi")
+    for copy in kv_away:
+        copy.wait()
+    sent[:] = [copy for copy in sent if all(copy is not other for other in kv_away)]
+    def first_blk_send(name):
+        hop[name] = send(
+            getattr(ref, name + "_kc").at[pl.ds((1 - spot_b) * n_sp, n_sp)], getattr(ref, name + "_rx"), blk_id
+        )
+
+    first_blk_send("o")
+    first_blk_done("cq")
+    hop["fo"] = send(ref.fo_kx, ref.fo_ry.at[0], pair_id)
+    lax.fori_loop(0, n_sp, functools.partial(unturn, 1), 0)
+    sums_away = [
+        send(sums_ref.at[spot_s], sums_ref.at[spot_s], line[k]) for k in range(n_sp - 1)
+    ]
+    then_pair_done("co")
+    for copy in sums_away:
+        copy.wait_recv()
+    means = sums_ref[0]
+    for k in range(1, n_sp):
+        means = means + sums_ref[k]
+    sums_ref[n_sp] = means / width
+    small_ref = ref.small
+    own = lanes_at(spot_s * cols, cols)
+    small_ref[0] = ref.small_in[...]
+    for row in (6, 7, 11, 12, 13):
+        small_ref[0, row : row + 1, :] = jnp.zeros((1, width), F32)
+
+    def project(block, carry):
+        at = tok(block)
+        for which in range(2):
+            mean = exact_first(sums_ref[n_sp, :, lanes_at(block * rows, rows)], row_pick(which))
+            rho = rho_ref[which, at, :]
+            cube = rho * rho * rho * mean
+            for h in range(heads_here):
+                head = pl.ds(h * HD, HD)
+                grad = dq_ref[at, head] if which == 0 else dkv_ref[0, at, head]
+                value = lin_ref[which, at, head]
+                low = (rho * gain_of(which, h) * grad - value * cube).astype(BF)
+                place = pl.ds(which * cols + h * HD, HD)
+                proj_ref[at, place] = low
+                here = lanes_at(spot_s * cols + h * HD, HD)
+                small_ref[0, 6 + which : 7 + which, here] += jnp.sum(
+                    grad * value * rho, 0, keepdims=True
+                )
+                small_ref[0, 11 + which : 12 + which, here] += jnp.sum(
+                    low.astype(F32), 0, keepdims=True
+                )
+        low = (dkv_ref[1, at, :] + kv_recv[1, at, :].astype(F32)).astype(BF)
+        proj_ref[at, 2 * cols :] = low
+        small_ref[0, 13:14, own] += jnp.sum(low.astype(F32), 0, keepdims=True)
+        return carry
+
+    lax.fori_loop(0, n_sp, project, 0)
+    dh1_ref, dh1_recv, sw_ref = ref.dh1, ref.dh1_recv, ref.sw
+    chain_send, chain_recv = ref.chain_send, ref.chain_recv
+
+    def chain_copy(way, block):
+        if way == 0:
+            slot, target = block, {SP: spot_s + 1}
+        else:
+            slot = jnp.where(block == spot_s - 1, n_sp, block)
+            target = {SP: spot_s - 1}
+        return remote_copy(
+            dh1_ref.at[block],
+            dh1_recv.at[slot],
+            chain_send.at[way * n_sp + block],
+            chain_recv.at[slot],
+            target,
+        )
+
+    def chain_wait(slot):
+        at = dh1_recv.at[slot]
+        remote_copy(at, at, chain_send.at[0], chain_recv.at[slot], blk_id).wait_recv()
+
+    def chain_pass(way, block, slot):
+        total = dh1_ref[block].astype(F32) + dh1_recv[slot].astype(F32)
+        dh1_ref[block] = total.astype(BF)
+        chain_copy(way, block).start()
+
+    def chain_step(time):
+        right = n_sp - 1 + spot_s - time
+        inside = jnp.logical_and(right >= spot_s, right < n_sp)
+
+        @pl.when(jnp.logical_and(spot_s > 0, inside))
+        def _():
+            chain_wait(right)
+
+            @pl.when(right > spot_s)
+            def _():
+                chain_pass(0, right, right)
+
+        left = time - (n_sp - 1 - spot_s)
+        inside = jnp.logical_and(left >= 0, left <= spot_s)
+
+        @pl.when(jnp.logical_and(spot_s < n_sp - 1, inside))
+        def _():
+            slot = jnp.where(left == spot_s, n_sp, left)
+            chain_wait(slot)
+
+            @pl.when(left < spot_s)
+            def _():
+                chain_pass(1, left, slot)
+
+    def products(w_ref, h1_ref, stage):
+        sw_copies = []
+        w_load = pltpu.make_async_copy(ref.w, w_ref, sem_local.at[0])
+        h1_load = pltpu.make_async_copy(ref.h1, h1_ref, sem_local.at[1])
+        w_load.start()
+        h1_load.start()
+        w_load.wait()
+        def away(step, carry):
+            turn = jnp.where(spot_s < n_sp // 2, n_sp - step, step)
+            block = lax.rem(spot_s + turn, n_sp)
+            for part in range(width // cols):
+                place = pl.ds(part * cols, cols)
+                value = mm_t(proj_ref[tok(block), :], w_ref[place, :])
+                dh1_ref[block, :, place] = value.astype(BF)
+
+            @pl.when(spot_s == 0)
+            def _():
+                chain_copy(0, block).start()
+
+            @pl.when(spot_s == n_sp - 1)
+            def _():
+                chain_copy(1, block).start()
+
+            return carry
+
+        lax.fori_loop(1, n_sp, away, 0)
+        for part in range(width // cols):
+            place = pl.ds(part * cols, cols)
+            ref.dh1_own[:, place] = mm_t(proj_ref[tok(spot_s), :], w_ref[place, :])
+        h1_load.wait()
+        for part in range(n_sp):
+            value = mm_first(h1_ref[:, part * cols : (part + 1) * cols], proj_ref[...])
+            value = value.astype(BF)
+            slot = part % 2
+            if part > 1:
+                sw_copies[part - 2].wait()
+            for k in range(4):
+                half = cols // 4
+                stage[slot, k // 2, k % 2] = value[k * half : (k + 1) * half]
+            copy = pltpu.make_async_copy(
+                stage.at[slot], sw_ref.at[pl.ds(2 * part, 2)], sem_local.at[2 + slot]
+            )
+            copy.start()
+            sw_copies.append(copy)
+        for copy in sw_copies[-2:]:
+            copy.wait()
+        hop["s"] = send(
+            sw_ref.at[:, 1 - core], ref.s_rc, core_id, lambda: ref.s_rc
+        )
+
+    pl.run_scoped(
+        products,
+        pltpu.VMEM(ref.w.shape, BF),
+        pltpu.VMEM(ref.h1.shape, BF),
+        pltpu.VMEM((2, 2, 2, cols // 4, 3 * cols), BF),
+    )
+
+    pair_done("ckv")
+    chain_step(1)
+    hop["s"].wait_recv()
+    add_blocks(ref.s_kc, [ref.sw.at[:, core], ref.s_rc])
+    hop["s"] = send(ref.s_kc.at[pl.ds((1 - spot_b) * n_sp, n_sp)], ref.s_rx, blk_id)
+    first_blk_done("o")
+    for k in range(2, n_sp - 1):
+        chain_step(k)
+    then_pair_done("cq")
+    for copy in hop["text"]:
+        copy.wait_recv()
+    add_blocks(
+        ref.text_out.at[0],
+        [text_kx.at[spot_s]] + [ref.text_rz.at[k] for k in range(n_sp - 1)],
+    )
+
+    chain_step(n_sp - 1)
+
+    @pl.when(spot_s > 0)
+    def _():
+        ref.dh1_own[...] += dh1_recv[spot_s].astype(F32)
+
+    @pl.when(spot_s < n_sp - 1)
+    def _():
+        ref.dh1_own[...] += dh1_recv[n_sp].astype(F32)
+
+    d_shift = ref.dh1_own[...]
+    values = ref.x[...].astype(F32)
+    centre = values - jnp.mean(values, axis=-1, keepdims=True)
+    spread = lax.rsqrt(jnp.mean(centre * centre, axis=-1, keepdims=True) + EPS)
+    normed = centre * spread
+    scale = 1.0 + (ref.time[1:2, :] + par_ref[1:2, :])
+    grad = d_shift * scale
+    lean = jnp.mean(grad, axis=-1, keepdims=True)
+    tilt = jnp.mean(grad * normed, axis=-1, keepdims=True)
+    ref.tokens_out[...] = ref.dx1[...] + spread * (grad - lean - normed * tilt)
+    small_ref[0, 0:1, :] = jnp.sum(d_shift, 0, keepdims=True)
+    small_ref[0, 1:2, :] = jnp.sum(d_shift * normed, 0, keepdims=True)
+    partners = [core_id, pair_id] + [dp_id(bit) for bit in bits] + [blk_id]
+    bit = 1
+    while bit < n_sp:
+        partners.append({SP: spot_s + bit - 2 * bit * lax.rem(spot_s // bit, 2)})
+        bit *= 2
+
+    def small_send(k):
+        hop["small"] = send(small_ref.at[k], ref.small_recv.at[k], partners[k])
+
+    def small_done(k):
+        hop["small"].wait_recv()
+        small_ref[k + 1] = small_ref[k] + ref.small_recv[k]
+        if k + 1 < len(partners):
+            small_send(k + 1)
+        else:
+            ref.small_out[...] = small_ref[k + 1]
+
+    small_send(0)
+    blk_done("ckv")
+    line_send("ckv")
+    hop["s"].wait_recv()
+    own_blk = ref.s_kc.at[pl.ds(spot_b * n_sp, n_sp)]
+    add_blocks(ref.s_kx, [own_blk, ref.s_rx])
+    small_done(0)
+    s_line = []
+    s_keep = []
+    for j in range(3):
+        place = lanes_at(j * width + spot_s * cols, cols)
+        part = pl.ds(j * cols, cols)
+        copy = pltpu.make_async_copy(
+            ref.s_kx.at[spot_s, :, part], ref.s_z.at[:, place], sem_local.at[2 + j]
+        )
+        copy.start()
+        s_keep.append(copy)
+        for step in range(1, n_sp):
+            s_line.append(
+                send(
+                    ref.s_kx.at[lax.rem(spot_s + step, n_sp), :, part],
+                    ref.s_z.at[:, place],
+                    line[step - 1],
+                )
+            )
+    then_pair_done("o")
+
+    def line_done(name):
+        for copy in hop[name]:
+            copy.wait_recv()
+        kx, rz = getattr(ref, name + "_kx"), getattr(ref, name + "_rz")
+        out = getattr(ref, name + "_out").at[core]
+        kz = getattr(ref, name + "_kz")
+        add_blocks(
+            kz.at[0], [kx.at[spot_s]] + [rz.at[k] for k in range(n_sp - 1)]
+        )
+        for k, bit in enumerate(bits):
+            got = getattr(ref, name + "_rw").at[k]
+            send(kz.at[k], got, dp_id(bit)).wait_recv()
+            add_blocks(kz.at[k + 1], [kz.at[k], got])
+        last = kz.at[len(bits)]
+        own_copy = pltpu.make_async_copy(last, out.at[pair], sem_local.at[1])
+        own_copy.start()
+        hop[name] = send(last, out.at[pair], pair_id)
+        own_copy.wait()
+
+    def pair_back(name):
+        hop[name].wait_recv()
+        out = getattr(ref, name + "_out").at[core]
+        hop[name] = send(out, out, core_id)
+
+    small_done(1)
+    line_done("co")
+    for k in range(2, len(partners) - 2):
+        small_done(k)
+    line_done("cq")
+    for copy in s_keep:
+        copy.wait()
+    for copy in s_line:
+        copy.wait_recv()
+    hop["s"] = send(ref.s_z, ref.s_ry.at[0], pair_id)
+    small_done(len(partners) - 2)
+    line_done("ckv")
+    ff_last("fo")
+    small_done(len(partners) - 1)
+    pair_back("co")
+    pair_back("cq")
+    line_done("o")
+    hop["s"].wait_recv()
+    s_ry, s_out = ref.s_ry, ref.s_out
+    for k in range(len(bits) + 1):
+        source = ref.s_z if k == 0 else ref.s_kw.at[k - 1]
+        goal = s_out.at[core] if k == len(bits) else ref.s_kw.at[k]
+        add_blocks(goal, [source, s_ry.at[k]])
+        if k < len(bits):
+            send(goal, s_ry.at[k + 1], dp_id(bits[k])).wait_recv()
+    hop["s"] = send(s_out.at[core], s_out.at[core], core_id)
+    pair_back("ckv")
+    pair_back("o")
+    for name in ("ckv", "co", "cq", "o", "fi", "fo", "s"):
+        hop[name].wait_recv()
+    for copy in sent:
+        copy.wait_send()
+    for block in range(n_sp):
+
+        @pl.when(block > spot_s)
+        def _():
+            chain_copy(0, block).wait_send()
+
+        @pl.when(block < spot_s)
+        def _():
+            chain_copy(1, block).wait_send()
+
+
+def back(**values):
+    arrays = types.SimpleNamespace(**values)
+    n_sp = lax.axis_size(SP)
+    n_dp = lax.axis_size(DP)
+    shape = jax.ShapeDtypeStruct
+    rows, width = arrays.d_att.shape
+    total = n_sp * rows
+    cols = arrays.q.shape[1]
+    g8 = 2 * n_sp
+    more = max(n_dp.bit_length() - 3, 0)
+    any_names = ["ckv", "cq", "co", "o", "fi", "fo", "fi_rx", "fo_rx", "d_att", "text", "q", "kv", "lse", "w", "h1"]
+    vmem_names = ["lin", "rho", "trig", "par", "x", "dx1", "time", "small_in"]
+    outs = {}
+    for name in ("ckv", "cq", "co", "o"):
+        quarter, lanes = getattr(arrays, name).shape[3:]
+        outs[name + "_rc"] = shape((g8, 2, quarter, lanes), BF)
+        outs[name + "_kc"] = shape((g8, 2, quarter, lanes), BF)
+        if name == "ckv":
+            outs[name + "_ry"] = shape((g8, quarter, lanes), BF)
+            outs[name + "_ky"] = shape((g8, quarter, lanes), BF)
+            outs[name + "_rx"] = shape((n_sp, quarter, lanes), BF)
+        else:
+            outs[name + "_rx"] = shape((n_sp, 2, quarter, lanes), BF)
+            outs[name + "_ky"] = shape((n_sp, 2, quarter, lanes), BF)
+            outs[name + "_ry"] = shape((n_sp, quarter, lanes), BF)
+        outs[name + "_kx"] = shape((n_sp, quarter, lanes), BF)
+        outs[name + "_rz"] = shape((n_sp - 1, quarter, lanes), BF)
+        outs[name + "_kz"] = shape((more + 1, quarter, lanes), BF)
+        outs[name + "_rw"] = shape((more + 1, quarter, lanes), BF)
+        outs[name + "_out"] = shape((2, 2, quarter, lanes), BF)
+    for name in ("fi", "fo"):
+        half = getattr(arrays, name).shape
+        outs[name + "_kx"] = shape(half, BF)
+        outs[name + "_ry"] = shape((more + 1,) + half, BF)
+        outs[name + "_ky"] = shape((more + 1,) + half, BF)
+        outs[name + "_out"] = shape((2,) + half, BF)
+    text_rows = arrays.text.shape[2]
+    outs.update(text_rx=shape((n_sp, text_rows, width), BF))
+    outs.update(text_kx=shape((n_sp, text_rows, width), BF))
+    outs.update(text_rz=shape((n_sp - 1, text_rows, width), BF))
+    outs.update(text_out=shape((1, text_rows, width), F32))
+    half_rows = width // g8 // 2
+    outs.update(sw=shape((g8, 2, half_rows, 3 * cols), BF))
+    outs.update(s_rc=shape((g8, half_rows, 3 * cols), BF))
+    outs.update(s_kc=shape((g8, half_rows, 3 * cols), BF))
+    outs.update(s_rx=shape((n_sp, half_rows, 3 * cols), BF))
+    outs.update(s_kx=shape((n_sp, half_rows, 3 * cols), BF))
+    outs.update(s_z=shape((half_rows, 3 * width), BF))
+    outs.update(s_ry=shape((more + 1, half_rows, 3 * width), BF))
+    outs.update(s_kw=shape((more + 1, half_rows, 3 * width), BF))
+    outs.update(s_out=shape((2, half_rows, 3 * width), BF))
+    in_any = len(outs)
+    outs.update(tokens_out=shape((rows, width), F32))
+    outs.update(small_out=shape(arrays.small_in.shape, F32))
+    steps = 3 + more + n_sp.bit_length() - 1
+    vmem = pltpu.VMEM
+    scratch = dict(
+        do=vmem((total, cols), BF),
+        dq=vmem((total, cols), F32),
+        dkv=vmem((2, 2 * total, cols), F32),
+        kv_recv=vmem((2, total, cols), BF),
+        sums=vmem((n_sp + 1, 8, total), F32),
+        proj=vmem((total, 3 * cols), BF),
+        dh1=vmem((n_sp, rows, width), BF),
+        dh1_own=vmem((rows, width), F32),
+        dh1_recv=vmem((n_sp + 1, rows, width), BF),
+        chain_send=pltpu.SemaphoreType.DMA((2 * n_sp,)),
+        chain_recv=pltpu.SemaphoreType.DMA((n_sp + 1,)),
+        small=vmem((steps + 1,) + arrays.small_in.shape, F32),
+        small_recv=vmem((steps,) + arrays.small_in.shape, F32),
+        send=pltpu.SemaphoreType.DMA((128,)),
+        recv=pltpu.SemaphoreType.DMA((128,)),
+        local=pltpu.SemaphoreType.DMA((5,)),
+    )
+    any_place = pl.BlockSpec(memory_space=pl.ANY)
+    in_vmem = pl.BlockSpec(memory_space=pltpu.VMEM)
+    names = any_names + vmem_names + list(outs) + list(scratch)
+    results = pl.pallas_call(
+        functools.partial(back_kernel, n_sp, n_dp, names),
+        out_shape=tuple(outs.values()),
+        in_specs=[any_place] * len(any_names) + [in_vmem] * len(vmem_names),
+        out_specs=(any_place,) * in_any + (in_vmem,) * (len(outs) - in_any),
+        scratch_shapes=list(scratch.values()),
+        compiler_params=pltpu.CompilerParams(
+            collective_id=2, has_side_effects=True, vmem_limit_bytes=60 * 2**20
+        ),
+    )(*[getattr(arrays, name) for name in any_names + vmem_names])
+    return types.SimpleNamespace(**dict(zip(outs, results)))
 
 
 def swap_blk(value):
-    return lax.ppermute(value, "blk", [(0, 1), (1, 0)])
-
-
-def swap_dp(value, bit):
-    size = lax.axis_size("dp")
-    return lax.ppermute(value, "dp", [(i, i ^ bit) for i in range(size)])
-
-
-def gather_sp(value):
-    size = lax.axis_size("sp")
-    return [value] + [from_back(value, step) for step in range(1, size)]
-
-
-def total_sp(own, parts):
-    total = own
-    for step in range(1, len(parts)):
-        total = total + to_back(parts[step].astype(BF), step).astype(F32)
-    return total
-
-
-def in_order_back(blocks, place, axis):
-    size = len(blocks)
-    back = blocks[::-1]
-    whole = jnp.concatenate(back + back[:-1], axis)
-    width = blocks[0].shape[axis]
-    return lax.dynamic_slice_in_dim(whole, (size - 1 - place) * width, size * width, axis)
-
-
-def in_order_ahead(blocks, place, axis):
-    size = len(blocks)
-    whole = jnp.concatenate(blocks + blocks[:-1], axis)
-    width = blocks[0].shape[axis]
-    return lax.dynamic_slice_in_dim(whole, ((size - place) % size) * width, size * width, axis)
-
-
-def pair_order(own, other, place, axis):
-    return jnp.where(
-        place == 0, jnp.concatenate([own, other], axis), jnp.concatenate([other, own], axis)
-    )
-
-
-def part_of(value, index, count, axis):
-    width = value.shape[axis] // count
-    return lax.dynamic_slice_in_dim(value, index * width, width, axis)
-
-
-def sum_sp_rows(sums):
-    size = lax.axis_size("sp")
-    total = sums
-    for step in range(1, size):
-        total = total + from_back(sums, step)
-    return total
+    return lax.ppermute(value, BLK, [(0, 1), (1, 0)])
 
 
 def local(
@@ -915,11 +2081,11 @@
     ffn_bias,
     cotangent,
 ):
-    n_sp = lax.axis_size("sp")
-    n_dp = lax.axis_size("dp")
-    spot_dp = lax.axis_index("dp")
-    spot_b = lax.axis_index("blk")
-    spot_s = lax.axis_index("sp")
+    n_sp = lax.axis_size(SP)
+    n_dp = lax.axis_size(DP)
+    spot_dp = lax.axis_index(DP)
+    spot_b = lax.axis_index(BLK)
+    spot_s = lax.axis_index(SP)
     core = spot_dp % 2
     pair = (spot_dp // 2) % 2
     x_own = clip_tokens[0]
@@ -970,343 +2136,131 @@
         cotangent[0],
         time_embed[0],
     )
-    out_self = rest_all[:, :width]
-    out_cross = rest_all[:, width : 2 * width]
-    qkv_cross = rest_all[:, 2 * width :]
-    in_all = jnp.concatenate([ffn_in, in_other], 0)
-    out_all = jnp.concatenate([ffn_out, out_other], 0)
-    cot_blocks = [part_of(cot_every, (spot_s - step) % n_sp, n_sp, 0) for step in range(n_sp)]
     mods = time_embed[0] + params[:6]
     gain_all = params[6:11]
     bias_all = params[11:21]
     ff_here = ffn_in.shape[0]
     bias_own = ffn_bias.astype(F32)
     bias_ff = jnp.concatenate([bias_own, swap_blk(ffn_bias).astype(F32)])
-    half_rows = shard_rows // 2
-
-    def own_cols(row):
-        return part_of(row, spot_s, n_sp, row.ndim - 1)
-
-    gain_cols = own_cols(gain_all)
-    q_lin = lin_parts[0]
-    k_lin = lin_parts[1]
-    rows_all = q_lin.shape[0]
-    rho = rho[:, :, :1]
-    cosine = trig[0]
-    sine_part = trig[1]
-
-    def heads(value):
-        return value.reshape(-1, heads_here, HD)
-
-    q_own = heads(q_flat)
-    k_every = heads(kv_flat[0])
-    v_every = heads(kv_flat[1])
-
-    block_count = 2
-    block_rows = rows_all // block_count
-    lse_parts = [
-        lse_wide[:, block * block_rows : (block + 1) * block_rows, 0]
-        for block in range(block_count)
-    ]
-
-    tokens = x_own.astype(F32)
-    a_lin = dot(att_tok, out_self) + bias_all[3]
-    x_one = tokens + mods[2] * a_lin
-    normed_three = layer_norm(x_one)
-    cross_in = (normed_three * gain_all[2] + bias_all[8]).astype(BF)
-    qc_lin = dot(cross_in, qkv_cross[:, :width]) + bias_all[4]
-    q_cross = rms_norm(qc_lin, gain_all[3]).astype(BF).reshape(tok_rows, H, HD)
-    kv_lin = dot(text_every, qkv_cross[:, width:]) + jnp.concatenate([bias_all[5], bias_all[6]])
-    k_cross = rms_norm(kv_lin[:, :width], gain_all[4]).astype(BF).reshape(-1, H, HD)
-    v_cross = kv_lin[:, width:].astype(BF).reshape(-1, H, HD)
-    text_rows = text_tokens.shape[1]
-    valid = jnp.arange(text_every.shape[0], dtype=jnp.int32) < text_lengths[0]
-    scores_c = (
-        jnp.einsum("rhe,khe->hrk", q_cross, k_cross, preferred_element_type=F32) * scale
-    )
-    probs_c = softmax_rows(jnp.where(valid[None, None, :], scores_c, NEG))
-    probs_cb = probs_c.astype(BF)
-    crossed = (
-        jnp.einsum("hrk,khe->rhe", probs_cb, v_cross, preferred_element_type=F32)
-        .reshape(tok_rows, width)
-        .astype(BF)
-    )
-    c_lin = dot(crossed, out_cross) + bias_all[7]
-    x_two = x_one + c_lin
-    normed_two = layer_norm(x_two)
-    ffn_rows = (normed_two * (1.0 + mods[4]) + mods[3]).astype(BF)
-
-    h2_blocks = gather_sp(ffn_rows)
-    z_parts = []
-    dh2_parts = []
-    g_blocks = []
-    du_blocks = []
-    dz_blocks = []
-    for step in range(n_sp):
-        u_lin = dot_t(h2_blocks[step], in_all) + bias_ff
-        g_act, gelu_back = jax.vjp(gelu_tanh, u_lin)
-        g_low = g_act.astype(BF)
-        d_z = (cot_blocks[step].astype(F32) * mods[5]).astype(BF)
-        d_g = dot_t(d_z, out_all)
-        d_u = gelu_back(d_g)[0].astype(BF)
-        dh2_parts.append(dot(d_u, in_all))
-        z_parts.append(dot(g_low, out_all))
-        g_blocks.append(g_low)
-        du_blocks.append(d_u)
-        dz_blocks.append(d_z)
-    d_rows = total_sp(dh2_parts[0], dh2_parts)
-    z_line = jnp.zeros((n_sp, tok_rows, width), BF)
-    for step in range(n_sp):
-        z_line = lax.dynamic_update_index_in_dim(
-            z_line, z_parts[step].astype(BF), (spot_s - step) % n_sp, 0
-        )
+    own = own_tokens(
+        text_lengths, rest_all, x_own, att_tok, text_every, time_embed[0], params
+    )
+    ffn_rows = own.h2
+    x_two = own.two
+
+    fed = feed(**dict(
+            in_own=ffn_in,
+            in_other=in_other,
+            out_own=ffn_out,
+            out_other=out_other,
+            h2=ffn_rows,
+            cot=cot_every,
+            bias=bias_ff[None],
+            time=time_embed[0],
+            par=params,
+        )
+    )
+    d_rows = fed.d_rows
+    du_sums = fed.du_sums[0]
     z_lin = (
-        lax.psum_scatter(z_line, "sp", scatter_dimension=0, tiled=False).astype(F32) + bias_all[9]
+        lax.psum_scatter(fed.z_out, SP, scatter_dimension=0, tiled=False).astype(F32)
+        + bias_all[9]
     )
     grad_y = cotangent[0].astype(F32)
     result = x_two + mods[5] * z_lin
     block_out = result.astype(BF)[None]
     d_gate2 = jnp.sum(grad_y * z_lin, 0)
-    du_all = jnp.concatenate(du_blocks, 0)
-    g_all = jnp.concatenate(g_blocks, 0)
-    h2_all = jnp.concatenate(h2_blocks, 0)
-    dz_all = jnp.concatenate(dz_blocks, 0)
-    g_hidden_in = dot_g(du_all, h2_all).astype(BF)
-    g_hidden_out = dot_g(g_all, dz_all).astype(BF)
-    du_sums = col_sum(du_all)
-
-    def round_add(own, got):
-        return own.astype(F32) + got.astype(F32)
-
-    def core_half(grad, which):
-        return part_of(grad[:ff_here], which, 2, 0), part_of(grad[ff_here:], which, 2, 0)
-
-    keep_in = core_half(g_hidden_in, core)
-    keep_out = core_half(g_hidden_out, core)
-    away_in = core_half(g_hidden_in, 1 - core)
-    away_out = core_half(g_hidden_out, 1 - core)
-    ff_core = swap_dp(jnp.stack([away_in[0], away_out[0], away_in[1], away_out[1]]), 1)
-    ff_sum = round_add(
-        jnp.stack([keep_in[0], keep_out[0], keep_in[1], keep_out[1]]), ff_core
-    )
-    ff_part = ff_sum[:2] + swap_blk(ff_sum[2:].astype(BF)).astype(F32)
-    bit = 2
-    while bit < n_dp:
-        low = ff_part.astype(BF)
-        ff_part = round_add(low, swap_dp(low, bit))
-        bit *= 2
-    ff_low = ff_part.astype(BF)
-    ff_final = pair_order(ff_low, swap_dp(ff_low, 1), core, 1).astype(F32)
-
-    d_shift2 = jnp.sum(d_rows, 0)
-    d_scale2 = jnp.sum(d_rows * normed_two, 0)
-    d_x_two = grad_y + layer_back(x_two, d_rows * (1.0 + mods[4]))
-
-    def scatter_weight(rows, grads):
-        def half(which):
-            return dot_g(rows, part_of(grads, which, 2, 1))
-
-        got = swap_dp(half(1 - core).astype(BF), 1)
-        total = half(core) + got.astype(F32)
-        away = part_of(total, 1 - pair, 2, 1).astype(BF)
-        total = part_of(total, pair, 2, 1) + swap_dp(away, 2).astype(F32)
-        return lax.psum_scatter(
-            total.astype(BF), ("blk", "sp"), scatter_dimension=0, tiled=True
-        ).astype(F32)
-
-    def spread_weight(total):
-        bit = 4
-        while bit < n_dp:
-            low = total.astype(BF)
-            total = round_add(low, swap_dp(low, bit))
-            bit *= 2
-        low = total.astype(BF)
-        low = pair_order(low, swap_dp(low, 2), pair, 1)
-        return pair_order(low, swap_dp(low, 1), core, 1).astype(F32)
-
-    d_c = d_x_two.astype(BF)
-    g_out_cross = scatter_weight(crossed, d_c)
-    d_oc = dot_t(d_c, out_cross).astype(BF).reshape(tok_rows, H, HD)
-    d_vc = jnp.einsum("hrk,rhe->khe", probs_cb, d_oc, preferred_element_type=F32)
-    d_pc = jnp.einsum("rhe,khe->hrk", d_oc, v_cross, preferred_element_type=F32)
-    d_sc = (probs_c * (d_pc - jnp.sum(probs_c * d_pc, -1, keepdims=True))).astype(BF)
-    d_qc = jnp.einsum("hrk,khe->rhe", d_sc, k_cross, preferred_element_type=F32) * scale
-    d_kc = jnp.einsum("hrk,rhe->khe", d_sc, q_cross, preferred_element_type=F32) * scale
-    d_qc_lin, d_gain3 = jax.vjp(rms_norm, qc_lin, gain_all[3])[1](d_qc.reshape(tok_rows, width))
-    d_qc_low = d_qc_lin.astype(BF)
-    d_cross_in = dot_t(d_qc_low, qkv_cross[:, :width])
-    d_gain2 = jnp.sum(d_cross_in * normed_three, 0)
-    d_bias8 = jnp.sum(d_cross_in, 0)
-    d_x_one = d_x_two + layer_back(x_one, d_cross_in * gain_all[2])
-    d_a = (d_x_one * mods[2]).astype(BF)
-    d_gate1 = jnp.sum(d_x_one * a_lin, 0)
-    d_att = dot_t(d_a, out_self).astype(BF)
-
-    d_o_line = lax.all_to_all(
-        d_att.reshape(tok_rows, n_sp, cols_here).transpose(1, 0, 2),
-        "sp",
-        split_axis=0,
-        concat_axis=0,
-        tiled=True,
-    )
-    d_o = heads(d_o_line.reshape(rows_all, cols_here))
-
-    text_all = d_kc.shape[0]
-    d_kc_lin, d_gain4 = jax.vjp(rms_norm, kv_lin[:, :width], gain_all[4])[1](
-        d_kc.reshape(text_all, width)
-    )
-    d_kv_lin = jnp.concatenate(
-        [d_kc_lin.astype(BF), d_vc.reshape(text_all, width).astype(BF)], -1
-    )
-    text_part = dot_t(d_kv_lin, qkv_cross[:, width:])
-    grad_text = lax.psum_scatter(
-        text_part.astype(BF), ("blk", "sp"), scatter_dimension=0, tiled=True
-    ).astype(F32)
-    g_q_cross = scatter_weight(cross_in, d_qc_low)
-    g_kv_cross = scatter_weight(text_every, d_kv_lin)
-    g_out_self = scatter_weight(att_tok, d_a)
-
-    acc_k = jnp.zeros(k_every.shape, F32)
-    acc_v = jnp.zeros(k_every.shape, F32)
-    dq_parts = []
-    for block in range(block_count):
-        q_block = q_own[block * block_rows : (block + 1) * block_rows]
-        do_block = d_o[block * block_rows : (block + 1) * block_rows]
-        scores = (
-            jnp.einsum("rhe,khe->hrk", q_block, k_every, preferred_element_type=F32) * scale
-        )
-        probs = jnp.exp(scores - lse_parts[block][..., None])
-        acc_v = acc_v + jnp.einsum(
-            "hrk,rhe->khe", probs.astype(BF), do_block, preferred_element_type=F32
-        )
-        d_p = jnp.einsum("rhe,khe->hrk", do_block, v_every, preferred_element_type=F32)
-        d_s = (probs * (d_p - jnp.sum(probs * d_p, -1, keepdims=True))).astype(BF)
-        dq_parts.append(
-            jnp.einsum("hrk,khe->rhe", d_s, k_every, preferred_element_type=F32) * scale
-        )
-        acc_k = (
-            acc_k
-            + jnp.einsum("hrk,rhe->khe", d_s, q_block, preferred_element_type=F32) * scale
-        )
-    kv_away = jnp.stack([acc_k[rows_all:].astype(BF), acc_v[rows_all:].astype(BF)])
-    kv_got = swap_blk(kv_away.reshape(2, rows_all, cols_here)).astype(F32)
-    d_k = acc_k[:rows_all].reshape(rows_all, cols_here) + kv_got[0]
-    d_v = acc_v[:rows_all].reshape(rows_all, cols_here) + kv_got[1]
-    d_q = jnp.concatenate(dq_parts, 0)
-
-    def unturn(grad):
-        return rotate(heads(grad), cosine, -sine_part).reshape(rows_all, cols_here)
-
-    e_q = unturn(d_q)
-    e_k = unturn(d_k)
-    vge_q = q_lin * gain_cols[0] * e_q
-    vge_k = k_lin * gain_cols[1] * e_k
-    means = jnp.stack([jnp.sum(vge_q, -1), jnp.sum(vge_k, -1)])
-    means = sum_sp_rows(means) / width
-    cubes = (rho * rho * rho) * means[..., None]
-    d_q_lin = rho[0] * gain_cols[0] * e_q - q_lin * cubes[0]
-    d_k_lin = rho[1] * gain_cols[1] * e_k - k_lin * cubes[1]
-    d_gain0 = jnp.sum(e_q * q_lin * rho[0], 0)
-    d_gain1 = jnp.sum(e_k * k_lin * rho[1], 0)
-    d_proj = jnp.concatenate([d_q_lin.astype(BF), d_k_lin.astype(BF), d_v.astype(BF)], -1)
-    dh1_part = dot_t(d_proj, qkv_mine)
-    dh1_steps = [part_of(dh1_part, (spot_s - step) % n_sp, n_sp, 0) for step in range(n_sp)]
-    d_shift = total_sp(dh1_steps[0], dh1_steps)
-    normed_one = layer_norm(tokens)
-    grad_tokens = d_x_one + layer_back(tokens, d_shift * (1.0 + mods[1]))
-    d_shift1 = jnp.sum(d_shift, 0)
-    d_scale1 = jnp.sum(d_shift * normed_one, 0)
-
-    g_qkv = dot_g(h1_all, d_proj).astype(BF).reshape(2 * n_sp, 2, half_rows, 3 * cols_here)
-    qkv_core = swap_dp(jnp.take(g_qkv, 1 - core, axis=1), 1)
-    qkv_sum = round_add(jnp.take(g_qkv, core, axis=1), qkv_core)
-    qkv_sum = part_of(qkv_sum, spot_b, 2, 0) + swap_blk(
-        part_of(qkv_sum, 1 - spot_b, 2, 0).astype(BF)
-    ).astype(F32)
-    qkv_line = lax.all_to_all(
-        qkv_sum.astype(BF), "sp", split_axis=0, concat_axis=0, tiled=True
-    )
-    bit = 2
-    while bit < n_dp:
-        qkv_line = round_add(qkv_line, swap_dp(qkv_line, bit)).astype(BF)
-        bit *= 2
-    qkv_rows = pair_order(qkv_line, swap_dp(qkv_line, 1), core, 1)
-    part_sqkv = (
-        qkv_rows.reshape(n_sp, shard_rows, 3, cols_here)
-        .transpose(1, 2, 0, 3)
-        .reshape(shard_rows, 3 * width)
-        .astype(F32)
-    )
-
-    def wide(row):
-        return lax.dynamic_update_slice_in_dim(
-            jnp.zeros((width,), F32), row, spot_s * cols_here, 0
-        )
-
-    proj_sums = col_sum(d_proj)
-    kv_sums = col_sum(d_kv_lin)
+    last = own_back(**dict(
+            len=text_lengths,
+            rest=rest_all,
+            x_two=x_two,
+            x_one=own.one,
+            d_rows=d_rows,
+            cot=cotangent[0],
+            time=time_embed[0],
+            par=params,
+            a=own.a,
+            cin=own.cin,
+            ql=own.ql,
+            kl=own.kl,
+            q=own.q,
+            kv=own.kv,
+            lse=own.lse,
+            oc=own.oc,
+            att=att_tok,
+            text_in=text_every,
+        )
+    )
+
     ff_total = ff_here * 2 * n_sp
     ff_row = jnp.zeros((-(-ff_total // width) * width,), F32)
     own_at = (spot_b * n_sp + spot_s) * ff_here
     far_at = ((1 - spot_b) * n_sp + spot_s) * ff_here
     ff_row = lax.dynamic_update_slice_in_dim(ff_row, du_sums[:ff_here], own_at, 0)
     ff_row = lax.dynamic_update_slice_in_dim(ff_row, du_sums[ff_here:], far_at, 0)
-    small = jnp.concatenate(
-        [
-            jnp.stack(
-                [
-                    d_shift1,
-                    d_scale1,
-                    d_gate1,
-                    d_shift2,
-                    d_scale2,
-                    d_gate2,
-                    wide(d_gain0),
-                    wide(d_gain1),
-                    d_gain2,
-                    d_gain3,
-                    d_gain4,
-                    wide(proj_sums[:cols_here]),
-                    wide(proj_sums[cols_here : 2 * cols_here]),
-                    wide(proj_sums[2 * cols_here :]),
-                    col_sum(d_a),
-                    col_sum(d_qc_low),
-                    kv_sums[:width],
-                    kv_sums[width:],
-                    col_sum(d_c),
-                    d_bias8,
-                    col_sum(dz_blocks[0]),
-                ]
-            ),
-            ff_row.reshape(-1, width),
-        ],
-        0,
-    )
-    bit = 1
-    while bit < n_dp:
-        small = small + swap_dp(small, bit)
-        bit *= 2
-    small = small + swap_blk(small)
-    bit = 1
-    while bit < n_sp:
-        small = small + lax.ppermute(small, "sp", [(i, i ^ bit) for i in range(n_sp)])
-        bit *= 2
+    small = last.sums
+    small = lax.dynamic_update_slice(small, d_gate2[None], (5, 0))
+    small = lax.dynamic_update_slice(small, ff_row.reshape(-1, width), (21, 0))
+
+    def quarters(grad):
+        return grad.reshape(2 * n_sp, 2, 2, shard_rows // 4, grad.shape[1])
+
+    ff_low = fed.f_out.reshape(2, 2, 5, ff_here // 10, width)
+    ff_got = swap_blk(ff_low[:, 1])
+
+    ended = back(**dict(
+            ckv=quarters(jnp.concatenate([last.ck, last.cv], 1)),
+            cq=quarters(last.cq),
+            co=quarters(last.co),
+            o=quarters(last.o),
+            fi=ff_low[0, 0],
+            fo=ff_low[1, 0],
+            fi_rx=ff_got[0],
+            fo_rx=ff_got[1],
+            d_att=last.d_att,
+            text=last.text_part.reshape(2, n_sp, -1, width),
+            q=q_flat,
+            kv=kv_flat,
+            lse=lse_wide,
+            w=qkv_mine,
+            h1=h1_all,
+            lin=lin_parts,
+            rho=rho,
+            trig=trig,
+            par=params,
+            x=x_own,
+            dx1=last.dx,
+            time=time_embed[0],
+            small_in=small,
+        )
+    )
+    small = ended.small_out
     spot = spot_b * n_sp + spot_s
     small_own = lax.dynamic_slice_in_dim(small[:21], spot * lanes_here, lanes_here, 1)
     part_bias = lax.dynamic_slice_in_dim(small[21:].reshape(-1), own_at, ff_here, 0)
+
+    def whole(name, rows):
+        return getattr(ended, name + "_out").reshape(rows, -1).astype(F32)
+
     return (
         block_out,
-        grad_tokens[None],
-        grad_text[None],
+        ended.tokens_out[None],
+        ended.text_out,
         small_own[:6],
         small_own[6:11],
         small_own[11:21],
-        part_sqkv,
-        spread_weight(g_out_self),
-        jnp.concatenate([spread_weight(g_q_cross), spread_weight(g_kv_cross)], 1),
-        spread_weight(g_out_cross),
-        ff_final[0],
-        ff_final[1],
+        whole("s", shard_rows),
+        whole("o", shard_rows),
+        jnp.concatenate(
+            [
+                whole("cq", shard_rows),
+                whole("ckv", shard_rows),
+            ],
+            1,
+        ),
+        whole("co", shard_rows),
+        whole("fi", ff_here),
+        whole("fo", ff_here),
         part_bias,
     )
 
@@ -1316,37 +2270,37 @@
         local,
         mesh=mesh,
         in_specs=(
-            P("dp", ("blk", "sp"), None),
-            P("dp", ("blk", "sp"), None),
-            P("dp"),
-            P("dp", None, ("blk", "sp")),
-            P("dp", None, None),
-            P(None, ("blk", "sp")),
-            P(None, ("blk", "sp")),
-            P(None, ("blk", "sp")),
-            P(("blk", "sp"), None),
-            P(("blk", "sp"), None),
-            P(("blk", "sp"), None),
-            P(("blk", "sp"), None),
-            P(("blk", "sp"), None),
-            P(("blk", "sp"), None),
-            P(("blk", "sp")),
-            P("dp", ("blk", "sp"), None),
+            P(DP, (BLK, SP), None),
+            P(DP, (BLK, SP), None),
+            P(DP),
+            P(DP, None, (BLK, SP)),
+            P(DP, None, None),
+            P(None, (BLK, SP)),
+            P(None, (BLK, SP)),
+            P(None, (BLK, SP)),
+            P((BLK, SP), None),
+            P((BLK, SP), None),
+            P((BLK, SP), None),
+            P((BLK, SP), None),
+            P((BLK, SP), None),
+            P((BLK, SP), None),
+            P((BLK, SP)),
+            P(DP, (BLK, SP), None),
         ),
         out_specs=(
-            P("dp", ("blk", "sp"), None),
-            P("dp", ("blk", "sp"), None),
-            P("dp", ("blk", "sp"), None),
-            P(None, ("blk", "sp")),
-            P(None, ("blk", "sp")),
-            P(None, ("blk", "sp")),
-            P(("blk", "sp"), None),
-            P(("blk", "sp"), None),
-            P(("blk", "sp"), None),
-            P(("blk", "sp"), None),
-            P(("blk", "sp"), None),
-            P(("blk", "sp"), None),
-            P(("blk", "sp")),
+            P(DP, (BLK, SP), None),
+            P(DP, (BLK, SP), None),
+            P(DP, (BLK, SP), None),
+            P(None, (BLK, SP)),
+            P(None, (BLK, SP)),
+            P(None, (BLK, SP)),
+            P((BLK, SP), None),
+            P((BLK, SP), None),
+            P((BLK, SP), None),
+            P((BLK, SP), None),
+            P((BLK, SP), None),
+            P((BLK, SP), None),
+            P((BLK, SP)),
         ),
         check_vma=False,
     )

time: 1170 us -> 821 us (0.70)
  Pallas kernels: 278 us -> 719 us
  matrix products: 245 us -> 0 us
  waiting for transfers between devices: 240 us -> 12.2 us
  local copies, waits for them, and re-layouts: 167 us -> 28 us
  other arithmetic: 146 us -> 32.4 us
  starting transfers between devices: 58 us -> 0.36 us
    pallas_call x0 -> x4, Pallas kernels: none -> 477 us  [the longest x1 293 us: back(): pl.pallas_call(functools.partial(back_kernel, n_sp, n_dp, names), out_sha...]
    dot_general x51 -> x0, matrix products: 239 us -> none  [the longest x13 68 us: dot_t(): return jnp.einsum('te,de->td', a, b, preferred_element_type=F32)]
    ppermute x43 -> x2, waiting for transfers between devices: 201 us -> 12.2 us  [swap_blk(): return lax.ppermute(value, BLK, [(0, 1), (1, 0)])]
    convert_element_type x24 -> x5, other arithmetic: 78.6 us -> 14.3 us  [whole(): return getattr(ended, name + '_out').reshape(rows, -1).astype(F32)]
    ppermute x43 -> x2, starting transfers between devices: 47.2 us -> 0.32 us  [swap_blk(): return lax.ppermute(value, BLK, [(0, 1), (1, 0)])]
    unnamed x397 -> x33, local copies, waits for them, and re-layouts: 49.1 us -> 4.51 us
    reduce_scatter x6 -> x1, waiting for transfers between devices: 39.3 us -> 0.01 us  [local(): lax.psum_scatter(fed.z_out, SP, scatter_dimension=0, tiled=False)]
    pallas_call x1, Pallas kernels: 278 us -> 242 us  [front(): pl.pallas_call(functools.partial(front_kernel, n_sp), out_shape=outs, in_...]
  transfers between devices with their start and end apart: 51 -> 3, of which waited for: 16 -> 1; matrix products, arithmetic and copies ran while one was open for 40% -> 4% of each run, Pallas kernels for 0% -> 39%
where the time goes in v2:
time: 821 us; the launch traced here: 807 us
  Pallas kernels  719 us (88%)
  other arithmetic  32.4 us (4%)
  local copies, waits for them, and re-layouts  28 us (3%)
  between operations  15.4 us (2%)
  waiting for transfers between devices  12.2 us (1%)
    pallas_call x1, Pallas kernels, back(): pl.pallas_call(functools.partial(back_kernel, n_sp, n_dp, names), out_sha...  293 us
    pallas_call x1, Pallas kernels, front(): pl.pallas_call(functools.partial(front_kernel, n_sp), out_shape=outs, in_...  242 us
    pallas_call x1, Pallas kernels, feed(): pl.pallas_call(functools.partial(feed_kernel, n_sp, names), out_shape=tup...  109 us
    pallas_call x1, Pallas kernels, own_back(): pl.pallas_call(functools.partial(own_back_kernel, names), out_shape=tuple...  48.8 us
    pallas_call x1, Pallas kernels, own_tokens(): pl.pallas_call(own_kernel, out_shape=outs, in_specs=[pl.BlockSpec(memory_...  26.2 us
  transfers between devices with their start and end apart: 3, of which 1 were waited for; matrix products, arithmetic and copies ran while one was open for 4% of the time, Pallas kernels for 39%

profile of v2, /device:TPU:27, one launch (start us, length us, event | category | flops | bytes accessed | tf_op | source)
XLA Modules:
  0.0 807.1 jit_solution(2973127842320298922)
XLA Ops:
  9.0 3.6 pad_maximum_fusion.1.rest_ref
  14.4 242.1 %shard_map.264 = (f32[32,1536]{1,0:T(8,128)}, bf16[1024,1536]{1,0:T(8,128)(2,1)}, bf16[1536,1152]{1,0:T(8,128)(2,1)}, f32[2,1024,384]{2,1,0:T(8,128)}, f32[2,102...) custom-call(bf16[256,1536]{1,0:T(8,128)(2,1)} %bitcast.54, ...), custom_call_target="tpu_custom_call" | custom-call | tf_op jit(solution)/shard_map/pallas_call | solution.py:789
  256.5 26.2 %shard_map.265 = (f32[256,1536]{1,0:T(8,128)}, f32[256,1536]{1,0:T(8,128)}, bf16[256,1536]{1,0:T(8,128)(2,1)}, f32[256,1536]{1,0:T(8,128)}, f32[512,1536]{1,0:T(...) custom-call(s32[1]{0:T(128)S(6)} %copy.44.len_ref.refs_0_, ...), custom_call_target="tpu_custom_call" | custom-call | tf_op jit(solution)/shard_map/pallas_call | solution.py:955
  283.5 108.5 %shard_map.266 = (bf16[4,256,1536]{2,1,0:T(8,128)(2,1)}, bf16[2,2,560,1536]{3,2,1,0:T(8,128)(2,1)}, f32[256,1536]{1,0:T(8,128)}, f32[1,2240]{1,0:T(1,128)}) custom-call(bf16[1120,1536]{1,0:T(8,128)(2,1)} %refs_0_.2, bf16[1120,1536]{1,0:T(8,128)(2,1)} %get-tuple-element.67.refs_1_, bf16[1120,1536]{1,0:T(8,128)(2,1)} %refs_2_.1, ...), custom_call_target="tpu_custom_call" | custom-call | tf_op jit(solution)/shard_map/pallas_call | solution.py:1371
  392.0 3.6 copy.31
  395.6 2.2 slice_bitcast_fusion
  397.8 1.7 copy-done
  401.9 48.8 %shard_map.267 = (bf16[1536,1536]{1,0:T(8,128)(2,1)}, bf16[1536,1536]{1,0:T(8,128)(2,1)}, bf16[1536,1536]{1,0:T(8,128)(2,1)}, bf16[1536,1536]{1,0:T(8,128)(2,1)}...) custom-call(s32[1]{0:T(128)S(6)} %copy.44.len_ref.refs_0_, ...), custom_call_target="tpu_custom_call" | custom-call | tf_op jit(solution)/shard_map/pallas_call | solution.py:1112
  450.8 4.2 slice_bitcast_fusion.3
  454.9 7.0 pad_maximum_fusion
  461.9 12.1 %collective-permute-done.1 = bf16[2,5,112,1536]{3,2,1,0:T(8,128)(2,1)} collective-permute-done((bf16[2,5,112,1536]{3,2,1,0:T(8,128)(2,1)}, bf16[2,5,112,1536]{3,2,1,0:T(8,128)(2,1)}, u32[]{:S(2)}, u32[]{:S(2)}) %collective-permute-start.1) | collective-permute-done | bytes 3440672 | tf_op jit(solution)/shard_map/ppermute | solution.py:2063
  474.1 4.0 slice_bitcast_fusion.1
  478.1 2.4 fusion.4
  480.5 1.4 dynamic_update_slice.12
  481.9 1.5 dynamic_update_slice.15.refs_22_
  483.4 293.1 %shard_map.268 = (bf16[8,2,48,3072]{3,2,1,0:T(8,128)(2,1)}, bf16[8,2,48,3072]{3,2,1,0:T(8,128)(2,1)}, bf16[8,48,3072]{2,1,0:T(8,128)(2,1)}, bf16[8,48,3072]{2,1,...) custom-call(bf16[8,2,2,48,3072]{4,3,2,1,0:T(8,128)(2,1)} %bitcast.49, ...), custom_call_target="tpu_custom_call" | custom-call | tf_op jit(solution)/shard_map/pallas_call | solution.py:2049
  776.5 0.9 slice.65
  780.4 3.8 bitcast_convert_fusion.2
  784.1 1.2 bitcast_convert_fusion.4
  785.3 1.2 bitcast_convert_fusion.3
  786.7 4.1 bitcast_convert_fusion.1
  790.8 4.1 bitcast_convert_fusion
  795.0 2.2 maximum_convert_fusion
  797.8 1.1 copy.45
  (56 shorter events, 10.8 us)
Async XLA Ops:
  7.2 470.9 %reduce-scatter.2.cloned.1.call-start = ((), (), s32[]{:S(2)}) async-start(), calls=%async_computation.1 | async-start | bytes 3932160 | tf_op jit(solution)/shard_map/reduce_scatter | solution.py:2166
  7.2 275.5 %collective-permute-start = (bf16[1120]{0:T(1024)(128)(2,1)}, bf16[1120]{0:T(1024)(128)(2,1)S(1)}, u32[]{:S(2)}, u32[]{:S(2)}) collective-permute-start(bf16[1120]{0:T(1024)(128)(2,1)} %param.31), channel_id=1, source_target_pairs={{0,4},{4,0},{1,5},{5,1},{2,6},{6,2},{3,7},{7,3},{8,12},{12,8},{9,1... | collective-permute-start | bytes 6728 | tf_op jit(solution)/shard_map/ppermute | solution.py:2063
  9.0 4.2 copy-start.12
  256.5 26.3 %copy-start.14 = (bf16[1120]{0:T(1024)(128)(2,1)S(1)}, bf16[1120]{0:T(1024)(128)(2,1)}, u32[]{:S(2)}) copy-start(bf16[1120]{0:T(1024)(128)(2,1)} %param.31) | copy-start | bytes 6724
  395.6 3.9 copy-start
  395.6 5.6 copy-start.13
  399.5 74.6 %collective-permute-start.1 = (bf16[2,5,112,1536]{3,2,1,0:T(8,128)(2,1)}, bf16[2,5,112,1536]{3,2,1,0:T(8,128)(2,1)}, u32[]{:S(2)}, u32[]{:S(2)}) collective-permute-start(bf16[2,5,112,1536]{3,2,1,0:T(8,128)(2,1)} %slice_bitcast_fusion), channel_id=1, source_target_pairs={{0,4},{4,0},{1,5},{5,1},{2,6},{6,2},{3,7},{7,3},{8,12},{12,8},{9,1... | collective-permute-start | bytes 10321928 | tf_op jit(solution)/shard_map/ppermute | solution.py:2063
  450.8 4.2 copy-start.3
  461.9 16.1 %copy-start.1 = (bf16[1,256,1536]{2,1,0:T(8,128)(2,1)S(1)}, bf16[1,256,1536]{2,1,0:T(8,128)(2,1)}, u32[]{:S(2)}) copy-start(bf16[1,256,1536]{2,1,0:T(8,128)(2,1)} %param.32) | copy-start | bytes 2359300
  461.9 16.1 %copy-start.2 = (f32[256,1536]{1,0:T(8,128)S(1)}, f32[256,1536]{1,0:T(8,128)}, u32[]{:S(2)}) copy-start(f32[256,1536]{1,0:T(8,128)} %get-tuple-element.66.refs_2_) | copy-start | bytes 4718596
  780.4 3.8 copy-start.9
  780.4 5.0 copy-start.8
  784.1 2.6 copy-start.5
  786.7 4.1 copy-start.4
  790.8 4.1 copy-start.7
  790.8 4.1 copy-start.10
  794.9 2.9 copy-start.6
  797.1 1.8 copy-start.11
Sparse Core Ops, SparseCore 0:
  392.1 60.2 reduce-scatter.1

commit v3 on v2

--- a/solution.py
+++ b/solution.py
@@ -143,6 +143,7 @@
     out_out,
     text_out,
     cot_out,
+    small_out,
     xall_ref,
     sall_ref,
     w_ref,
@@ -620,6 +621,7 @@
     rest_from_blk(2)
     cot_step(0)
     saves = [
+        pltpu.make_async_copy(sall_ref, small_out, out.at[12]),
         pltpu.make_async_copy(h1_ref, h1_out, out.at[0]),
         pltpu.make_async_copy(lin_ref, lin_out, out.at[1]),
         pltpu.make_async_copy(rho_ref, rho_out, out.at[2]),
@@ -763,7 +765,7 @@
     line = n_sp - 1
     counts = [6, 4 * line, 4 * line, line, line, 3 * line, 3 * line, n_sp, n_sp]
     counts += [2 * n_sp - 1, 2 * n_sp - 1, n_sp, n_sp, 2 * n_sp, 2 * n_sp, line, line]
-    counts += [line, line, 12]
+    counts += [line, line, 13]
     counts += [2 * line, 2 * line, n_sp, n_sp, groups, groups, 2 * groups, 2 * groups, 4, 4]
     counts += [2 * line, 2 * line, n_sp, n_sp, 2 * line, 2 * line]
     shape = jax.ShapeDtypeStruct
@@ -784,6 +786,7 @@
         shape(shard_out.shape, BF),
         shape((groups * text.shape[0], width), BF),
         shape((total, width), BF),
+        shape((groups,) + small_own.shape, BF),
     )
     vmem = pltpu.VMEM
     return pl.pallas_call(
@@ -991,7 +994,7 @@
 
     saves = []
 
-    def weight_grad(name, left, right):
+    def weight_grad(name, left, right, column=0):
         stage = ref.stage
         tile = 384
         for k, start in enumerate(range(0, width, tile)):
@@ -1000,7 +1003,9 @@
                 saves[-2].wait()
             stage[slot] = mm_first(left[:, start : start + tile], right[...]).astype(BF)
             copy = pltpu.make_async_copy(
-                stage.at[slot], getattr(ref, name).at[pl.ds(start, tile)], out_sem.at[slot]
+                stage.at[slot],
+                getattr(ref, name).at[pl.ds(start, tile), pl.ds(column, width)],
+                out_sem.at[slot],
             )
             copy.start()
             saves.append(copy)
@@ -1065,8 +1070,8 @@
     vlow_ref[...] = dkv_ref[1].astype(BF)
     sums[16:17, :] = column_total(klow_ref[...])
     sums[17:18, :] = column_total(vlow_ref[...])
-    weight_grad("ck", ref.text_in, klow_ref)
-    weight_grad("cv", ref.text_in, vlow_ref)
+    weight_grad("ckv", ref.text_in, klow_ref)
+    weight_grad("ckv", ref.text_in, vlow_ref, width)
     loads[3].wait()
     wide_dot_t(dkv_ref.at[0], klow_ref[...], w_c)
     loads[4].wait()
@@ -1083,7 +1088,8 @@
     in_any = ["rest"]
     ins = ["x_two", "x_one", "d_rows", "cot", "time", "par", "a", "cin", "ql", "kl", "q", "kv"]
     ins += ["lse", "oc", "att", "text_in"]
-    any_outs = {name: shape((width, width), BF) for name in ("o", "co", "cq", "ck", "cv")}
+    any_outs = {name: shape((width, width), BF) for name in ("o", "co", "cq")}
+    any_outs.update(ckv=shape((width, 2 * width), BF))
     outs = dict(
         d_att=shape((rows, width), BF),
         dx=shape((rows, width), F32),
@@ -1300,7 +1306,7 @@
                 low_ref[which, part, k * chunk : (k + 1) * chunk] = value.astype(BF)
             copy = pltpu.make_async_copy(
                 low_ref.at[which, part],
-                ref.f_out.at[which, part],
+                (ref.fi_own, ref.fi_far, ref.fo_own, ref.fo_far)[2 * which + part],
                 saves_sem.at[2 * which + part],
             )
             copy.start()
@@ -1339,7 +1345,10 @@
     ins = ["cot", "bias", "time", "par"]
     any_outs = dict(
         z_out=shape((n_sp, rows, width), BF),
-        f_out=shape((2, 2, hidden // 2, width), BF),
+        fi_own=shape((hidden // 2, width), BF),
+        fi_far=shape((hidden // 2, width), BF),
+        fo_own=shape((hidden // 2, width), BF),
+        fo_far=shape((hidden // 2, width), BF),
     )
     outs = {"d_rows": shape((rows, width), F32), "du_sums": shape((1, 2 * hidden), F32)}
     vmem = pltpu.VMEM
@@ -1572,11 +1581,9 @@
                 dkv_ref[0, :, head] += mm_first(d_scores, query) * score_scale
             return carry
 
-        for name in ("fi", "fo"):
-            add_blocks(getattr(ref, name + "_kx"), [getattr(ref, name), getattr(ref, name + "_rx")])
-            if name == "fi":
-                goal = lambda: ref.fi_ry.at[0]
-                hop[name] = send(ref.fi_kx, goal(), pair_id, goal)
+        add_blocks(ref.fi_kx, [ref.fi, ref.fi_rx])
+        goal = lambda: ref.fi_ry.at[0]
+        hop["fi"] = send(ref.fi_kx, goal(), pair_id, goal)
         for copy in loads:
             copy.wait()
         do_own.wait()
@@ -1595,11 +1602,14 @@
             goal = lambda name=name: getattr(ref, name + "_rc")
             hop[name] = send(getattr(ref, name).at[:, 1 - core], goal(), core_id, goal)
         lax.fori_loop(1, 2, attend, 0)
+        core_done("o")
+        hop["o"] = []
+        for step in range(1, n_sp):
+            for half in range(2):
+                goal = lambda step=step, half=half: ref.o_rz.at[step - 1, half]
+                src = ref.o_kc.at[half * n_sp + lax.rem(spot_s + step, n_sp)]
+                hop["o"].append(send(src, goal(), line[step - 1], goal))
         core_done("cq")
-        goal = lambda: ref.cq_rx
-        hop["cq"] = send(
-            ref.cq_kc.at[pl.ds((1 - spot_b) * n_sp, n_sp)], goal(), blk_id, goal
-        )
         lax.fori_loop(2, n_sp, attend, 0)
 
     pl.run_scoped(
@@ -1615,7 +1625,6 @@
         place = pl.ds(which * cols, cols)
         proj_ref[:, place] = dkv_ref[which, total_rows:, :].astype(BF)
         kv_away.append(send(proj_ref.at[:, place], kv_recv.at[which], blk_id))
-    core_done("o")
     hop["text"].wait_recv()
     text_kx = ref.text_kx
     add_blocks(text_kx, [ref.text.at[spot_b], ref.text_rx])
@@ -1667,14 +1676,25 @@
             getattr(ref, name + "_kc").at[pl.ds((1 - spot_b) * n_sp, n_sp)], getattr(ref, name + "_rx"), blk_id
         )
 
-    first_blk_send("o")
-    first_blk_done("cq")
-    hop["fo"] = send(ref.fo_kx, ref.fo_ry.at[0], pair_id)
+    first_blk_send("cq")
+    early, late = pl.ds(0, 2), pl.ds(2, 3)
+    hop["fo"] = send(ref.fo_far.at[late], ref.fo_rx, blk_id)
+    add_blocks(ref.fo_kx.at[early], [ref.fo.at[early], ref.fo_rx1])
+    fo_early = send(ref.fo_kx.at[early], ref.fo_ry.at[0, early], pair_id)
     lax.fori_loop(0, n_sp, functools.partial(unturn, 1), 0)
     sums_away = [
         send(sums_ref.at[spot_s], sums_ref.at[spot_s], line[k]) for k in range(n_sp - 1)
     ]
     then_pair_done("co")
+    for copy in hop["o"]:
+        copy.wait_recv()
+    for half in range(2):
+        add_blocks(
+            ref.o_kl.at[half],
+            [ref.o_kc.at[half * n_sp + spot_s]]
+            + [ref.o_rz.at[k, half] for k in range(n_sp - 1)],
+        )
+    hop["o"] = send(ref.o_kl.at[1 - spot_b], ref.o_rx, blk_id)
     for copy in sums_away:
         copy.wait_recv()
     means = sums_ref[0]
@@ -1684,6 +1704,8 @@
     small_ref = ref.small
     own = lanes_at(spot_s * cols, cols)
     small_ref[0] = ref.small_in[...]
+    small_ref[0, 5:6, :] = ref.gate2[...]
+    small_ref[0, 21 : 21 + ref.hidden_rows.shape[0], :] = ref.hidden_rows[...]
     for row in (6, 7, 11, 12, 13):
         small_ref[0, row : row + 1, :] = jnp.zeros((1, width), F32)
 
@@ -1825,9 +1847,15 @@
     hop["s"].wait_recv()
     add_blocks(ref.s_kc, [ref.sw.at[:, core], ref.s_rc])
     hop["s"] = send(ref.s_kc.at[pl.ds((1 - spot_b) * n_sp, n_sp)], ref.s_rx, blk_id)
-    first_blk_done("o")
+    hop["o"].wait_recv()
+    add_blocks(ref.o_kx, [ref.o_kl.at[spot_b], ref.o_rx])
+    hop["o"] = send(ref.o_kx.at[1 - pair], ref.o_ry, pair_id)
+    first_blk_done("cq")
     for k in range(2, n_sp - 1):
         chain_step(k)
+    hop["fo"].wait_recv()
+    add_blocks(ref.fo_kx.at[late], [ref.fo.at[late], ref.fo_rx])
+    hop["fo"] = send(ref.fo_kx.at[late], ref.fo_ry.at[0, late], pair_id)
     then_pair_done("cq")
     for copy in hop["text"]:
         copy.wait_recv()
@@ -1900,17 +1928,20 @@
                     line[step - 1],
                 )
             )
-    then_pair_done("o")
-
     def line_done(name):
-        for copy in hop[name]:
-            copy.wait_recv()
-        kx, rz = getattr(ref, name + "_kx"), getattr(ref, name + "_rz")
+        if name == "o":
+            hop[name].wait_recv()
+        else:
+            for copy in hop[name]:
+                copy.wait_recv()
+        kx = getattr(ref, name + "_kx")
         out = getattr(ref, name + "_out").at[core]
         kz = getattr(ref, name + "_kz")
-        add_blocks(
-            kz.at[0], [kx.at[spot_s]] + [rz.at[k] for k in range(n_sp - 1)]
-        )
+        if name == "o":
+            add_blocks(kz.at[0], [kx.at[pair], ref.o_ry])
+        else:
+            rz = getattr(ref, name + "_rz")
+            add_blocks(kz.at[0], [kx.at[spot_s]] + [rz.at[k] for k in range(n_sp - 1)])
         for k, bit in enumerate(bits):
             got = getattr(ref, name + "_rw").at[k]
             send(kz.at[k], got, dp_id(bit)).wait_recv()
@@ -1927,6 +1958,7 @@
         hop[name] = send(out, out, core_id)
 
     small_done(1)
+    line_done("o")
     line_done("co")
     for k in range(2, len(partners) - 2):
         small_done(k)
@@ -1937,12 +1969,13 @@
         copy.wait_recv()
     hop["s"] = send(ref.s_z, ref.s_ry.at[0], pair_id)
     small_done(len(partners) - 2)
+    pair_back("o")
+    pair_back("co")
     line_done("ckv")
+    fo_early.wait_recv()
     ff_last("fo")
     small_done(len(partners) - 1)
-    pair_back("co")
     pair_back("cq")
-    line_done("o")
     hop["s"].wait_recv()
     s_ry, s_out = ref.s_ry, ref.s_out
     for k in range(len(bits) + 1):
@@ -1953,7 +1986,6 @@
             send(goal, s_ry.at[k + 1], dp_id(bits[k])).wait_recv()
     hop["s"] = send(s_out.at[core], s_out.at[core], core_id)
     pair_back("ckv")
-    pair_back("o")
     for name in ("ckv", "co", "cq", "o", "fi", "fo", "s"):
         hop[name].wait_recv()
     for copy in sent:
@@ -1979,14 +2011,19 @@
     cols = arrays.q.shape[1]
     g8 = 2 * n_sp
     more = max(n_dp.bit_length() - 3, 0)
-    any_names = ["ckv", "cq", "co", "o", "fi", "fo", "fi_rx", "fo_rx", "d_att", "text", "q", "kv", "lse", "w", "h1"]
-    vmem_names = ["lin", "rho", "trig", "par", "x", "dx1", "time", "small_in"]
+    any_names = ["ckv", "cq", "co", "o", "fi", "fo", "fi_rx", "fo_rx1", "fo_far", "d_att", "text", "q", "kv", "lse", "w", "h1"]
+    vmem_names = ["lin", "rho", "trig", "par", "x", "dx1", "time", "small_in", "gate2", "hidden_rows"]
     outs = {}
     for name in ("ckv", "cq", "co", "o"):
         quarter, lanes = getattr(arrays, name).shape[3:]
         outs[name + "_rc"] = shape((g8, 2, quarter, lanes), BF)
         outs[name + "_kc"] = shape((g8, 2, quarter, lanes), BF)
-        if name == "ckv":
+        if name == "o":
+            outs[name + "_rz"] = shape((n_sp - 1, 2, 2, quarter, lanes), BF)
+            outs[name + "_kl"] = shape((2, 2, quarter, lanes), BF)
+            outs[name + "_rx"] = shape((2, quarter, lanes), BF)
+            outs[name + "_ry"] = shape((quarter, lanes), BF)
+        elif name == "ckv":
             outs[name + "_ry"] = shape((g8, quarter, lanes), BF)
             outs[name + "_ky"] = shape((g8, quarter, lanes), BF)
             outs[name + "_rx"] = shape((n_sp, quarter, lanes), BF)
@@ -1994,8 +2031,9 @@
             outs[name + "_rx"] = shape((n_sp, 2, quarter, lanes), BF)
             outs[name + "_ky"] = shape((n_sp, 2, quarter, lanes), BF)
             outs[name + "_ry"] = shape((n_sp, quarter, lanes), BF)
-        outs[name + "_kx"] = shape((n_sp, quarter, lanes), BF)
-        outs[name + "_rz"] = shape((n_sp - 1, quarter, lanes), BF)
+        outs[name + "_kx"] = shape((2 if name == "o" else n_sp, quarter, lanes), BF)
+        if name != "o":
+            outs[name + "_rz"] = shape((n_sp - 1, quarter, lanes), BF)
         outs[name + "_kz"] = shape((more + 1, quarter, lanes), BF)
         outs[name + "_rw"] = shape((more + 1, quarter, lanes), BF)
         outs[name + "_out"] = shape((2, 2, quarter, lanes), BF)
@@ -2005,6 +2043,7 @@
         outs[name + "_ry"] = shape((more + 1,) + half, BF)
         outs[name + "_ky"] = shape((more + 1,) + half, BF)
         outs[name + "_out"] = shape((2,) + half, BF)
+    outs.update(fo_rx=shape((3,) + arrays.fo.shape[1:], BF))
     text_rows = arrays.text.shape[2]
     outs.update(text_rx=shape((n_sp, text_rows, width), BF))
     outs.update(text_kx=shape((n_sp, text_rows, width), BF))
@@ -2102,9 +2141,10 @@
             jnp.pad(
                 positions[0].astype(BF), ((0, 13), (0, SMALL_LANES - positions.shape[2]))
             ),
+            jnp.pad(small_rows, ((0, 0), (0, SMALL_LANES - lanes_here))),
             jnp.pad(
-                small_rows, ((0, PARAM_ROWS - 21), (0, SMALL_LANES - lanes_here))
-            ),
+                ffn_bias, (0, (PARAM_ROWS - 21) * SMALL_LANES - ffn_bias.shape[0])
+            ).reshape(-1, SMALL_LANES),
         ],
         0,
     )
@@ -2125,6 +2165,7 @@
         out_other,
         text_every,
         cot_every,
+        small_every,
     ) = front(
         x_own,
         small_own,
@@ -2140,8 +2181,15 @@
     gain_all = params[6:11]
     bias_all = params[11:21]
     ff_here = ffn_in.shape[0]
-    bias_own = ffn_bias.astype(F32)
-    bias_ff = jnp.concatenate([bias_own, swap_blk(ffn_bias).astype(F32)])
+    bias_rows = small_every.reshape(2, n_sp, SMALL_ROWS, SMALL_LANES)
+    bias_rows = lax.dynamic_index_in_dim(bias_rows, spot_s, 1, keepdims=False)[:, 37:]
+    bias_rows = bias_rows.reshape(2, -1)[:, :ff_here].astype(F32)
+    bias_ff = jnp.where(
+        spot_b == 0,
+        jnp.concatenate([bias_rows[0], bias_rows[1]]),
+        jnp.concatenate([bias_rows[1], bias_rows[0]]),
+    )
+
     own = own_tokens(
         text_lengths, rest_all, x_own, att_tok, text_every, time_embed[0], params
     )
@@ -2198,25 +2246,22 @@
     far_at = ((1 - spot_b) * n_sp + spot_s) * ff_here
     ff_row = lax.dynamic_update_slice_in_dim(ff_row, du_sums[:ff_here], own_at, 0)
     ff_row = lax.dynamic_update_slice_in_dim(ff_row, du_sums[ff_here:], far_at, 0)
-    small = last.sums
-    small = lax.dynamic_update_slice(small, d_gate2[None], (5, 0))
-    small = lax.dynamic_update_slice(small, ff_row.reshape(-1, width), (21, 0))
-
     def quarters(grad):
         return grad.reshape(2 * n_sp, 2, 2, shard_rows // 4, grad.shape[1])
 
-    ff_low = fed.f_out.reshape(2, 2, 5, ff_here // 10, width)
-    ff_got = swap_blk(ff_low[:, 1])
+    def chunks(grad):
+        return grad.reshape(5, ff_here // 10, width)
 
     ended = back(**dict(
-            ckv=quarters(jnp.concatenate([last.ck, last.cv], 1)),
+            ckv=quarters(last.ckv),
             cq=quarters(last.cq),
             co=quarters(last.co),
             o=quarters(last.o),
-            fi=ff_low[0, 0],
-            fo=ff_low[1, 0],
-            fi_rx=ff_got[0],
-            fo_rx=ff_got[1],
+            fi=chunks(fed.fi_own),
+            fo=chunks(fed.fo_own),
+            fi_rx=chunks(swap_blk(fed.fi_far)),
+            fo_rx1=swap_blk(fed.fo_far[: ff_here // 5]).reshape(2, -1, width),
+            fo_far=chunks(fed.fo_far),
             d_att=last.d_att,
             text=last.text_part.reshape(2, n_sp, -1, width),
             q=q_flat,
@@ -2231,7 +2276,9 @@
             x=x_own,
             dx1=last.dx,
             time=time_embed[0],
-            small_in=small,
+            small_in=last.sums,
+            gate2=d_gate2[None],
+            hidden_rows=ff_row.reshape(-1, width),
         )
     )
     small = ended.small_out

time: 821 us -> 792 us (0.965)
  local copies, waits for them, and re-layouts: 28 us -> 15.8 us
  Pallas kernels: 719 us -> 709 us
    ppermute x2, waiting for transfers between devices: 12.2 us -> 0.01 us  [swap_blk(): return lax.ppermute(value, BLK, [(0, 1), (1, 0)])]
    squeeze x3 -> x1, local copies, waits for them, and re-layouts: 10.3 us -> 0.81 us  [local(): lax.dynamic_index_in_dim(bias_rows, spot_s, 1, keepdims=False)[:, 37:]]
  transfers between devices with their start and end apart: 3 -> 3, of which waited for: 1 -> 1; matrix products, arithmetic and copies ran while one was open for 4% -> 1% of each run, Pallas kernels for 39% -> 6%
where the time goes in v3:
time: 792 us; the launch traced here: 776 us
  Pallas kernels  709 us (90%)
  other arithmetic  24.8 us (3%)
  local copies, waits for them, and re-layouts  15.8 us (2%)
  between operations  15.3 us (2%)
    pallas_call x1, Pallas kernels, back(): pl.pallas_call(functools.partial(back_kernel, n_sp, n_dp, names), out_sha...  285 us
    pallas_call x1, Pallas kernels, front(): pl.pallas_call(functools.partial(front_kernel, n_sp), out_shape=outs, in_...  241 us
    pallas_call x1, Pallas kernels, feed(): pl.pallas_call(functools.partial(feed_kernel, n_sp, names), out_shape=tup...  108 us
    pallas_call x1, Pallas kernels, own_back(): pl.pallas_call(functools.partial(own_back_kernel, names), out_shape=tuple...  49.6 us
    pallas_call x1, Pallas kernels, own_tokens(): pl.pallas_call(own_kernel, out_shape=outs, in_specs=[pl.BlockSpec(memory_...  26.2 us
  transfers between devices with their start and end apart: 3, of which 1 were waited for; matrix products, arithmetic and copies ran while one was open for 1% of the time, Pallas kernels for 6%

profile of v3, /device:TPU:27, one launch (start us, length us, event | category | flops | bytes accessed | tf_op | source)
XLA Modules:
  0.0 776.5 jit_solution(4410116561574079653)
XLA Ops:
  8.6 1.4 copy.38
  12.0 3.6 pad_maximum_fusion.rest_ref
  15.6 240.8 %shard_map.264 = (f32[32,1536]{1,0:T(8,128)}, bf16[1024,1536]{1,0:T(8,128)(2,1)}, bf16[1536,1152]{1,0:T(8,128)(2,1)}, f32[2,1024,384]{2,1,0:T(8,128)}, f32[2,102...) custom-call(bf16[256,1536]{1,0:T(8,128)(2,1)} %bitcast.52, ...), custom_call_target="tpu_custom_call" | custom-call | tf_op jit(solution)/shard_map/pallas_call | solution.py:792
  256.4 0.8 dynamic-slice_bitcast_fusion
  258.0 26.2 %shard_map.265 = (f32[256,1536]{1,0:T(8,128)}, f32[256,1536]{1,0:T(8,128)}, bf16[256,1536]{1,0:T(8,128)(2,1)}, f32[256,1536]{1,0:T(8,128)}, f32[512,1536]{1,0:T(...) custom-call(s32[1]{0:T(128)S(6)} %copy.43.len_ref.refs_0_, ...), custom_call_target="tpu_custom_call" | custom-call | tf_op jit(solution)/shard_map/pallas_call | solution.py:958
  284.3 107.7 %shard_map.266 = (bf16[4,256,1536]{2,1,0:T(8,128)(2,1)}, bf16[560,1536]{1,0:T(8,128)(2,1)}, bf16[560,1536]{1,0:T(8,128)(2,1)}, bf16[560,1536]{1,0:T(8,128)(2,1)}...) custom-call(bf16[1120,1536]{1,0:T(8,128)(2,1)} %refs_0_.2, ...), custom_call_target="tpu_custom_call" | custom-call | tf_op jit(solution)/shard_map/pallas_call | solution.py:1380
  392.0 6.3 collective-permute-start
  398.3 1.1 slice.62
  399.5 0.8 slice.55
  401.6 49.6 %shard_map.267 = (bf16[1536,1536]{1,0:T(8,128)(2,1)}, bf16[1536,1536]{1,0:T(8,128)(2,1)}, bf16[1536,1536]{1,0:T(8,128)(2,1)}, bf16[1536,3072]{1,0:T(8,128)(2,1)}...) custom-call(s32[1]{0:T(128)S(6)} %copy.43.len_ref.refs_0_, ...), custom_call_target="tpu_custom_call" | custom-call | tf_op jit(solution)/shard_map/pallas_call | solution.py:1118
  451.3 0.8 slice_reduce_fusion
  452.1 0.8 fusion.14
  452.9 4.6 reduce-scatter.2.cloned.1.call-done
  457.5 2.4 fusion.4
  460.5 285.1 %shard_map.268 = (bf16[8,2,48,3072]{3,2,1,0:T(8,128)(2,1)}, bf16[8,2,48,3072]{3,2,1,0:T(8,128)(2,1)}, bf16[8,48,3072]{2,1,0:T(8,128)(2,1)}, bf16[8,48,3072]{2,1,...) custom-call(bf16[8,2,2,48,3072]{4,3,2,1,0:T(8,128)(2,1)} %bitcast.49, ...), custom_call_target="tpu_custom_call" | custom-call | tf_op jit(solution)/shard_map/pallas_call | solution.py:2088
  745.6 0.9 slice.67
  746.6 0.9 slice.71
  749.5 3.8 bitcast_convert_fusion.2
  753.3 1.8 bitcast_convert_fusion.3
  755.1 2.2 maximum_convert_fusion
  757.3 1.7 copy-done.2
  759.0 7.6 bitcast_convert_fusion
  767.3 1.1 copy.44
  768.4 0.7 copy.45
  (47 shorter events, 8.3 us)
Async XLA Ops:
  7.2 450.3 %reduce-scatter.2.cloned.1.call-start = ((), (), s32[]{:S(2)}) async-start(), calls=%async_computation.1 | async-start | bytes 3932160 | tf_op jit(solution)/shard_map/reduce_scatter | solution.py:2214
  391.9 8.4 %copy-start.10 = (f32[1,2240]{1,0:T(1,128)S(1)}, f32[1,2240]{1,0:T(1,128)}, u32[]{:S(2)}) copy-start(f32[1,2240]{1,0:T(1,128)} %get-tuple-element.106) | copy-start | bytes 26884
  392.0 68.5 %collective-permute-start = (bf16[560,1536]{1,0:T(8,128)(2,1)}, bf16[560,1536]{1,0:T(8,128)(2,1)}, u32[]{:S(2)}, u32[]{:S(2)}) collective-permute-start(bf16[560,1536]{1,0:T(8,128)(2,1)} %get-tuple-element.92), channel_id=1, source_target_pairs={{0,4},{4,0},{1,5},{5,1},{2,6},{6,2},{3,7},{7,3},{8,12},{12,8},{9,1... | collective-permute-start | bytes 5160968 | tf_op jit(solution)/shard_map/ppermute | solution.py:2102
  399.4 61.1 %collective-permute-start.1 = (bf16[224,1536]{1,0:T(8,128)(2,1)S(1)}, bf16[224,1536]{1,0:T(8,128)(2,1)}, u32[]{:S(2)}, u32[]{:S(2)}) collective-permute-start(bf16[224,1536]{1,0:T(8,128)(2,1)S(1)} %slice.62), channel_id=1, source_target_pairs={{0,4},{4,0},{1,5},{5,1},{2,6},{6,2},{3,7},{7,3},{8,12},{12,8},{9,1... | collective-permute-start | bytes 2064392 | tf_op jit(solution)/shard_map/ppermute | solution.py:2102
  401.6 55.9 %copy-start = (bf16[1,256,1536]{2,1,0:T(8,128)(2,1)S(1)}, bf16[1,256,1536]{2,1,0:T(8,128)(2,1)}, u32[]{:S(2)}) copy-start(bf16[1,256,1536]{2,1,0:T(8,128)(2,1)} %param.32) | copy-start | bytes 2359300
  401.6 55.9 %copy-start.1 = (f32[256,1536]{1,0:T(8,128)S(1)}, f32[256,1536]{1,0:T(8,128)}, u32[]{:S(2)}) copy-start(f32[256,1536]{1,0:T(8,128)} %get-tuple-element.69.refs_2_) | copy-start | bytes 4718596
  749.5 3.8 copy-start.6
  749.5 3.8 copy-start.7
  753.3 1.8 copy-start.5
  753.3 1.8 copy-start.8
  753.3 4.0 copy-start.3
  755.1 3.9 copy-start.2
  759.0 8.2 %copy-start.4 = (f32[256,1536]{1,0:T(8,128)S(1)}, f32[256,1536]{1,0:T(8,128)}, u32[]{:S(2)}) copy-start(f32[256,1536]{1,0:T(8,128)} %get-tuple-element.107) | copy-start | bytes 4718596
  766.6 1.8 copy-start.9
Sparse Core Ops, SparseCore 0:
  392.1 65.3 reduce-scatter.1

commit v4 on v3

--- a/solution.py
+++ b/solution.py
@@ -1857,59 +1857,9 @@
     add_blocks(ref.fo_kx.at[late], [ref.fo.at[late], ref.fo_rx])
     hop["fo"] = send(ref.fo_kx.at[late], ref.fo_ry.at[0, late], pair_id)
     then_pair_done("cq")
-    for copy in hop["text"]:
-        copy.wait_recv()
-    add_blocks(
-        ref.text_out.at[0],
-        [text_kx.at[spot_s]] + [ref.text_rz.at[k] for k in range(n_sp - 1)],
-    )
-
-    chain_step(n_sp - 1)
-
-    @pl.when(spot_s > 0)
-    def _():
-        ref.dh1_own[...] += dh1_recv[spot_s].astype(F32)
-
-    @pl.when(spot_s < n_sp - 1)
-    def _():
-        ref.dh1_own[...] += dh1_recv[n_sp].astype(F32)
-
-    d_shift = ref.dh1_own[...]
-    values = ref.x[...].astype(F32)
-    centre = values - jnp.mean(values, axis=-1, keepdims=True)
-    spread = lax.rsqrt(jnp.mean(centre * centre, axis=-1, keepdims=True) + EPS)
-    normed = centre * spread
-    scale = 1.0 + (ref.time[1:2, :] + par_ref[1:2, :])
-    grad = d_shift * scale
-    lean = jnp.mean(grad, axis=-1, keepdims=True)
-    tilt = jnp.mean(grad * normed, axis=-1, keepdims=True)
-    ref.tokens_out[...] = ref.dx1[...] + spread * (grad - lean - normed * tilt)
-    small_ref[0, 0:1, :] = jnp.sum(d_shift, 0, keepdims=True)
-    small_ref[0, 1:2, :] = jnp.sum(d_shift * normed, 0, keepdims=True)
-    partners = [core_id, pair_id] + [dp_id(bit) for bit in bits] + [blk_id]
-    bit = 1
-    while bit < n_sp:
-        partners.append({SP: spot_s + bit - 2 * bit * lax.rem(spot_s // bit, 2)})
-        bit *= 2
-
-    def small_send(k):
-        hop["small"] = send(small_ref.at[k], ref.small_recv.at[k], partners[k])
-
-    def small_done(k):
-        hop["small"].wait_recv()
-        small_ref[k + 1] = small_ref[k] + ref.small_recv[k]
-        if k + 1 < len(partners):
-            small_send(k + 1)
-        else:
-            ref.small_out[...] = small_ref[k + 1]
-
-    small_send(0)
-    blk_done("ckv")
-    line_send("ckv")
     hop["s"].wait_recv()
     own_blk = ref.s_kc.at[pl.ds(spot_b * n_sp, n_sp)]
     add_blocks(ref.s_kx, [own_blk, ref.s_rx])
-    small_done(0)
     s_line = []
     s_keep = []
     for j in range(3):
@@ -1928,6 +1878,7 @@
                     line[step - 1],
                 )
             )
+
     def line_done(name):
         if name == "o":
             hop[name].wait_recv()
@@ -1957,9 +1908,62 @@
         out = getattr(ref, name + "_out").at[core]
         hop[name] = send(out, out, core_id)
 
+    line_done("co")
+    line_done("o")
+    for copy in hop["text"]:
+        copy.wait_recv()
+    add_blocks(
+        ref.text_out.at[0],
+        [text_kx.at[spot_s]] + [ref.text_rz.at[k] for k in range(n_sp - 1)],
+    )
+
+    chain_step(n_sp - 1)
+
+    @pl.when(spot_s > 0)
+    def _():
+        ref.dh1_own[...] += dh1_recv[spot_s].astype(F32)
+
+    @pl.when(spot_s < n_sp - 1)
+    def _():
+        ref.dh1_own[...] += dh1_recv[n_sp].astype(F32)
+
+    d_shift = ref.dh1_own[...]
+    values = ref.x[...].astype(F32)
+    centre = values - jnp.mean(values, axis=-1, keepdims=True)
+    spread = lax.rsqrt(jnp.mean(centre * centre, axis=-1, keepdims=True) + EPS)
+    normed = centre * spread
+    scale = 1.0 + (ref.time[1:2, :] + par_ref[1:2, :])
+    grad = d_shift * scale
+    lean = jnp.mean(grad, axis=-1, keepdims=True)
+    tilt = jnp.mean(grad * normed, axis=-1, keepdims=True)
+    ref.tokens_out[...] = ref.dx1[...] + spread * (grad - lean - normed * tilt)
+    small_ref[0, 0:1, :] = jnp.sum(d_shift, 0, keepdims=True)
+    small_ref[0, 1:2, :] = jnp.sum(d_shift * normed, 0, keepdims=True)
+    partners = [core_id, pair_id] + [dp_id(bit) for bit in bits] + [blk_id]
+    bit = 1
+    while bit < n_sp:
+        partners.append({SP: spot_s + bit - 2 * bit * lax.rem(spot_s // bit, 2)})
+        bit *= 2
+
+    def small_send(k):
+        hop["small"] = send(small_ref.at[k], ref.small_recv.at[k], partners[k])
+
+    def small_done(k):
+        hop["small"].wait_recv()
+        small_ref[k + 1] = small_ref[k] + ref.small_recv[k]
+        if k + 1 < len(partners):
+            small_send(k + 1)
+        else:
+            ref.small_out[...] = small_ref[k + 1]
+
+    small_send(0)
+    blk_done("ckv")
+    line_send("ckv")
+    small_done(0)
+
     small_done(1)
-    line_done("o")
-    line_done("co")
+    pair_back("o")
+    pair_back("co")
     for k in range(2, len(partners) - 2):
         small_done(k)
     line_done("cq")
@@ -1969,8 +1973,6 @@
         copy.wait_recv()
     hop["s"] = send(ref.s_z, ref.s_ry.at[0], pair_id)
     small_done(len(partners) - 2)
-    pair_back("o")
-    pair_back("co")
     line_done("ckv")
     fo_early.wait_recv()
     ff_last("fo")

time: 792 us -> 801 us (1.011)
  Pallas kernels: 709 us -> 724 us
    pallas_call x1, Pallas kernels: 285 us -> 299 us  [back(): pl.pallas_call(functools.partial(back_kernel, n_sp, n_dp, names), out_sha...]
where the time goes in v4:
time: 801 us; the launch traced here: 791 us
  Pallas kernels  724 us (90%)
  other arithmetic  24.8 us (3%)
  local copies, waits for them, and re-layouts  15.8 us (2%)
  between operations  15.3 us (2%)
    pallas_call x1, Pallas kernels, back(): pl.pallas_call(functools.partial(back_kernel, n_sp, n_dp, names), out_sha...  299 us
    pallas_call x1, Pallas kernels, front(): pl.pallas_call(functools.partial(front_kernel, n_sp), out_shape=outs, in_...  241 us
    pallas_call x1, Pallas kernels, feed(): pl.pallas_call(functools.partial(feed_kernel, n_sp, names), out_shape=tup...  108 us
    pallas_call x1, Pallas kernels, own_back(): pl.pallas_call(functools.partial(own_back_kernel, names), out_shape=tuple...  49.6 us
    pallas_call x1, Pallas kernels, own_tokens(): pl.pallas_call(own_kernel, out_shape=outs, in_specs=[pl.BlockSpec(memory_...  26.2 us
  transfers between devices with their start and end apart: 3, of which 1 were waited for; matrix products, arithmetic and copies ran while one was open for 1% of the time, Pallas kernels for 6%

profile of v4, /device:TPU:27, one launch (start us, length us, event | category | flops | bytes accessed | tf_op | source)
XLA Modules:
  0.0 790.6 jit_solution(8712443824844395663)
XLA Ops:
  8.6 1.4 copy.38
  12.0 3.6 pad_maximum_fusion.rest_ref
  15.6 240.8 %shard_map.264 = (f32[32,1536]{1,0:T(8,128)}, bf16[1024,1536]{1,0:T(8,128)(2,1)}, bf16[1536,1152]{1,0:T(8,128)(2,1)}, f32[2,1024,384]{2,1,0:T(8,128)}, f32[2,102...) custom-call(bf16[256,1536]{1,0:T(8,128)(2,1)} %bitcast.52, ...), custom_call_target="tpu_custom_call" | custom-call | tf_op jit(solution)/shard_map/pallas_call | solution.py:792
  256.4 0.8 dynamic-slice_bitcast_fusion
  258.0 26.2 %shard_map.265 = (f32[256,1536]{1,0:T(8,128)}, f32[256,1536]{1,0:T(8,128)}, bf16[256,1536]{1,0:T(8,128)(2,1)}, f32[256,1536]{1,0:T(8,128)}, f32[512,1536]{1,0:T(...) custom-call(s32[1]{0:T(128)S(6)} %copy.43.len_ref.refs_0_, ...), custom_call_target="tpu_custom_call" | custom-call | tf_op jit(solution)/shard_map/pallas_call | solution.py:958
  284.3 107.7 %shard_map.266 = (bf16[4,256,1536]{2,1,0:T(8,128)(2,1)}, bf16[560,1536]{1,0:T(8,128)(2,1)}, bf16[560,1536]{1,0:T(8,128)(2,1)}, bf16[560,1536]{1,0:T(8,128)(2,1)}...) custom-call(bf16[1120,1536]{1,0:T(8,128)(2,1)} %refs_0_.2, ...), custom_call_target="tpu_custom_call" | custom-call | tf_op jit(solution)/shard_map/pallas_call | solution.py:1380
  392.0 6.3 collective-permute-start
  398.3 1.1 slice.62
  399.5 0.8 slice.55
  401.6 49.6 %shard_map.267 = (bf16[1536,1536]{1,0:T(8,128)(2,1)}, bf16[1536,1536]{1,0:T(8,128)(2,1)}, bf16[1536,1536]{1,0:T(8,128)(2,1)}, bf16[1536,3072]{1,0:T(8,128)(2,1)}...) custom-call(s32[1]{0:T(128)S(6)} %copy.43.len_ref.refs_0_, ...), custom_call_target="tpu_custom_call" | custom-call | tf_op jit(solution)/shard_map/pallas_call | solution.py:1118
  451.3 0.8 slice_reduce_fusion
  452.1 0.8 fusion.14
  452.9 4.6 reduce-scatter.2.cloned.1.call-done
  457.5 2.4 fusion.4
  460.5 299.3 %shard_map.268 = (bf16[8,2,48,3072]{3,2,1,0:T(8,128)(2,1)}, bf16[8,2,48,3072]{3,2,1,0:T(8,128)(2,1)}, bf16[8,48,3072]{2,1,0:T(8,128)(2,1)}, bf16[8,48,3072]{2,1,...) custom-call(bf16[8,2,2,48,3072]{4,3,2,1,0:T(8,128)(2,1)} %bitcast.49, ...), custom_call_target="tpu_custom_call" | custom-call | tf_op jit(solution)/shard_map/pallas_call | solution.py:2090
  759.8 0.9 slice.67
  760.7 0.9 slice.71
  763.6 3.8 bitcast_convert_fusion.2
  767.5 1.8 bitcast_convert_fusion.3
  769.2 2.2 maximum_convert_fusion
  771.4 1.7 copy-done.2
  773.2 7.6 bitcast_convert_fusion
  781.4 1.1 copy.44
  782.6 0.7 copy.45
  (47 shorter events, 8.3 us)
Async XLA Ops:
  7.2 450.3 %reduce-scatter.2.cloned.1.call-start = ((), (), s32[]{:S(2)}) async-start(), calls=%async_computation.1 | async-start | bytes 3932160 | tf_op jit(solution)/shard_map/reduce_scatter | solution.py:2216
  391.9 8.4 %copy-start.10 = (f32[1,2240]{1,0:T(1,128)S(1)}, f32[1,2240]{1,0:T(1,128)}, u32[]{:S(2)}) copy-start(f32[1,2240]{1,0:T(1,128)} %get-tuple-element.106) | copy-start | bytes 26884
  392.0 68.5 %collective-permute-start = (bf16[560,1536]{1,0:T(8,128)(2,1)}, bf16[560,1536]{1,0:T(8,128)(2,1)}, u32[]{:S(2)}, u32[]{:S(2)}) collective-permute-start(bf16[560,1536]{1,0:T(8,128)(2,1)} %get-tuple-element.92), channel_id=1, source_target_pairs={{0,4},{4,0},{1,5},{5,1},{2,6},{6,2},{3,7},{7,3},{8,12},{12,8},{9,1... | collective-permute-start | bytes 5160968 | tf_op jit(solution)/shard_map/ppermute | solution.py:2104
  399.4 61.1 %collective-permute-start.1 = (bf16[224,1536]{1,0:T(8,128)(2,1)S(1)}, bf16[224,1536]{1,0:T(8,128)(2,1)}, u32[]{:S(2)}, u32[]{:S(2)}) collective-permute-start(bf16[224,1536]{1,0:T(8,128)(2,1)S(1)} %slice.62), channel_id=1, source_target_pairs={{0,4},{4,0},{1,5},{5,1},{2,6},{6,2},{3,7},{7,3},{8,12},{12,8},{9,1... | collective-permute-start | bytes 2064392 | tf_op jit(solution)/shard_map/ppermute | solution.py:2104
  401.6 55.9 %copy-start = (bf16[1,256,1536]{2,1,0:T(8,128)(2,1)S(1)}, bf16[1,256,1536]{2,1,0:T(8,128)(2,1)}, u32[]{:S(2)}) copy-start(bf16[1,256,1536]{2,1,0:T(8,128)(2,1)} %param.32) | copy-start | bytes 2359300
  401.6 55.9 %copy-start.1 = (f32[256,1536]{1,0:T(8,128)S(1)}, f32[256,1536]{1,0:T(8,128)}, u32[]{:S(2)}) copy-start(f32[256,1536]{1,0:T(8,128)} %get-tuple-element.69.refs_2_) | copy-start | bytes 4718596
  763.6 3.8 copy-start.6
  763.6 3.8 copy-start.7
  767.4 1.8 copy-start.5
  767.4 1.8 copy-start.8
  767.4 4.0 copy-start.3
  769.2 3.9 copy-start.2
  773.2 8.2 %copy-start.4 = (f32[256,1536]{1,0:T(8,128)S(1)}, f32[256,1536]{1,0:T(8,128)}, u32[]{:S(2)}) copy-start(f32[256,1536]{1,0:T(8,128)} %get-tuple-element.107) | copy-start | bytes 4718596
  780.7 1.8 copy-start.9
Sparse Core Ops, SparseCore 0:
  392.1 65.3 reduce-scatter.1
